TPU v7x, 32 devices: a whole 2x2x4 slice. The times are simulated.
32 devices in a mesh: map: 4 (over z), gx: 4 (over x, core), gy: 2 (over y).
Axes of the slice: x: 2, y: 2, z: 4, core: 2. Of those that a mesh axis runs over, the one named last changes fastest.
Arguments:
- densities: float32 [4, 1536, 2048], P('map', 'gx', 'gy'), may hold values from 0.2 to 41, as said below
- scaling: float32 [4, 1536, 2048], P('map', 'gx', 'gy'), may hold values from 0.5 to 2
- weights: float32 [4], P('map'), as said below
Outputs:
- barycenter: float32 [1536, 2048], P('gx', 'gy')
- new_scaling: float32 [4, 1536, 2048], P('map', 'gx', 'gy')
Inputs may be any that keep to these rules, and one draw needn't show every extreme that they name: `densities`: every cell's demand density is positive. The weights are positive and sum to one.
All inputs are finite; a program needn't handle non-finite values.
Results may differ from a plain program's by a relative error of at most 0.0001.
Values sent between devices are 32-bit elements; how exact they have to be, the bound alone decides.
No kernel may reach another device: no remote copies, remote signals or barrier semaphores. Data moves between devices by JAX's collectives and lax.ppermute only.
A program may use at most 64 MiB of HBM per device.

v0:
```python
import jax
import jax.numpy as jnp
from jax import lax
from jax.sharding import PartitionSpec as P

HALF = 32
SIGMA = 16


def extended(block, sides, width):
    for axis, dim in sides:
        count = lax.axis_size(axis)
        forward = [(i, i + 1) for i in range(count - 1)]
        backward = [(target, source) for source, target in forward]
        low = lax.ppermute(
            lax.slice_in_dim(block, block.shape[dim] - width, None, axis=dim), axis, forward
        )
        high = lax.ppermute(lax.slice_in_dim(block, 0, width, axis=dim), axis, backward)
        block = jnp.concatenate([low, block, high], axis=dim)
    return block


def kernel_band(count):
    rows = jnp.arange(count, dtype=jnp.int32)[:, None]
    cols = jnp.arange(count + 2 * HALF, dtype=jnp.int32)[None, :]
    offset = (cols - rows - HALF).astype(jnp.float32)
    inside = jnp.abs(cols - rows - HALF) <= HALF
    taps = jnp.arange(2 * HALF + 1, dtype=jnp.float32) - HALF
    total = jnp.sum(jnp.exp(-taps * taps / (2.0 * SIGMA * SIGMA)))
    values = jnp.exp(-offset * offset / (2.0 * SIGMA * SIGMA)) / total
    return jnp.where(inside, values, jnp.float32(0.0))


def smooth_axis(padded, axis, length):
    block = min(128, length)
    nblocks = length // block
    pieces = -(-(block + 2 * HALF) // block)
    extra = (nblocks + pieces - 1) * block - (length + 2 * HALF)
    widths = [(0, 0)] * padded.ndim
    widths[axis] = (0, extra)
    padded = jnp.pad(padded, widths)
    band = kernel_band(block)
    band = jnp.pad(band, ((0, 0), (0, pieces * block - block - 2 * HALF)))
    result = None
    for index in range(pieces):
        piece = lax.slice_in_dim(padded, index * block, index * block + length, axis=axis)
        small = band[:, index * block : (index + 1) * block]
        if axis == 1:
            piece = piece.reshape(piece.shape[0], nblocks, block, piece.shape[2])
            term = jnp.einsum(
                "ic,mbcj->mbij",
                small,
                piece,
                precision=lax.Precision.HIGHEST,
                preferred_element_type=jnp.float32,
            )
        else:
            piece = piece.reshape(piece.shape[0], piece.shape[1], nblocks, block)
            term = jnp.einsum(
                "mibc,kc->mibk",
                piece,
                small,
                precision=lax.Precision.HIGHEST,
                preferred_element_type=jnp.float32,
            )
        result = term if result is None else result + term
    if axis == 1:
        return result.reshape(result.shape[0], length, result.shape[3])
    return result.reshape(result.shape[0], result.shape[1], length)


def convolve(field):
    tile_rows = field.shape[1]
    tile_cols = field.shape[2]
    padded = extended(field, (("gx", 1), ("gy", 2)), HALF)
    rows_done = smooth_axis(padded, 1, tile_rows)
    return smooth_axis(rows_done, 2, tile_cols)


def local(densities, scaling, weights):
    tile_rows = densities.shape[1]
    tile_cols = densities.shape[2]
    kv = convolve(scaling)
    u_field = densities / kv
    ku = convolve(u_field)
    partial_log = jnp.sum(weights[:, None, None] * jnp.log(scaling * ku), axis=0)
    cells = jnp.float32(tile_rows * tile_cols * lax.axis_size("gx") * lax.axis_size("gy"))
    logsum = lax.psum(partial_log, "map")
    raw = jnp.exp(logsum)
    mass = lax.psum(jnp.sum(raw), ("gx", "gy"))
    barycenter = cells * raw / mass
    new_scaling = barycenter[None, :, :] / ku
    return (barycenter, new_scaling)


def solution(mesh):
    placed = (P("map", "gx", "gy"), P("map", "gx", "gy"), P("map"))
    return jax.shard_map(
        local,
        mesh=mesh,
        in_specs=placed,
        out_specs=(P("gx", "gy"), P("map", "gx", "gy")),
        check_vma=False,
    )
```

profile of v0, /device:TPU:0, one launch (start us, length us, event | category | flops | bytes accessed | tf_op | source)
XLA Modules:
  0.0 196.5 jit_solution(3449931219668783035)
XLA Ops:
  7.2 1.0 fusion.27
  8.2 2.4 %collective-permute-start = (f32[1,32,1024]{2,1,0:T(8,128)S(1)}, f32[1,32,1024]{2,1,0:T(8,128)S(1)}, u32[]{:S(2)}, u32[]{:S(2)}) collective-permute-start(f32[1,32,1024]{2,1,0:T(8,128)S(1)} %get-tuple-element.19), channel_id=1, source_target_pairs={{0,2},{2,4},{4,6},{1,3},{3,5},{5,7},{8,10},{10,12},{12,14},{9,11},... | collective-permute-start | bytes 393224 | tf_op jit(solution)/shard_map/ppermute | solution.py:15
  10.6 1.3 collective-permute-start.1
  11.9 0.6 fusion.17
  12.5 1.5 constant_dynamic-update-slice_fusion.1
  14.0 1.9 collective-permute-done.1
  16.1 3.4 %collective-permute-start.2 = (f32[1,448,32]{2,1,0:T(8,128)S(1)}, f32[1,448,32]{2,1,0:T(8,128)S(1)}, u32[]{:S(2)}, u32[]{:S(2)}) collective-permute-start(f32[1,448,32]{2,1,0:T(8,128)S(1)} %get-tuple-element.9), channel_id=1, source_target_pairs={{0,1},{2,3},{4,5},{6,7},{8,9},{10,11},{12,13},{14,15},{16,17},{18,... | collective-permute-start | bytes 172040 | tf_op jit(solution)/shard_map/ppermute | solution.py:15
  19.5 1.3 collective-permute-start.3
  20.8 0.7 fusion.5
  21.5 1.5 collective-permute-done.2
  23.0 4.5 %collective-permute-done.3 = f32[1,448,32]{2,1,0:T(8,128)S(1)} collective-permute-done((f32[1,448,32]{2,1,0:T(8,128)S(1)}, f32[1,448,32]{2,1,0:T(8,128)S(1)}, u32[]{:S(2)}, u32[]{:S(2)}) %collective-permute-start.3) | collective-permute-done | bytes 57376 | tf_op jit(solution)/shard_map/ppermute | solution.py:18
  27.5 2.9 %concatenate.13 = f32[1,448,1088]{2,1,0:T(8,128)S(1)} concatenate(f32[1,448,32]{2,1,0:T(8,128)S(1)} %collective-permute-done.2, f32[1,448,1024]{2,1,0:T(8,128)} %copy-done.8, f32[1,448,32]{2,1,0:T(8,128)S(1)} %collective-permute-done.3), dimensions={2} | concatenate | bytes 3899392 | tf_op jit(solution)/shard_map/concatenate | solution.py:19
  30.5 0.2 fusion.23
  30.7 3.0 %fusion.13 = f32[3,1088,128]{2,1,0:T(8,128)S(1)} fusion(f32[3,128,1088]{2,1,0:T(8,128)S(1)} %bitcast.52, f32[128,192]{1,0:T(8,128)S(1)} %fusion.5), kind=kOutput, calls=%fused_computation.28 | convolution fusion | flops 641728512 | bytes 3440640 | tf_op jit(solution)/shard_map/ic,mbcj->mbij/dot_general | solution.py:50
  33.7 3.8 %fusion = f32[1,3,128,1088]{2,3,1,0:T(8,128)S(1)} fusion(f32[3,1088,128]{2,1,0:T(8,128)S(1)} %fusion.13, f32[3,128,1088]{2,1,0:T(8,128)S(1)} %bitcast.50, f32[128,192]{1,0:T(8,128)} %copy-done.2), kind=kOutput, calls=%fused_computation.2 | convolution fusion | flops 642146304 | bytes 5079040 | tf_op jit(solution)/shard_map/ic,mbcj->mbij/dot_general | solution.py:50
  37.5 1.1 copy.10
  38.7 1.4 pad_slice_fusion.3
  40.1 1.9 copy.11
  42.0 2.7 %fusion.8 = f32[384,8,128]{0,2,1:T(8,128)} fusion(f32[384,8,128]{0,2,1:T(8,128)S(1)} %bitcast.54, f32[128,192]{1,0:T(8,128)S(1)} %copy-done.3), kind=kOutput, calls=%fused_computation.26 | convolution fusion | flops 603979776 | bytes 3211264 | tf_op jit(solution)/shard_map/mibc,kc->mibk/dot_general | solution.py:59
  44.7 1.6 copy.13
  46.3 2.9 %convolution_add_fusion.3 = f32[384,8,128]{0,2,1:T(8,128)S(1)} fusion(f32[384,8,128]{0,2,1:T(8,128)S(1)} %copy-done.7, f32[384,8,128]{0,2,1:T(8,128)} %bitcast.57, f32[128,192]{1,0:T(8,128)S(1)} %copy-done.3), kind=kOutput, calls=%fused_computation.12 | convolution fusion | flops 604372992 | bytes 4816896 | tf_op jit(solution)/shard_map/mibc,kc->mibk/dot_general | solution.py:59
  49.2 0.5 copy.15
  49.7 1.7 div.45
  51.4 4.1 %collective-permute-start.4 = (f32[1,32,1024]{2,1,0:T(8,128)S(1)}, f32[1,32,1024]{2,1,0:T(8,128)S(1)}, u32[]{:S(2)}, u32[]{:S(2)}) collective-permute-start(f32[1,32,1024]{2,1,0:T(8,128)S(1)} %get-tuple-element.16), channel_id=1, source_target_pairs={{0,2},{2,4},{4,6},{1,3},{3,5},{5,7},{8,10},{10,12},{12,14},{9,11},... | collective-permute-start | bytes 393224 | tf_op jit(solution)/shard_map/ppermute | solution.py:15
  55.5 1.3 collective-permute-start.5
  56.8 2.6 %collective-permute-done.5 = f32[1,32,1024]{2,1,0:T(8,128)S(1)} collective-permute-done((f32[1,32,1024]{2,1,0:T(8,128)S(1)}, f32[1,32,1024]{2,1,0:T(8,128)S(1)}, u32[]{:S(2)}, u32[]{:S(2)}) %collective-permute-start.5) | collective-permute-done | bytes 131104 | tf_op jit(solution)/shard_map/ppermute | solution.py:18
  59.8 1.5 collective-permute-start.6
  61.2 1.5 collective-permute-start.7
  63.4 1.4 collective-permute-done.6
  64.8 4.4 %collective-permute-done.7 = f32[1,448,32]{2,1,0:T(8,128)S(1)} collective-permute-done((f32[1,448,32]{2,1,0:T(8,128)S(1)}, f32[1,448,32]{2,1,0:T(8,128)S(1)}, u32[]{:S(2)}, u32[]{:S(2)}) %collective-permute-start.7) | collective-permute-done | bytes 57376 | tf_op jit(solution)/shard_map/ppermute | solution.py:18
  69.2 2.9 %concatenate.15 = f32[1,448,1088]{2,1,0:T(8,128)S(1)} concatenate(f32[1,448,32]{2,1,0:T(8,128)S(1)} %collective-permute-done.6, f32[1,448,1024]{2,1,0:T(8,128)} %copy-done, f32[1,448,32]{2,1,0:T(8,128)S(1)} %collective-permute-done.7), dimensions={2} | concatenate | bytes 3899392 | tf_op jit(solution)/shard_map/concatenate | solution.py:19
  72.1 0.2 fusion.22
  72.3 3.0 %fusion.10 = f32[3,1088,128]{2,1,0:T(8,128)S(1)} fusion(f32[3,128,1088]{2,1,0:T(8,128)S(1)} %bitcast.53, f32[128,192]{1,0:T(8,128)S(1)} %copy-done.3), kind=kOutput, calls=%fused_computation.27 | convolution fusion | flops 641728512 | bytes 3440640 | tf_op jit(solution)/shard_map/ic,mbcj->mbij/dot_general | solution.py:50
  75.3 3.0 %fusion.1 = f32[1,3,128,1088]{2,3,1,0:T(8,128)S(1)} fusion(f32[3,1088,128]{2,1,0:T(8,128)S(1)} %fusion.10, f32[3,128,1088]{2,1,0:T(8,128)S(1)} %bitcast.51, f32[128,192]{1,0:T(8,128)S(1)} %copy-done.4), kind=kOutput, calls=%fused_computation.3 | convolution fusion | flops 642146304 | bytes 5177344 | tf_op jit(solution)/shard_map/ic,mbcj->mbij/dot_general | solution.py:50
  78.3 1.1 copy.18
  79.5 1.4 pad_slice_fusion.2
  80.9 1.9 copy.19
  82.8 2.7 %fusion.7 = f32[384,8,128]{0,2,1:T(8,128)} fusion(f32[384,8,128]{0,2,1:T(8,128)S(1)} %bitcast.55, f32[128,192]{1,0:T(8,128)S(1)} %copy-done.5), kind=kOutput, calls=%fused_computation.25 | convolution fusion | flops 603979776 | bytes 3211264 | tf_op jit(solution)/shard_map/mibc,kc->mibk/dot_general | solution.py:59
  85.5 1.6 copy.21
  87.1 3.4 %convolution_add_fusion.2 = f32[384,8,128]{0,2,1:T(8,128)S(1)} fusion(f32[384,8,128]{0,2,1:T(8,128)} %fusion.7, f32[384,8,128]{0,2,1:T(8,128)} %bitcast.56, f32[128,192]{1,0:T(8,128)S(1)} %copy-done.5), kind=kOutput, calls=%fused_computation.11 | convolution fusion | flops 604372992 | bytes 4816896 | tf_op jit(solution)/shard_map/mibc,kc->mibk/dot_general | solution.py:59
  90.5 1.6 copy.23
  92.1 2.9 %multiply_bitcast_fusion = f32[384,1024]{1,0:T(8,128)} fusion(f32[1,384,1024]{2,1,0:T(8,128)S(1)} %copy-done.1, f32[1,384,1024]{2,1,0:T(8,128)} %copy.23, f32[]{:T(128)} %bitcast.46), kind=kLoop, calls=%fused_computation.10 | loop fusion | flops 786432 | bytes 4718596 | tf_op jit(solution)/shard_map/reduce_sum | solution.py:86
  95.0 71.4 %all-reduce.7.cloned.1.call-done = f32[384,1024]{1,0:T(8,128)} async-done(((f32[384,1024]{1,0:T(8,128)}), f32[384,1024]{1,0:T(8,128)}) %all-reduce.7.cloned.1.call-update) | async-done | bytes 1572880 | tf_op jit(solution)/shard_map/psum | solution.py:88
  166.4 2.4 %exponential_reduce_fusion = f32[]{:T(128)} fusion(f32[384,1024]{1,0:T(8,128)} %all-reduce.7.cloned.1.call-done), kind=kLoop, calls=%fused_computation.14 | loop fusion | flops 393215 | bytes 1572868 | tf_op jit(solution)/shard_map/reduce_sum | solution.py:90
  168.8 14.1 %psum.15 = f32[]{:T(128)} all-reduce(f32[]{:T(128)} %exponential_reduce_fusion), channel_id=1, replica_groups=mesh['map'=4,'gx'=4,'gy'=2] {'gx','gy'}, use_global_device_ids=true, to_apply=%region_3.4 | all-reduce | flops 1 | bytes 8 | tf_op jit(solution)/shard_map/psum | solution.py:90
  182.9 2.0 broadcast_multiply_fusion
  184.9 2.0 %copy.24 = f32[384,1024]{1,0:T(8,128)S(1)} copy(f32[384,1024]{0,1:T(8,128)} %bitcast.59) | data formatting | bytes 3145728 | tf_op jit(solution)/shard_map/reshape.50
  186.9 2.8 %divide_bitcast_fusion = (f32[1,384,1024]{2,1,0:T(8,128)}, f32[384,1024]{1,0:T(8,128)}) fusion(f32[384,1024]{1,0:T(8,128)S(1)} %copy.24, f32[384,1024]{1,0:T(8,128)S(1)} %copy-done.6, f32[]{:T(128)} %psum.15), kind=kLoop, calls=%fused_computation.9 | loop fusion | flops 1179648 | bytes 6291460 | tf_op jit(solution)/shard_map/div | solution.py:92
  (28 shorter events, 0.6 us)
Async XLA Ops:
  7.2 159.3 %all-reduce.7.cloned.1.call-start = ((), (), s32[]{:S(2)}) async-start(), calls=%async_computation | async-start | bytes 3145728 | tf_op jit(solution)/shard_map/psum | solution.py:88
  8.2 4.3 %collective-permute-start = (f32[1,32,1024]{2,1,0:T(8,128)S(1)}, f32[1,32,1024]{2,1,0:T(8,128)S(1)}, u32[]{:S(2)}, u32[]{:S(2)}) collective-permute-start(f32[1,32,1024]{2,1,0:T(8,128)S(1)} %get-tuple-element.19), channel_id=1, source_target_pairs={{0,2},{2,4},{4,6},{1,3},{3,5},{5,7},{8,10},{10,12},{12,14},{9,11},... | collective-permute-start | bytes 393224 | tf_op jit(solution)/shard_map/ppermute | solution.py:15
  10.6 5.3 %collective-permute-start.1 = (f32[1,32,1024]{2,1,0:T(8,128)S(1)}, f32[1,32,1024]{2,1,0:T(8,128)S(1)}, u32[]{:S(2)}, u32[]{:S(2)}) collective-permute-start(f32[1,32,1024]{2,1,0:T(8,128)S(1)} %get-tuple-element.18), channel_id=1, source_target_pairs={{2,0},{4,2},{6,4},{3,1},{5,3},{7,5},{10,8},{12,10},{14,12},{11,9},... | collective-permute-start | bytes 393224 | tf_op jit(solution)/shard_map/ppermute | solution.py:18
  15.9 7.1 %copy-start.8 = (f32[1,448,1024]{2,1,0:T(8,128)}, f32[1,448,1024]{2,1,0:T(8,128)S(1)}, u32[]{:S(2)}) copy-start(f32[1,448,1024]{2,1,0:T(8,128)S(1)} %constant_dynamic-update-slice_fusion) | copy-start | bytes 5505028
  16.1 7.0 %collective-permute-start.2 = (f32[1,448,32]{2,1,0:T(8,128)S(1)}, f32[1,448,32]{2,1,0:T(8,128)S(1)}, u32[]{:S(2)}, u32[]{:S(2)}) collective-permute-start(f32[1,448,32]{2,1,0:T(8,128)S(1)} %get-tuple-element.9), channel_id=1, source_target_pairs={{0,1},{2,3},{4,5},{6,7},{8,9},{10,11},{12,13},{14,15},{16,17},{18,... | collective-permute-start | bytes 172040 | tf_op jit(solution)/shard_map/ppermute | solution.py:15
  19.5 8.0 %collective-permute-start.3 = (f32[1,448,32]{2,1,0:T(8,128)S(1)}, f32[1,448,32]{2,1,0:T(8,128)S(1)}, u32[]{:S(2)}, u32[]{:S(2)}) collective-permute-start(f32[1,448,32]{2,1,0:T(8,128)S(1)} %get-tuple-element.8), channel_id=1, source_target_pairs={{1,0},{3,2},{5,4},{7,6},{9,8},{11,10},{13,12},{15,14},{17,16},{19,... | collective-permute-start | bytes 172040 | tf_op jit(solution)/shard_map/ppermute | solution.py:18
  21.5 9.2 %copy-start.2 = (f32[128,192]{1,0:T(8,128)}, f32[128,192]{1,0:T(8,128)S(1)}, u32[]{:S(2)}) copy-start(f32[128,192]{1,0:T(8,128)S(1)} %fusion.5) | copy-start | bytes 294916
  40.1 1.9 copy-start.3
  44.7 1.6 copy-start.7
  51.4 5.4 %collective-permute-start.4 = (f32[1,32,1024]{2,1,0:T(8,128)S(1)}, f32[1,32,1024]{2,1,0:T(8,128)S(1)}, u32[]{:S(2)}, u32[]{:S(2)}) collective-permute-start(f32[1,32,1024]{2,1,0:T(8,128)S(1)} %get-tuple-element.16), channel_id=1, source_target_pairs={{0,2},{2,4},{4,6},{1,3},{3,5},{5,7},{8,10},{10,12},{12,14},{9,11},... | collective-permute-start | bytes 393224 | tf_op jit(solution)/shard_map/ppermute | solution.py:15
  55.5 3.9 %collective-permute-start.5 = (f32[1,32,1024]{2,1,0:T(8,128)S(1)}, f32[1,32,1024]{2,1,0:T(8,128)S(1)}, u32[]{:S(2)}, u32[]{:S(2)}) collective-permute-start(f32[1,32,1024]{2,1,0:T(8,128)S(1)} %get-tuple-element.17), channel_id=1, source_target_pairs={{2,0},{4,2},{6,4},{3,1},{5,3},{7,5},{10,8},{12,10},{14,12},{11,9},... | collective-permute-start | bytes 393224 | tf_op jit(solution)/shard_map/ppermute | solution.py:18
  59.6 5.1 %copy-start = (f32[1,448,1024]{2,1,0:T(8,128)}, f32[1,448,1024]{2,1,0:T(8,128)S(1)}, u32[]{:S(2)}) copy-start(f32[1,448,1024]{2,1,0:T(8,128)S(1)} %pad_maximum_fusion) | copy-start | bytes 5505028
  59.8 5.0 %collective-permute-start.6 = (f32[1,448,32]{2,1,0:T(8,128)S(1)}, f32[1,448,32]{2,1,0:T(8,128)S(1)}, u32[]{:S(2)}, u32[]{:S(2)}) collective-permute-start(f32[1,448,32]{2,1,0:T(8,128)S(1)} %get-tuple-element.7), channel_id=1, source_target_pairs={{0,1},{2,3},{4,5},{6,7},{8,9},{10,11},{12,13},{14,15},{16,17},{18,... | collective-permute-start | bytes 172040 | tf_op jit(solution)/shard_map/ppermute | solution.py:15
  61.2 7.9 %collective-permute-start.7 = (f32[1,448,32]{2,1,0:T(8,128)S(1)}, f32[1,448,32]{2,1,0:T(8,128)S(1)}, u32[]{:S(2)}, u32[]{:S(2)}) collective-permute-start(f32[1,448,32]{2,1,0:T(8,128)S(1)} %get-tuple-element.6), channel_id=1, source_target_pairs={{1,0},{3,2},{5,4},{7,6},{9,8},{11,10},{13,12},{15,14},{17,16},{19,... | collective-permute-start | bytes 172040 | tf_op jit(solution)/shard_map/ppermute | solution.py:18
  72.3 3.0 %copy-start.4 = (f32[128,192]{1,0:T(8,128)S(1)}, f32[128,192]{1,0:T(8,128)}, u32[]{:S(2)}) copy-start(f32[128,192]{1,0:T(8,128)} %copy-done.2) | copy-start | bytes 294916
  80.9 1.9 copy-start.5
  90.5 1.6 copy-start.1
  184.9 2.0 %copy-start.6 = (f32[384,1024]{1,0:T(8,128)S(1)}, f32[384,1024]{1,0:T(8,128)}, u32[]{:S(2)}) copy-start(f32[384,1024]{1,0:T(8,128)} %all-reduce.7.cloned.1.call-done) | copy-start | bytes 4718596
Sparse Core Ops, SparseCore 0:
  95.2 71.2 all-reduce.6
where the time goes:
time: 197 us
  waiting for transfers between devices  87.6 us (44%)
  local copies, waits for them, and re-layouts  25.4 us (13%)
  matrix products  24.4 us (12%)
  starting transfers between devices  16.7 us (8%)
  between operations  15 us (8%)
  blocking collectives  14.1 us (7%)
  other arithmetic  13.2 us (7%)
    psum x1, waiting for transfers between devices, local(): logsum = lax.psum(partial_log, 'map')  71.4 us
    psum x1, blocking collectives, local(): mass = lax.psum(jnp.sum(raw), ('gx', 'gy'))  14.1 us
    ppermute x4, waiting for transfers between devices, extended(): lax.ppermute(lax.slice_in_dim(block, 0, width, axis=dim), axis, backward)  13.4 us
    dot_general x4, matrix products, smooth_axis(): jnp.einsum('ic,mbcj->mbij', small, piece, precision=lax.Precision.HIGHEST...  12.8 us
    dot_general x4, matrix products, smooth_axis(): jnp.einsum('mibc,kc->mibk', piece, small, precision=lax.Precision.HIGHEST...  11.6 us
    ppermute x4, starting transfers between devices, extended(): lax.ppermute(lax.slice_in_dim(block, block.shape[dim] - width, None, axis...  11.4 us
    slice x8, local copies, waits for them, and re-layouts, smooth_axis(): lax.slice_in_dim(padded, index * block, index * block + length, axis=axis)  10.3 us
    concatenate x3, local copies, waits for them, and re-layouts, extended(): block = jnp.concatenate([low, block, high], axis=dim)  5.87 us
  transfers between devices with their start and end apart: 9, of which 7 were waited for; matrix products, arithmetic and copies ran while one was open for 1% of the time, Pallas kernels for 0%

commit v1 on v0

v1 whole, which is shorter than its diff:
```python
import math

import jax
import jax.numpy as jnp
import numpy as np
from jax import lax
from jax.experimental import pallas as pl
from jax.experimental.pallas import tpu as pltpu
from jax.sharding import PartitionSpec as P

HALF = 32
SIGMA = 16
WIDE = 2 * HALF
LANES = 128
F32 = jnp.float32
BF16 = jnp.bfloat16


def gauss(offset):
    taps = np.arange(-HALF, HALF + 1, dtype=np.float64)
    total = np.exp(-taps * taps / (2.0 * SIGMA * SIGMA)).sum()
    values = np.exp(-offset * offset / (2.0 * SIGMA * SIGMA)) / total
    return np.where(np.abs(offset) <= HALF, values, 0.0)


def halves(values):
    high = values.astype(np.float32).astype(BF16)
    low = (values - high.astype(np.float64)).astype(np.float32).astype(BF16)
    return jnp.asarray(np.stack([high, low]))


def row_band(count):
    i = np.arange(count, dtype=np.float64)[:, None]
    c = np.arange(count + WIDE, dtype=np.float64)[None, :]
    return halves(gauss(c - HALF - i))


def col_band(rows, cols, shift):
    c = np.arange(rows, dtype=np.float64)[:, None]
    j = np.arange(cols, dtype=np.float64)[None, :]
    return halves(gauss(c - shift - j))


def split(x):
    high = x.astype(BF16)
    low = (x - high.astype(F32)).astype(BF16)
    return high, low


def mm(a, b):
    return jnp.dot(a, b, preferred_element_type=F32)


def rows_of(band, x):
    (bh, bl), (xh, xl) = band, split(x)
    return mm(bh, xh) + mm(bh, xl) + mm(bl, xh)


def times(parts, band):
    (xh, xl), (bh, bl) = parts, band
    return mm(xh, bh) + mm(xl, bh) + mm(xh, bl)


def cols_all(x, band):
    width = x.shape[1]
    xh, xl = split(x)
    out = []
    for start in range(0, width, 256):
        lo, hi = max(start - LANES, 0), min(start + 256 + LANES, width)
        top, bottom = lo - (start - LANES), hi - (start - LANES)
        out.append(times((xh[:, lo:hi], xl[:, lo:hi]), (band[0][top:bottom], band[1][top:bottom])))
    return jnp.concatenate(out, axis=1)


def cols_inner(x, band):
    width = x.shape[1]
    xh, xl = split(x)
    out = []
    for start in range(0, width - 2 * LANES, 256):
        stop = min(start + 512, width)
        n = stop - start - 2 * LANES
        out.append(times((xh[:, start:stop], xl[:, start:stop]), (band[0][: stop - start, :n], band[1][: stop - start, :n])))
    return jnp.concatenate(out, axis=1)


def quotient(dens, kv):
    return jnp.where(dens > 0.0, dens / kv, 0.0)


def strip(scal, dens, tband, cband):
    n = dens.shape[0]
    kv = cols_all(rows_of((tband[0][:n, : n + WIDE], tband[1][:n, : n + WIDE]), scal), cband)
    u = quotient(dens, kv)
    m = n - WIDE
    return cols_inner(rows_of((tband[0][:m, :n], tband[1][:m, :n]), u), cband)


def band_of(ref):
    return (ref[0], ref[1])


def log_term(weight, scal, ku):
    return weight * jnp.log(scal * ku)


def vmem():
    return pl.BlockSpec(memory_space=pltpu.VMEM)


def smem():
    return pl.BlockSpec(memory_space=pltpu.SMEM)


def rowblock(rows, cols, index):
    return pl.BlockSpec((1, rows, cols), lambda i: (0, index, 0))


def call(body, out, in_specs, flops, name):
    return pl.pallas_call(
        body,
        grid=(1,),
        out_shape=[jax.ShapeDtypeStruct(s, F32) for s in out],
        in_specs=in_specs,
        out_specs=[vmem()] * len(out),
        compiler_params=pltpu.CompilerParams(vmem_limit_bytes=48 * 1024 * 1024),
        cost_estimate=pl.CostEstimate(flops=flops, bytes_accessed=4 * 1024 * 1024, transcendentals=0),
        name=name,
    )


def inner_chunk(weights, scaling, densities, tband, cband, index, pieces, pack):
    rows, cols = scaling.shape[1:]

    def body(*refs):
        w, s0, s1, d0, d1, tb, cb = refs[:7]
        refs = refs[7:]
        scal = jnp.concatenate([s0[0], s1[0]], axis=0)
        dens = jnp.concatenate([d0[0], d1[0]], axis=0)
        if pack:
            sl, dl, up, down = refs[0], refs[1], refs[-2], refs[-1]
            refs = refs[2:-2]
            up[:WIDE] = s0[0, :WIDE]
            up[WIDE:] = d0[0, :HALF]
            down[:WIDE] = sl[0]
            down[WIDE:] = dl[0, HALF:]
        ku = strip(scal, dens[HALF:-HALF], band_of(tb), band_of(cb))
        term = log_term(w[0], scal[WIDE:-WIDE, LANES:-LANES], ku)
        size = LANES // pieces
        for k in range(pieces):
            refs[2 * k][...] = term[k * size : (k + 1) * size]
            refs[2 * k + 1][...] = ku[k * size : (k + 1) * size]

    inner = (LANES // pieces, cols - 2 * LANES)
    out = [inner] * (2 * pieces)
    specs = [smem()] + [rowblock(128, cols, index), rowblock(128, cols, index + 1)] * 2 + [vmem(), vmem()]
    args = [weights, scaling, scaling, densities, densities, tband, cband]
    if pack:
        out += [(WIDE + HALF, cols)] * 2
        last = rows // WIDE - 1
        specs += [rowblock(WIDE, cols, last)] * 2
        args += [scaling, densities]
    return call(body, out, specs, 4_000_000_000, "inner")(*args)


def edge_chunk(weights, scaling, densities, tband, cband, up, down):
    rows, cols = scaling.shape[1:]

    def body(w, s0, s1, d0, d1, tb, cb, hu, hd, term, ku):
        tb, cb = band_of(tb), band_of(cb)
        top = jnp.concatenate([hu[:WIDE], s0[0]], axis=0)
        dens = jnp.concatenate([hu[WIDE:], d0[0, : 128 - HALF]], axis=0)
        k = strip(top, dens, tb, cb)
        ku[:WIDE] = k
        term[:WIDE] = log_term(w[0], s0[0, :WIDE, LANES:-LANES], k)
        low = jnp.concatenate([s1[0], hd[:WIDE]], axis=0)
        dens = jnp.concatenate([d1[0, HALF:], hd[WIDE:]], axis=0)
        k = strip(low, dens, tb, cb)
        ku[WIDE:] = k
        term[WIDE:] = log_term(w[0], s1[0, WIDE:, LANES:-LANES], k)

    last = rows // 128 - 1
    specs = [smem()] + [rowblock(128, cols, 0), rowblock(128, cols, last)] * 2 + [vmem()] * 4
    out = [(2 * WIDE, cols - 2 * LANES)] * 2
    return call(body, out, specs, 4_000_000_000, "edge")(
        weights, scaling, scaling, densities, densities, tband, cband, up, down
    )


def colblock(rows, index):
    return pl.BlockSpec((1, rows, LANES), lambda i: (0, 0, index))


def colblock2(rows, index):
    return pl.BlockSpec((rows, LANES), lambda i: (0, index))


def side_pack(scaling, densities, up, down):
    rows, cols = scaling.shape[1:]
    tall = rows + 2 * WIDE
    last = cols // LANES - 1
    two = lax.axis_size("gy") == 2

    def body(sl, sr, dl, dr, ul, ur, ol, orr, *outs):
        lane = lax.broadcasted_iota(jnp.int32, (tall, LANES), 1)
        zero = jnp.zeros((HALF, LANES), F32)

        def tallest(s, d, u, o):
            scal = jnp.concatenate([u[:WIDE], s[0], o[:WIDE]], axis=0)
            dens = jnp.concatenate([zero, u[WIDE:], d[0], o[WIDE:], zero], axis=0)
            return scal, dens

        scal, dens = tallest(sl, dl, ul, ol)
        left = jnp.where(lane < WIDE, scal, pltpu.roll(dens, WIDE, 1))
        scal, dens = tallest(sr, dr, ur, orr)
        right = jnp.where(lane >= WIDE, scal, pltpu.roll(dens, HALF, 1))
        if two:
            outs[0][...] = jnp.where(lax.axis_index("gy") == 0, right, left)
        else:
            outs[0][...] = left
            outs[1][...] = right

    specs = [colblock(rows, 0), colblock(rows, last)] * 2 + [colblock2(WIDE + HALF, 0), colblock2(WIDE + HALF, last)] * 2
    out = [(tall, LANES)] * (1 if two else 2)
    return call(body, out, specs, 1_000_000, "side_pack")(scaling, scaling, densities, densities, up, up, down, down)


def side_chunk(weights, scaling, densities, tband, gband, up, down, from_left, from_right, pieces):
    rows, cols = scaling.shape[1:]
    tall = rows + 2 * WIDE
    blocks = cols // LANES
    two = lax.axis_size("gy") == 2

    def body(*refs):
        w, s, d, u, o = refs[0], refs[1:5], refs[5:9], refs[9:13], refs[13:17]
        tb, gb, hl, hr = refs[17:21]
        outs = refs[21:]
        lane = lax.broadcasted_iota(jnp.int32, (tall, LANES), 1)
        tb, gb = band_of(tb), band_of(gb)
        here = lax.axis_index("gy")
        left, right = hl[...], hr[...]
        if two:
            left = jnp.where(here == 0, 0.0, left)
            right = jnp.where(here == 0, right, 0.0)
        left_s = jnp.where(lane >= WIDE, left, 0.0)
        left_d = jnp.where(lane >= LANES - HALF, pltpu.roll(left, LANES - HALF, 1), 0.0)
        right_s = jnp.where(lane < WIDE, right, 0.0)
        right_d = jnp.where(lane < HALF, pltpu.roll(right, WIDE, 1), 0.0)

        def scal(k):
            return jnp.concatenate([u[k][:WIDE], s[k][0], o[k][:WIDE]], axis=0)

        def dens(k):
            return jnp.concatenate([u[k][WIDE:], d[k][0], o[k][WIDE:]], axis=0)

        def side(sx, dx):
            n = tall - WIDE
            kv = times(split(rows_of((tb[0][:n, :tall], tb[1][:n, :tall]), sx)), gb)
            ux = quotient(dx, kv)
            r = rows_of((tb[0][:rows, :n], tb[1][:rows, :n]), ux)
            return times(split(r), (gb[0][:, LANES : 2 * LANES], gb[1][:, LANES : 2 * LANES]))

        inner = slice(HALF, tall - HALF)
        k0 = side(
            jnp.concatenate([left_s, scal(0), scal(1)], axis=1),
            jnp.concatenate([left_d[inner], dens(0), dens(1)], axis=1),
        )
        k1 = side(
            jnp.concatenate([scal(2), scal(3), right_s], axis=1),
            jnp.concatenate([dens(2), dens(3), right_d[inner]], axis=1),
        )
        size = rows // pieces
        for p in range(pieces):
            part = slice(p * size, (p + 1) * size)
            outs[2 * p][:, :LANES] = log_term(w[0], s[0][0, part], k0[part])
            outs[2 * p][:, LANES:] = log_term(w[0], s[3][0, part], k1[part])
            outs[2 * p + 1][:, :LANES] = k0[part]
            outs[2 * p + 1][:, LANES:] = k1[part]

    which = [0, 1, blocks - 2, blocks - 1]
    specs = [smem()] + [colblock(rows, k) for k in which] * 2 + [colblock2(WIDE + HALF, k) for k in which] * 2
    specs += [vmem()] * 4
    args = [weights] + [scaling] * 4 + [densities] * 4 + [up] * 4 + [down] * 4 + [tband, gband, from_left, from_right]
    out = [(rows // pieces, 2 * LANES)] * (2 * pieces)
    return call(body, out, specs, 6_000_000_000, "sides")(*args)


def finish(held, landed, ku, mass):
    count = lax.axis_size("map")

    def body(*refs):
        held_ref, landed_ref, ku_ref = refs[:3]
        raw_ref, quot_ref, mass_ref = refs[-3:]
        z = lax.axis_index("map")
        middle = (z == count // 2 - 1) | (z == count // 2)
        raw = jnp.exp(jnp.where(middle, held_ref[...], landed_ref[...]))
        raw_ref[...] = raw
        quot_ref[...] = raw / ku_ref[...]
        rows, cols = raw.shape
        part = jnp.sum(raw.reshape(rows // 8, 8, cols), axis=0)
        total = part[:, :LANES]
        for k in range(1, cols // LANES):
            total = total + part[:, k * LANES : (k + 1) * LANES]
        if len(refs) == 7:
            total = total + refs[3][...]
        mass_ref[...] = total

    args = [held, landed, ku] + ([] if mass is None else [mass])
    return call(body, [held.shape, held.shape, (8, LANES)], [vmem()] * len(args), 4_000_000, "finish")(*args)


def sum_grid(mass):
    for axis in ("gx", "gy"):
        count = lax.axis_size(axis)
        if count & (count - 1):
            mass = lax.psum(mass, axis)
            continue
        step = 1
        while step < count:
            mass = mass + lax.ppermute(mass, axis, [(i, i ^ step) for i in range(count)])
            step *= 2
    return mass


def assemble(mass, places, raws, quots, rows, cols, cells):
    n = len(places)

    def body(*refs):
        mass_ref, raw, quot = refs[0], refs[1 : 1 + n], refs[1 + n : 1 + 2 * n]
        bary, new = refs[-2:]
        scale = cells / jnp.sum(mass_ref[...])
        for k, place in enumerate(places):
            for source, r0, c0, height, width, from_row, from_col in place:
                piece = (slice(from_row, from_row + height), slice(from_col, from_col + width))
                bary[r0 : r0 + height, c0 : c0 + width] = raw[k][piece] * scale
                new[0, r0 : r0 + height, c0 : c0 + width] = quot[k][piece] * scale

    return call(body, [(rows, cols), (1, rows, cols)], [vmem()] * (1 + 2 * n), 4_000_000, "assemble")(
        mass, *raws, *quots
    )


def after(value, *others):
    return lax.optimization_barrier((value,) + others)[0]


def local(densities, scaling, weights):
    rows, cols = scaling.shape[1:]
    tband = row_band(rows + WIDE)
    cband = col_band(512, 256, LANES)
    gband = col_band(3 * LANES, 3 * LANES, 0)
    count = lax.axis_size("map")
    half = count // 2
    cells = float(rows * cols * lax.axis_size("gx") * lax.axis_size("gy"))

    def inward(x):
        for hop in range(half - 1):
            x = x + lax.ppermute(x, "map", [(hop, hop + 1), (count - 1 - hop, count - 2 - hop)])
        return x

    def across(x):
        return x + lax.ppermute(x, "map", [(half - 1, half), (half, half - 1)])

    def outward(x):
        got = x
        z = lax.axis_index("map")
        for hop in range(half - 2, -1, -1):
            pairs = [(hop + 1, hop), (count - 2 - hop, count - 1 - hop)]
            new = lax.ppermute(x, "map", pairs)
            if hop:
                x = jnp.where((z == hop) | (z == count - 1 - hop), new, x)
                got = x
            else:
                got = jnp.where((z == 0) | (z == count - 1), new, got) if half > 2 else new
        return got

    gx = lax.axis_size("gx")
    forward = [(i, i + 1) for i in range(gx - 1)]
    backward = [(i + 1, i) for i in range(gx - 1)]

    chunks, places = [], []
    nblocks = rows // 128 - 1
    wide = cols - 2 * LANES
    first = inner_chunk(weights, scaling, densities, tband, cband, 0, 2, True)
    packed_up, packed_down = first[-2:]
    chunks += [first[0:2], first[2:4]]
    places += [[(0, WIDE, LANES, 64, wide, 0, 0)], [(0, WIDE + 64, LANES, 64, wide, 0, 0)]]
    down = lax.ppermute(packed_up, "gx", backward)
    up = lax.ppermute(packed_down, "gx", forward)
    for k in range(1, nblocks):
        chunks.append(inner_chunk(weights, scaling, densities, tband, cband, k, 1, False))
        places.append([(0, WIDE + 128 * k, LANES, 128, wide, 0, 0)])
    chunks.append(edge_chunk(weights, scaling, densities, tband, cband, up, down))
    places.append([(0, 0, LANES, WIDE, wide, 0, 0), (0, rows - WIDE, LANES, WIDE, wide, WIDE, 0)])
    packs = side_pack(scaling, densities, up, down)
    gy = lax.axis_size("gy")
    if gy == 2:
        from_left = from_right = lax.ppermute(packs[0], "gy", [(0, 1), (1, 0)])
    else:
        from_right = lax.ppermute(packs[0], "gy", [(i + 1, i) for i in range(gy - 1)])
        from_left = lax.ppermute(packs[1], "gy", [(i, i + 1) for i in range(gy - 1)])
    sides = side_chunk(weights, scaling, densities, tband, gband, up, down, from_left, from_right, 2)
    size = rows // 2
    for k in range(2):
        chunks.append(sides[2 * k : 2 * k + 2])
        places.append(
            [(0, k * size, 0, size, LANES, 0, 0), (0, k * size, cols - LANES, size, LANES, 0, LANES)]
        )

    mass = None
    raws, quots = [], []
    for term, ku in chunks:
        held = across(inward(term))
        landed = outward(held)
        raw, quot, mass = finish(held, landed, ku, mass)
        raws.append(raw)
        quots.append(quot)
    mass = sum_grid(mass)
    bary, new = assemble(mass, places, raws, quots, rows, cols, cells)
    return bary, new


def solution(mesh):
    placed = (P("map", "gx", "gy"), P("map", "gx", "gy"), P("map"))
    return jax.shard_map(
        local,
        mesh=mesh,
        in_specs=placed,
        out_specs=(P("gx", "gy"), P("map", "gx", "gy")),
        check_vma=False,
    )
```

time: 197 us -> 108 us (0.55)
  waiting for transfers between devices: 87.6 us -> 44.8 us
  matrix products: 24.4 us -> 0 us
  starting transfers between devices: 16.7 us -> 38.8 us
  local copies, waits for them, and re-layouts: 25.4 us -> 5.05 us
  Pallas kernels: 0 us -> 16.5 us
  blocking collectives: 14.1 us -> 0 us
  between operations: 15 us -> 1.75 us
  other arithmetic: 13.2 us -> 0.4 us
    psum x1 -> x0, waiting for transfers between devices: 71.4 us -> none  [local(): logsum = lax.psum(partial_log, 'map')]
    ppermute x8 -> x24, waiting for transfers between devices: 16.2 us -> 44.8 us  [the longest x6 29.9 us: outward(): new = lax.ppermute(x, 'map', pairs)]
    dot_general x8 -> x0, matrix products: 24.4 us -> none  [the longest x4 12.8 us: smooth_axis(): jnp.einsum('ic,mbcj->mbij', small, piece, precision=lax.Precision.HIGHEST...]
    ppermute x8 -> x24, starting transfers between devices: 16.7 us -> 38.8 us  [the longest x6 16.9 us: inward(): lax.ppermute(x, 'map', [(hop, hop + 1), (count - 1 - hop, count - 2 - hop)])]
    pallas_call x0 -> x12, Pallas kernels: none -> 16.5 us  [the longest x1 6.36 us: side_chunk(): return call(body, out, specs, 6000000000, 'sides')(*args)]
    psum x1 -> x0, blocking collectives: 14.1 us -> none  [local(): mass = lax.psum(jnp.sum(raw), ('gx', 'gy'))]
    slice x12 -> x0, local copies, waits for them, and re-layouts: 11.6 us -> none  [the longest x8 10.3 us: smooth_axis(): lax.slice_in_dim(padded, index * block, index * block + length, axis=axis)]
    reduce_sum x3 -> x0, other arithmetic: 5.92 us -> none  [the longest x1 2.88 us: local(): jnp.sum(weights[:, None, None] * jnp.log(scaling * ku), axis=0)]
  transfers between devices with their start and end apart: 9 -> 24, of which waited for: 7 -> 10; matrix products, arithmetic and copies ran while one was open for 1% -> 0% of each run, Pallas kernels for 0% -> 11%
where the time goes in v1:
time: 108 us; the launch traced here: 107 us
  waiting for transfers between devices  44.8 us (41%)
  starting transfers between devices  38.8 us (36%)
  Pallas kernels  16.5 us (15%)
  local copies, waits for them, and re-layouts  5.05 us (5%)
  between operations  1.75 us (2%)
    ppermute x6, waiting for transfers between devices, outward(): new = lax.ppermute(x, 'map', pairs)  29.9 us
    ppermute x6, starting transfers between devices, inward(): lax.ppermute(x, 'map', [(hop, hop + 1), (count - 1 - hop, count - 2 - hop)])  16.9 us
    ppermute x6, waiting for transfers between devices, inward(): lax.ppermute(x, 'map', [(hop, hop + 1), (count - 1 - hop, count - 2 - hop)])  8.81 us
    ppermute x6, starting transfers between devices, outward(): new = lax.ppermute(x, 'map', pairs)  7.73 us
    pallas_call x1, Pallas kernels, side_chunk(): return call(body, out, specs, 6000000000, 'sides')(*args)  6.36 us
    ppermute x3, waiting for transfers between devices, sum_grid(): lax.ppermute(mass, axis, [(i, i ^ step) for i in range(count)])  6.08 us
    unnamed x14, local copies, waits for them, and re-layouts  5.05 us
    ppermute x3, starting transfers between devices, sum_grid(): lax.ppermute(mass, axis, [(i, i ^ step) for i in range(count)])  4.9 us
  transfers between devices with their start and end apart: 24, of which 10 were waited for; matrix products, arithmetic and copies ran while one was open for 0% of the time, Pallas kernels for 11%

profile of v1, /device:TPU:0, one launch (start us, length us, event | category | flops | bytes accessed | tf_op | source)
XLA Modules:
  0.0 107.3 jit_solution(5498234467005220130)
XLA Ops:
  1.3 1.4 %copy-done = f32[1,384,1024]{2,1,0:T(8,128)S(1)} copy-done((f32[1,384,1024]{2,1,0:T(8,128)S(1)}, f32[1,384,1024]{2,1,0:T(8,128)}, u32[]{:S(2)}) %copy-start) | copy-done | bytes 1572888
  2.7 1.4 %copy-done.1 = f32[1,384,1024]{2,1,0:T(8,128)S(1)} copy-done((f32[1,384,1024]{2,1,0:T(8,128)S(1)}, f32[1,384,1024]{2,1,0:T(8,128)}, u32[]{:S(2)}) %copy-start.1) | copy-done | bytes 1572888
  4.1 1.2 %copy-done.2 = bf16[2,448,512]{2,1,0:T(8,128)(2,1)S(1)} copy-done((bf16[2,448,512]{2,1,0:T(8,128)(2,1)S(1)}, bf16[2,448,512]{2,1,0:T(8,128)(2,1)}, u32[]{:S(2)}) %copy-start.2) | copy-done | bytes 917528
  5.3 1.0 copy-done.5
  6.3 2.1 %inner.2 = (f32[64,768]{1,0:T(8,128)S(1)}, f32[64,768]{1,0:T(8,128)S(1)}, f32[64,768]{1,0:T(8,128)S(1)}, f32[64,768]{1,0:T(8,128)S(1)}, f32[96,1024]{1,0:T(8,128)S(1)}, /*index=5*/f32[96,1024]{1,0:T(8,128)S(1)}) custom-call(f32[1]{0:T(128)S(6)} %copy.8.refs_0_.w, f32[1,384,1024]{2,1,0:T(8,128)S(1)} %copy-done, f32[1,384,1024]{2,1,0:T(8,128)S(1)} %copy-done, ...), custom_call_target="tpu_custom_call" | custom-call | flops 4000000000 | bytes 4194304 | tf_op jit(solution)/shard_map/inner/pallas_call | solution.py:162
  8.4 2.4 %collective-permute-start = (f32[96,1024]{1,0:T(8,128)S(1)}, f32[96,1024]{1,0:T(8,128)S(1)}, u32[]{:S(2)}, u32[]{:S(2)}) collective-permute-start(f32[96,1024]{1,0:T(8,128)S(1)} %get-tuple-element.34), channel_id=1, source_target_pairs={{0,2},{2,4},{4,6},{1,3},{3,5},{5,7},{8,10},{10,12},{12,14},{9,11},... | collective-permute-start | bytes 1179656 | tf_op jit(solution)/shard_map/ppermute | solution.py:388
  10.8 1.3 %collective-permute-start.1 = (f32[96,1024]{1,0:T(8,128)S(1)}, f32[96,1024]{1,0:T(8,128)S(1)}, u32[]{:S(2)}, u32[]{:S(2)}) collective-permute-start(f32[96,1024]{1,0:T(8,128)S(1)} %get-tuple-element.35), channel_id=1, source_target_pairs={{2,0},{4,2},{6,4},{3,1},{5,3},{7,5},{10,8},{12,10},{14,12},{11,9},... | collective-permute-start | bytes 1179656 | tf_op jit(solution)/shard_map/ppermute | solution.py:387
  12.1 2.1 %inner.3 = (f32[128,768]{1,0:T(8,128)S(1)}, f32[128,768]{1,0:T(8,128)S(1)}) custom-call(f32[1]{0:T(128)S(6)} %copy.8.refs_0_.w, f32[1,384,1024]{2,1,0:T(8,128)S(1)} %copy-done, f32[1,384,1024]{2,1,0:T(8,128)S(1)} %copy-done, f32[1,384,1024]{2,1,0:T(8,128)S(1)} %copy-done.1, f32[1,384,1024]{2,1,0:T(8,128)S(1)} %copy-done.1, ...), custom_call_target="tpu_custom_call" | custom-call | flops 4000000000 | bytes 4194304 | tf_op jit(solution)/shard_map/inner/pallas_call | solution.py:162
  14.2 4.3 %collective-permute-start.12 = (f32[128,768]{1,0:T(8,128)S(1)}, f32[128,768]{1,0:T(8,128)S(1)}, u32[]{:S(2)}, u32[]{:S(2)}) collective-permute-start(f32[128,768]{1,0:T(8,128)S(1)} %get-tuple-element.42), channel_id=1, source_target_pairs={{0,8},{24,16},{1,9},{25,17},{2,10},{26,18},{3,11},{27,19},{4,12},{... | collective-permute-start | bytes 1179656 | tf_op jit(solution)/shard_map/ppermute | solution.py:357
  18.5 3.2 %edge.1 = (f32[128,768]{1,0:T(8,128)S(1)}, f32[128,768]{1,0:T(8,128)S(1)}) custom-call(f32[1]{0:T(128)S(6)} %copy.8.refs_0_.w, f32[1,384,1024]{2,1,0:T(8,128)S(1)} %copy-done, f32[1,384,1024]{2,1,0:T(8,128)S(1)} %copy-done, f32[1,384,1024]{2,1,0:T(8,128)S(1)} %copy-done.1, f32[1,384,1024]{2,1,0:T(8,128)S(1)} %copy-done.1, ...), custom_call_target="tpu_custom_call" | custom-call | flops 4000000000 | bytes 4194304 | tf_op jit(solution)/shard_map/edge/pallas_call | solution.py:184
  21.7 1.5 %collective-permute-start.9 = (f32[128,768]{1,0:T(8,128)S(1)}, f32[128,768]{1,0:T(8,128)S(1)}, u32[]{:S(2)}, u32[]{:S(2)}) collective-permute-start(f32[128,768]{1,0:T(8,128)S(1)} %get-tuple-element.40), channel_id=1, source_target_pairs={{0,8},{24,16},{1,9},{25,17},{2,10},{26,18},{3,11},{27,19},{4,12},{... | collective-permute-start | bytes 1179656 | tf_op jit(solution)/shard_map/ppermute | solution.py:357
  23.2 0.2 side_pack.1
  23.4 1.6 %collective-permute-start.2 = (f32[512,128]{1,0:T(8,128)S(1)}, f32[512,128]{1,0:T(8,128)S(1)}, u32[]{:S(2)}, u32[]{:S(2)}) collective-permute-start(f32[512,128]{1,0:T(8,128)S(1)} %side_pack.1), channel_id=1, source_target_pairs={{0,1},{1,0},{2,3},{3,2},{4,5},{5,4},{6,7},{7,6},{8,9},{9,8},{10,11... | collective-permute-start | bytes 786440 | tf_op jit(solution)/shard_map/ppermute | solution.py:397
  25.0 1.3 %collective-permute-start.15 = (f32[64,768]{1,0:T(8,128)S(1)}, f32[64,768]{1,0:T(8,128)S(1)}, u32[]{:S(2)}, u32[]{:S(2)}) collective-permute-start(f32[64,768]{1,0:T(8,128)S(1)} %get-tuple-element.44), channel_id=1, source_target_pairs={{0,8},{24,16},{1,9},{25,17},{2,10},{26,18},{3,11},{27,19},{4,12},{... | collective-permute-start | bytes 589832 | tf_op jit(solution)/shard_map/ppermute | solution.py:357
  26.3 1.3 %collective-permute-start.18 = (f32[64,768]{1,0:T(8,128)S(1)}, f32[64,768]{1,0:T(8,128)S(1)}, u32[]{:S(2)}, u32[]{:S(2)}) collective-permute-start(f32[64,768]{1,0:T(8,128)S(1)} %get-tuple-element.46), channel_id=1, source_target_pairs={{0,8},{24,16},{1,9},{25,17},{2,10},{26,18},{3,11},{27,19},{4,12},{... | collective-permute-start | bytes 589832 | tf_op jit(solution)/shard_map/ppermute | solution.py:357
  27.7 0.7 collective-permute-start.13
  28.4 6.4 %collective-permute-done.9 = f32[128,768]{1,0:T(8,128)S(1)} collective-permute-done((f32[128,768]{1,0:T(8,128)S(1)}, f32[128,768]{1,0:T(8,128)S(1)}, u32[]{:S(2)}, u32[]{:S(2)}) %collective-permute-start.9) | collective-permute-done | bytes 393248 | tf_op jit(solution)/shard_map/ppermute | solution.py:357
  34.8 0.7 collective-permute-start.10
  35.6 6.4 %sides.1 = (f32[192,256]{1,0:T(8,128)S(1)}, f32[192,256]{1,0:T(8,128)S(1)}, f32[192,256]{1,0:T(8,128)S(1)}, f32[192,256]{1,0:T(8,128)S(1)}) custom-call(f32[1]{0:T(128)S(6)} %copy.8.refs_0_.w, f32[1,384,1024]{2,1,0:T(8,128)S(1)} %copy-done, f32[1,384,1024]{2,1,0:T(8,128)S(1)} %copy-done, f32[1,384,1024]{2,1,0:T(8,128)S(1)} %copy-done, ...), custom_call_target="tpu_custom_call" | custom-call | flops 6000000000 | bytes 4194304 | tf_op jit(solution)/shard_map/sides/pallas_call | solution.py:284
  41.9 7.2 %collective-permute-start.6 = (f32[192,256]{1,0:T(8,128)S(1)}, f32[192,256]{1,0:T(8,128)S(1)}, u32[]{:S(2)}, u32[]{:S(2)}) collective-permute-start(f32[192,256]{1,0:T(8,128)S(1)} %get-tuple-element.38), channel_id=1, source_target_pairs={{0,8},{24,16},{1,9},{25,17},{2,10},{26,18},{3,11},{27,19},{4,12},{... | collective-permute-start | bytes 589832 | tf_op jit(solution)/shard_map/ppermute | solution.py:357
  49.1 1.3 %collective-permute-start.3 = (f32[192,256]{1,0:T(8,128)S(1)}, f32[192,256]{1,0:T(8,128)S(1)}, u32[]{:S(2)}, u32[]{:S(2)}) collective-permute-start(f32[192,256]{1,0:T(8,128)S(1)} %get-tuple-element.36), channel_id=1, source_target_pairs={{0,8},{24,16},{1,9},{25,17},{2,10},{26,18},{3,11},{27,19},{4,12},{... | collective-permute-start | bytes 589832 | tf_op jit(solution)/shard_map/ppermute | solution.py:357
  50.5 0.7 collective-permute-start.19
  51.2 1.1 %collective-permute-done.6 = f32[192,256]{1,0:T(8,128)S(1)} collective-permute-done((f32[192,256]{1,0:T(8,128)S(1)}, f32[192,256]{1,0:T(8,128)S(1)}, u32[]{:S(2)}, u32[]{:S(2)}) %collective-permute-start.6) | collective-permute-done | bytes 196640 | tf_op jit(solution)/shard_map/ppermute | solution.py:357
  52.3 0.7 collective-permute-start.16
  53.0 0.7 collective-permute-start.7
  53.7 1.3 %collective-permute-start.14 = (f32[128,768]{1,0:T(8,128)S(1)}, f32[128,768]{1,0:T(8,128)S(1)}, u32[]{:S(2)}, u32[]{:S(2)}) collective-permute-start(f32[128,768]{1,0:T(8,128)S(1)} %add.52.refs_0_), channel_id=1, source_target_pairs={{8,0},{16,24},{9,1},{17,25},{10,2},{18,26},{11,3},{19,27},{12,4},{... | collective-permute-start | bytes 1179656 | tf_op jit(solution)/shard_map/ppermute | solution.py:368
  55.1 1.3 %collective-permute-done.3 = f32[192,256]{1,0:T(8,128)S(1)} collective-permute-done((f32[192,256]{1,0:T(8,128)S(1)}, f32[192,256]{1,0:T(8,128)S(1)}, u32[]{:S(2)}, u32[]{:S(2)}) %collective-permute-start.3) | collective-permute-done | bytes 196640 | tf_op jit(solution)/shard_map/ppermute | solution.py:357
  56.4 1.3 %collective-permute-start.11 = (f32[128,768]{1,0:T(8,128)S(1)}, f32[128,768]{1,0:T(8,128)S(1)}, u32[]{:S(2)}, u32[]{:S(2)}) collective-permute-start(f32[128,768]{1,0:T(8,128)S(1)} %add.50.refs_0_), channel_id=1, source_target_pairs={{8,0},{16,24},{9,1},{17,25},{10,2},{18,26},{11,3},{19,27},{12,4},{... | collective-permute-start | bytes 1179656 | tf_op jit(solution)/shard_map/ppermute | solution.py:368
  57.7 0.7 collective-permute-start.4
  58.5 1.3 %collective-permute-start.20 = (f32[64,768]{1,0:T(8,128)S(1)}, f32[64,768]{1,0:T(8,128)S(1)}, u32[]{:S(2)}, u32[]{:S(2)}) collective-permute-start(f32[64,768]{1,0:T(8,128)S(1)} %add.56.refs_0_), channel_id=1, source_target_pairs={{8,0},{16,24},{9,1},{17,25},{10,2},{18,26},{11,3},{19,27},{12,4},{... | collective-permute-start | bytes 589832 | tf_op jit(solution)/shard_map/ppermute | solution.py:368
  59.8 1.3 %collective-permute-start.17 = (f32[64,768]{1,0:T(8,128)S(1)}, f32[64,768]{1,0:T(8,128)S(1)}, u32[]{:S(2)}, u32[]{:S(2)}) collective-permute-start(f32[64,768]{1,0:T(8,128)S(1)} %add.54.refs_0_), channel_id=1, source_target_pairs={{8,0},{16,24},{9,1},{17,25},{10,2},{18,26},{11,3},{19,27},{12,4},{... | collective-permute-start | bytes 589832 | tf_op jit(solution)/shard_map/ppermute | solution.py:368
  61.1 1.3 %collective-permute-start.8 = (f32[192,256]{1,0:T(8,128)S(1)}, f32[192,256]{1,0:T(8,128)S(1)}, u32[]{:S(2)}, u32[]{:S(2)}) collective-permute-start(f32[192,256]{1,0:T(8,128)S(1)} %add.48.refs_0_), channel_id=1, source_target_pairs={{8,0},{16,24},{9,1},{17,25},{10,2},{18,26},{11,3},{19,27},{12,4},{... | collective-permute-start | bytes 589832 | tf_op jit(solution)/shard_map/ppermute | solution.py:368
  62.5 19.1 %collective-permute-done.20.refs_1_ = f32[64,768]{1,0:T(8,128)S(1)} collective-permute-done((f32[64,768]{1,0:T(8,128)S(1)}, f32[64,768]{1,0:T(8,128)S(1)}, u32[]{:S(2)}, u32[]{:S(2)}) %collective-permute-start.20) | collective-permute-done | bytes 196640 | tf_op jit(solution)/shard_map/ppermute | solution.py:368
  81.5 1.3 %collective-permute-start.5 = (f32[192,256]{1,0:T(8,128)S(1)}, f32[192,256]{1,0:T(8,128)S(1)}, u32[]{:S(2)}, u32[]{:S(2)}) collective-permute-start(f32[192,256]{1,0:T(8,128)S(1)} %add.46.refs_0_), channel_id=1, source_target_pairs={{8,0},{16,24},{9,1},{17,25},{10,2},{18,26},{11,3},{19,27},{12,4},{... | collective-permute-start | bytes 589832 | tf_op jit(solution)/shard_map/ppermute | solution.py:368
  82.8 0.1 finish.6
  82.9 2.8 %collective-permute-done.17.refs_1_ = f32[64,768]{1,0:T(8,128)S(1)} collective-permute-done((f32[64,768]{1,0:T(8,128)S(1)}, f32[64,768]{1,0:T(8,128)S(1)}, u32[]{:S(2)}, u32[]{:S(2)}) %collective-permute-start.17) | collective-permute-done | bytes 196640 | tf_op jit(solution)/shard_map/ppermute | solution.py:368
  85.8 0.2 finish.8
  86.0 0.1 finish.9
  86.1 3.8 %collective-permute-done.8.refs_1_ = f32[192,256]{1,0:T(8,128)S(1)} collective-permute-done((f32[192,256]{1,0:T(8,128)S(1)}, f32[192,256]{1,0:T(8,128)S(1)}, u32[]{:S(2)}, u32[]{:S(2)}) %collective-permute-start.8) | collective-permute-done | bytes 196640 | tf_op jit(solution)/shard_map/ppermute | solution.py:368
  90.0 4.1 %collective-permute-done.5.refs_1_ = f32[192,256]{1,0:T(8,128)S(1)} collective-permute-done((f32[192,256]{1,0:T(8,128)S(1)}, f32[192,256]{1,0:T(8,128)S(1)}, u32[]{:S(2)}, u32[]{:S(2)}) %collective-permute-start.5) | collective-permute-done | bytes 196640 | tf_op jit(solution)/shard_map/ppermute | solution.py:368
  94.2 0.1 finish.11
  94.3 2.9 %collective-permute-start.21 = (f32[8,128]{1,0:T(8,128)S(1)}, f32[8,128]{1,0:T(8,128)S(1)}, u32[]{:S(2)}, u32[]{:S(2)}) collective-permute-start(f32[8,128]{1,0:T(8,128)S(1)} %get-tuple-element.53), channel_id=1, source_target_pairs={{0,2},{2,0},{4,6},{6,4},{1,3},{3,1},{5,7},{7,5},{8,10},{10,8},{12,... | collective-permute-start | bytes 12296 | tf_op jit(solution)/shard_map/ppermute | solution.py:319
  97.2 0.8 collective-permute-done.21
  98.0 0.4 collective-permute-start.22
  98.4 3.2 %collective-permute-done.22 = f32[8,128]{1,0:T(8,128)S(1)} collective-permute-done((f32[8,128]{1,0:T(8,128)S(1)}, f32[8,128]{1,0:T(8,128)S(1)}, u32[]{:S(2)}, u32[]{:S(2)}) %collective-permute-start.22) | collective-permute-done | bytes 4128 | tf_op jit(solution)/shard_map/ppermute | solution.py:319
  101.6 1.5 %collective-permute-start.23 = (f32[8,128]{1,0:T(8,128)S(1)}, f32[8,128]{1,0:T(8,128)S(1)}, u32[]{:S(2)}, u32[]{:S(2)}) collective-permute-start(f32[8,128]{1,0:T(8,128)S(1)} %add.58), channel_id=1, source_target_pairs={{0,1},{1,0},{2,3},{3,2},{4,5},{5,4},{6,7},{7,6},{8,9},{9,8},{10,11... | collective-permute-start | bytes 12296 | tf_op jit(solution)/shard_map/ppermute | solution.py:319
  103.2 2.1 %collective-permute-done.23 = f32[8,128]{1,0:T(8,128)S(1)} collective-permute-done((f32[8,128]{1,0:T(8,128)S(1)}, f32[8,128]{1,0:T(8,128)S(1)}, u32[]{:S(2)}, u32[]{:S(2)}) %collective-permute-start.23) | collective-permute-done | bytes 4128 | tf_op jit(solution)/shard_map/ppermute | solution.py:319
  105.2 2.1 %assemble.1 = (f32[384,1024]{1,0:T(8,128)}, f32[1,384,1024]{2,1,0:T(8,128)}) custom-call(f32[8,128]{1,0:T(8,128)S(1)} %add.59.refs_0_, f32[64,768]{1,0:T(8,128)S(1)} %get-tuple-element.54.refs_1_, f32[64,768]{1,0:T(8,128)S(1)} %get-tuple-element.55.refs_2_, f32[128,768]{1,0:T(8,128)S(1)} %get-tuple-element.56.refs_3_, ...), custom_call_target="tpu_custom_call" | custom-call | flops 4000000 | bytes 4194304 | tf_op jit(solution)/shard_map/assemble/pallas_call | solution.py:337
  (41 shorter events, 0.6 us)
Async XLA Ops:
  1.3 1.4 %copy-start = (f32[1,384,1024]{2,1,0:T(8,128)S(1)}, f32[1,384,1024]{2,1,0:T(8,128)}, u32[]{:S(2)}) copy-start(f32[1,384,1024]{2,1,0:T(8,128)} %refs_2_.5) | copy-start | bytes 4718596
  2.7 1.4 %copy-start.1 = (f32[1,384,1024]{2,1,0:T(8,128)S(1)}, f32[1,384,1024]{2,1,0:T(8,128)}, u32[]{:S(2)}) copy-start(f32[1,384,1024]{2,1,0:T(8,128)} %refs_4_.5) | copy-start | bytes 4718596
  4.1 1.2 %copy-start.2 = (bf16[2,448,512]{2,1,0:T(8,128)(2,1)S(1)}, bf16[2,448,512]{2,1,0:T(8,128)(2,1)}, u32[]{:S(2)}) copy-start(bf16[2,448,512]{2,1,0:T(8,128)(2,1)} %constant.6.clone.refs_5_.refs_17_.tb) | copy-start | bytes 2752516
  5.3 1.0 copy-start.5
  6.3 5.8 %copy-start.6 = (bf16[2,512,256]{2,1,0:T(8,128)(2,1)S(1)}, bf16[2,512,256]{2,1,0:T(8,128)(2,1)}, u32[]{:S(2)}) copy-start(bf16[2,512,256]{2,1,0:T(8,128)(2,1)} %constant.7.clone.refs_6_.cb) | copy-start | bytes 1572868
  8.4 10.1 %collective-permute-start = (f32[96,1024]{1,0:T(8,128)S(1)}, f32[96,1024]{1,0:T(8,128)S(1)}, u32[]{:S(2)}, u32[]{:S(2)}) collective-permute-start(f32[96,1024]{1,0:T(8,128)S(1)} %get-tuple-element.34), channel_id=1, source_target_pairs={{0,2},{2,4},{4,6},{1,3},{3,5},{5,7},{8,10},{10,12},{12,14},{9,11},... | collective-permute-start | bytes 1179656 | tf_op jit(solution)/shard_map/ppermute | solution.py:388
  10.8 7.7 %collective-permute-start.1 = (f32[96,1024]{1,0:T(8,128)S(1)}, f32[96,1024]{1,0:T(8,128)S(1)}, u32[]{:S(2)}, u32[]{:S(2)}) collective-permute-start(f32[96,1024]{1,0:T(8,128)S(1)} %get-tuple-element.35), channel_id=1, source_target_pairs={{2,0},{4,2},{6,4},{3,1},{5,3},{7,5},{10,8},{12,10},{14,12},{11,9},... | collective-permute-start | bytes 1179656 | tf_op jit(solution)/shard_map/ppermute | solution.py:387
  14.2 13.5 %collective-permute-start.12 = (f32[128,768]{1,0:T(8,128)S(1)}, f32[128,768]{1,0:T(8,128)S(1)}, u32[]{:S(2)}, u32[]{:S(2)}) collective-permute-start(f32[128,768]{1,0:T(8,128)S(1)} %get-tuple-element.42), channel_id=1, source_target_pairs={{0,8},{24,16},{1,9},{25,17},{2,10},{26,18},{3,11},{27,19},{4,12},{... | collective-permute-start | bytes 1179656 | tf_op jit(solution)/shard_map/ppermute | solution.py:357
  21.7 13.1 %collective-permute-start.9 = (f32[128,768]{1,0:T(8,128)S(1)}, f32[128,768]{1,0:T(8,128)S(1)}, u32[]{:S(2)}, u32[]{:S(2)}) collective-permute-start(f32[128,768]{1,0:T(8,128)S(1)} %get-tuple-element.40), channel_id=1, source_target_pairs={{0,8},{24,16},{1,9},{25,17},{2,10},{26,18},{3,11},{27,19},{4,12},{... | collective-permute-start | bytes 1179656 | tf_op jit(solution)/shard_map/ppermute | solution.py:357
  23.4 12.1 %copy-start.3 = (bf16[2,448,512]{2,1,0:T(8,128)(2,1)S(1)}, bf16[2,448,512]{2,1,0:T(8,128)(2,1)}, u32[]{:S(2)}) copy-start(bf16[2,448,512]{2,1,0:T(8,128)(2,1)} %constant.6.clone.refs_5_.refs_17_.tb) | copy-start | bytes 2752516
  23.4 12.1 %copy-start.4 = (bf16[2,384,384]{2,1,0:T(8,128)(2,1)S(1)}, bf16[2,384,384]{2,1,0:T(8,128)(2,1)}, u32[]{:S(2)}) copy-start(bf16[2,384,384]{2,1,0:T(8,128)(2,1)} %constant.8.clone.refs_18_) | copy-start | bytes 1769476
  23.4 12.1 %collective-permute-start.2 = (f32[512,128]{1,0:T(8,128)S(1)}, f32[512,128]{1,0:T(8,128)S(1)}, u32[]{:S(2)}, u32[]{:S(2)}) collective-permute-start(f32[512,128]{1,0:T(8,128)S(1)} %side_pack.1), channel_id=1, source_target_pairs={{0,1},{1,0},{2,3},{3,2},{4,5},{5,4},{6,7},{7,6},{8,9},{9,8},{10,11... | collective-permute-start | bytes 786440 | tf_op jit(solution)/shard_map/ppermute | solution.py:397
  25.0 25.4 %collective-permute-start.15 = (f32[64,768]{1,0:T(8,128)S(1)}, f32[64,768]{1,0:T(8,128)S(1)}, u32[]{:S(2)}, u32[]{:S(2)}) collective-permute-start(f32[64,768]{1,0:T(8,128)S(1)} %get-tuple-element.44), channel_id=1, source_target_pairs={{0,8},{24,16},{1,9},{25,17},{2,10},{26,18},{3,11},{27,19},{4,12},{... | collective-permute-start | bytes 589832 | tf_op jit(solution)/shard_map/ppermute | solution.py:357
  26.3 22.8 %collective-permute-start.18 = (f32[64,768]{1,0:T(8,128)S(1)}, f32[64,768]{1,0:T(8,128)S(1)}, u32[]{:S(2)}, u32[]{:S(2)}) collective-permute-start(f32[64,768]{1,0:T(8,128)S(1)} %get-tuple-element.46), channel_id=1, source_target_pairs={{0,8},{24,16},{1,9},{25,17},{2,10},{26,18},{3,11},{27,19},{4,12},{... | collective-permute-start | bytes 589832 | tf_op jit(solution)/shard_map/ppermute | solution.py:357
  27.7 25.3 %collective-permute-start.13 = (f32[128,768]{1,0:T(8,128)S(1)}, f32[128,768]{1,0:T(8,128)S(1)}, u32[]{:S(2)}, u32[]{:S(2)}) collective-permute-start(f32[128,768]{1,0:T(8,128)S(1)} %add.51), channel_id=1, source_target_pairs={{8,16},{16,8},{9,17},{17,9},{10,18},{18,10},{11,19},{19,11},{12,20... | collective-permute-start | bytes 1179656 | tf_op jit(solution)/shard_map/ppermute | solution.py:361
  34.8 18.9 %collective-permute-start.10 = (f32[128,768]{1,0:T(8,128)S(1)}, f32[128,768]{1,0:T(8,128)S(1)}, u32[]{:S(2)}, u32[]{:S(2)}) collective-permute-start(f32[128,768]{1,0:T(8,128)S(1)} %add.49), channel_id=1, source_target_pairs={{8,16},{16,8},{9,17},{17,9},{10,18},{18,10},{11,19},{19,11},{12,20... | collective-permute-start | bytes 1179656 | tf_op jit(solution)/shard_map/ppermute | solution.py:361
  41.9 10.3 %collective-permute-start.6 = (f32[192,256]{1,0:T(8,128)S(1)}, f32[192,256]{1,0:T(8,128)S(1)}, u32[]{:S(2)}, u32[]{:S(2)}) collective-permute-start(f32[192,256]{1,0:T(8,128)S(1)} %get-tuple-element.38), channel_id=1, source_target_pairs={{0,8},{24,16},{1,9},{25,17},{2,10},{26,18},{3,11},{27,19},{4,12},{... | collective-permute-start | bytes 589832 | tf_op jit(solution)/shard_map/ppermute | solution.py:357
  49.1 7.3 %collective-permute-start.3 = (f32[192,256]{1,0:T(8,128)S(1)}, f32[192,256]{1,0:T(8,128)S(1)}, u32[]{:S(2)}, u32[]{:S(2)}) collective-permute-start(f32[192,256]{1,0:T(8,128)S(1)} %get-tuple-element.36), channel_id=1, source_target_pairs={{0,8},{24,16},{1,9},{25,17},{2,10},{26,18},{3,11},{27,19},{4,12},{... | collective-permute-start | bytes 589832 | tf_op jit(solution)/shard_map/ppermute | solution.py:357
  50.5 7.2 %collective-permute-start.19 = (f32[64,768]{1,0:T(8,128)S(1)}, f32[64,768]{1,0:T(8,128)S(1)}, u32[]{:S(2)}, u32[]{:S(2)}) collective-permute-start(f32[64,768]{1,0:T(8,128)S(1)} %add.55), channel_id=1, source_target_pairs={{8,16},{16,8},{9,17},{17,9},{10,18},{18,10},{11,19},{19,11},{12,20... | collective-permute-start | bytes 589832 | tf_op jit(solution)/shard_map/ppermute | solution.py:361
  52.3 6.2 %collective-permute-start.16 = (f32[64,768]{1,0:T(8,128)S(1)}, f32[64,768]{1,0:T(8,128)S(1)}, u32[]{:S(2)}, u32[]{:S(2)}) collective-permute-start(f32[64,768]{1,0:T(8,128)S(1)} %add.53), channel_id=1, source_target_pairs={{8,16},{16,8},{9,17},{17,9},{10,18},{18,10},{11,19},{19,11},{12,20... | collective-permute-start | bytes 589832 | tf_op jit(solution)/shard_map/ppermute | solution.py:361
  53.0 6.8 %collective-permute-start.7 = (f32[192,256]{1,0:T(8,128)S(1)}, f32[192,256]{1,0:T(8,128)S(1)}, u32[]{:S(2)}, u32[]{:S(2)}) collective-permute-start(f32[192,256]{1,0:T(8,128)S(1)} %add.47), channel_id=1, source_target_pairs={{8,16},{16,8},{9,17},{17,9},{10,18},{18,10},{11,19},{19,11},{12,20... | collective-permute-start | bytes 589832 | tf_op jit(solution)/shard_map/ppermute | solution.py:361
  53.7 32.1 %collective-permute-start.14 = (f32[128,768]{1,0:T(8,128)S(1)}, f32[128,768]{1,0:T(8,128)S(1)}, u32[]{:S(2)}, u32[]{:S(2)}) collective-permute-start(f32[128,768]{1,0:T(8,128)S(1)} %add.52.refs_0_), channel_id=1, source_target_pairs={{8,0},{16,24},{9,1},{17,25},{10,2},{18,26},{11,3},{19,27},{12,4},{... | collective-permute-start | bytes 1179656 | tf_op jit(solution)/shard_map/ppermute | solution.py:368
  56.4 29.6 %collective-permute-start.11 = (f32[128,768]{1,0:T(8,128)S(1)}, f32[128,768]{1,0:T(8,128)S(1)}, u32[]{:S(2)}, u32[]{:S(2)}) collective-permute-start(f32[128,768]{1,0:T(8,128)S(1)} %add.50.refs_0_), channel_id=1, source_target_pairs={{8,0},{16,24},{9,1},{17,25},{10,2},{18,26},{11,3},{19,27},{12,4},{... | collective-permute-start | bytes 1179656 | tf_op jit(solution)/shard_map/ppermute | solution.py:368
  57.7 3.4 %collective-permute-start.4 = (f32[192,256]{1,0:T(8,128)S(1)}, f32[192,256]{1,0:T(8,128)S(1)}, u32[]{:S(2)}, u32[]{:S(2)}) collective-permute-start(f32[192,256]{1,0:T(8,128)S(1)} %add.45), channel_id=1, source_target_pairs={{8,16},{16,8},{9,17},{17,9},{10,18},{18,10},{11,19},{19,11},{12,20... | collective-permute-start | bytes 589832 | tf_op jit(solution)/shard_map/ppermute | solution.py:361
  58.5 23.1 %collective-permute-start.20 = (f32[64,768]{1,0:T(8,128)S(1)}, f32[64,768]{1,0:T(8,128)S(1)}, u32[]{:S(2)}, u32[]{:S(2)}) collective-permute-start(f32[64,768]{1,0:T(8,128)S(1)} %add.56.refs_0_), channel_id=1, source_target_pairs={{8,0},{16,24},{9,1},{17,25},{10,2},{18,26},{11,3},{19,27},{12,4},{... | collective-permute-start | bytes 589832 | tf_op jit(solution)/shard_map/ppermute | solution.py:368
  59.8 26.0 %collective-permute-start.17 = (f32[64,768]{1,0:T(8,128)S(1)}, f32[64,768]{1,0:T(8,128)S(1)}, u32[]{:S(2)}, u32[]{:S(2)}) collective-permute-start(f32[64,768]{1,0:T(8,128)S(1)} %add.54.refs_0_), channel_id=1, source_target_pairs={{8,0},{16,24},{9,1},{17,25},{10,2},{18,26},{11,3},{19,27},{12,4},{... | collective-permute-start | bytes 589832 | tf_op jit(solution)/shard_map/ppermute | solution.py:368
  61.1 28.8 %collective-permute-start.8 = (f32[192,256]{1,0:T(8,128)S(1)}, f32[192,256]{1,0:T(8,128)S(1)}, u32[]{:S(2)}, u32[]{:S(2)}) collective-permute-start(f32[192,256]{1,0:T(8,128)S(1)} %add.48.refs_0_), channel_id=1, source_target_pairs={{8,0},{16,24},{9,1},{17,25},{10,2},{18,26},{11,3},{19,27},{12,4},{... | collective-permute-start | bytes 589832 | tf_op jit(solution)/shard_map/ppermute | solution.py:368
  81.5 12.6 %collective-permute-start.5 = (f32[192,256]{1,0:T(8,128)S(1)}, f32[192,256]{1,0:T(8,128)S(1)}, u32[]{:S(2)}, u32[]{:S(2)}) collective-permute-start(f32[192,256]{1,0:T(8,128)S(1)} %add.46.refs_0_), channel_id=1, source_target_pairs={{8,0},{16,24},{9,1},{17,25},{10,2},{18,26},{11,3},{19,27},{12,4},{... | collective-permute-start | bytes 589832 | tf_op jit(solution)/shard_map/ppermute | solution.py:368
  94.3 3.8 %collective-permute-start.21 = (f32[8,128]{1,0:T(8,128)S(1)}, f32[8,128]{1,0:T(8,128)S(1)}, u32[]{:S(2)}, u32[]{:S(2)}) collective-permute-start(f32[8,128]{1,0:T(8,128)S(1)} %get-tuple-element.53), channel_id=1, source_target_pairs={{0,2},{2,0},{4,6},{6,4},{1,3},{3,1},{5,7},{7,5},{8,10},{10,8},{12,... | collective-permute-start | bytes 12296 | tf_op jit(solution)/shard_map/ppermute | solution.py:319
  98.0 3.6 %collective-permute-start.22 = (f32[8,128]{1,0:T(8,128)S(1)}, f32[8,128]{1,0:T(8,128)S(1)}, u32[]{:S(2)}, u32[]{:S(2)}) collective-permute-start(f32[8,128]{1,0:T(8,128)S(1)} %add.57), channel_id=1, source_target_pairs={{0,4},{2,6},{4,0},{6,2},{1,5},{3,7},{5,1},{7,3},{8,12},{10,14},{12... | collective-permute-start | bytes 12296 | tf_op jit(solution)/shard_map/ppermute | solution.py:319
  101.6 3.6 %collective-permute-start.23 = (f32[8,128]{1,0:T(8,128)S(1)}, f32[8,128]{1,0:T(8,128)S(1)}, u32[]{:S(2)}, u32[]{:S(2)}) collective-permute-start(f32[8,128]{1,0:T(8,128)S(1)} %add.58), channel_id=1, source_target_pairs={{0,1},{1,0},{2,3},{3,2},{4,5},{5,4},{6,7},{7,6},{8,9},{9,8},{10,11... | collective-permute-start | bytes 12296 | tf_op jit(solution)/shard_map/ppermute | solution.py:319

commit v2 on v0

v2 whole, which is shorter than its diff:
```python
import jax
import jax.numpy as jnp
import numpy as np
from jax import lax
from jax.experimental import pallas as pl
from jax.experimental.pallas import tpu as pltpu
from jax.sharding import PartitionSpec as P

HALF = 32
SIGMA = 16
WIDE = 2 * HALF
LANES = 128
BLOCK = 192
LAG = 3
F32 = jnp.float32
BF16 = jnp.bfloat16


def inverse_total():
    taps = np.arange(-HALF, HALF + 1, dtype=np.float64)
    return float(1.0 / np.exp(-taps * taps / (2.0 * SIGMA * SIGMA)).sum())


def split(x):
    high = x.astype(BF16)
    low = (x - high.astype(F32)).astype(BF16)
    return high, low


def band(rows, cols, shift):
    r = lax.broadcasted_iota(jnp.int32, (rows, cols), 0)
    c = lax.broadcasted_iota(jnp.int32, (rows, cols), 1)
    off = (r - c - shift).astype(F32)
    values = jnp.exp(off * off * (-0.5 / (SIGMA * SIGMA))) * inverse_total()
    return split(jnp.where(jnp.abs(off) <= HALF, values, 0.0))


def mm(a, b):
    return jnp.dot(a, b, preferred_element_type=F32)


def times(left, right):
    (lh, ll), (rh, rl) = left, right
    return mm(lh, rh) + mm(ll, rh) + mm(lh, rl)


def part(pair, rows=slice(None), cols=slice(None)):
    return pair[0][rows, cols], pair[1][rows, cols]


def rows_of(tall, x):
    x = split(x)
    n = x[0].shape[0] - WIDE
    out = []
    for start in range(0, n, BLOCK):
        m = min(BLOCK, n - start)
        out.append(times(part(tall, slice(m), slice(m + WIDE)), part(x, slice(start, start + m + WIDE))))
    return out[0] if len(out) == 1 else jnp.concatenate(out, axis=0)


def cols_all(wide, x):
    width = x.shape[1]
    x = split(x)
    out = []
    for start in range(0, width, 256):
        lo, hi = max(start - LANES, 0), min(start + 256 + LANES, width)
        rows = slice(lo - (start - LANES), hi - (start - LANES))
        out.append(times(part(x, cols=slice(lo, hi)), part(wide, rows)))
    return jnp.concatenate(out, axis=1)


def cols_inner(wide, x):
    width = x.shape[1]
    x = split(x)
    out = []
    for start in range(0, width - 2 * LANES, 256):
        stop = min(start + 512, width)
        band_part = part(wide, slice(stop - start), slice(stop - start - 2 * LANES))
        out.append(times(part(x, cols=slice(start, stop)), band_part))
    return jnp.concatenate(out, axis=1)


def quotient(dens, kv):
    return jnp.where(dens > 0.0, dens / kv, 0.0)


def pair_of(ref):
    return ref[0], ref[1]


def log_term(weight, scal, ku):
    return weight * jnp.log(scal * ku)


def vmem():
    return pl.BlockSpec(memory_space=pltpu.VMEM)


def smem():
    return pl.BlockSpec(memory_space=pltpu.SMEM)


def hbm():
    return pl.BlockSpec(memory_space=pltpu.HBM)


def call(body, out, in_specs, name, deps=(), scratch=()):
    n = len(in_specs)

    def run(*refs):
        body(*refs[:n], *refs[n + len(deps) :])

    kernel = pl.pallas_call(
        run,
        out_shape=[jax.ShapeDtypeStruct(s, F32) if isinstance(s, tuple) else s for s in out],
        in_specs=list(in_specs) + [pl.BlockSpec(memory_space=pl.ANY)] * len(deps),
        out_specs=[vmem()] * len(out),
        scratch_shapes=list(scratch),
        compiler_params=pltpu.CompilerParams(vmem_limit_bytes=40 * 1024 * 1024),
        cost_estimate=pl.CostEstimate(flops=0, bytes_accessed=0, transcendentals=0),
        name=name,
    )
    return lambda *args: kernel(*args, *deps)


def first_chunk(weights, scaling, densities):
    rows, cols = scaling.shape[1:]
    tall_n, dens_n = 3 * WIDE, 2 * WIDE

    def body(w, s_hbm, d_hbm, term, ku, tall_ref, wide_ref, one, two, s, d, sems):
        odd = lax.rem(lax.axis_index("gx"), 2)
        ends = ((one, (1 - odd) * (rows - WIDE), (1 - odd) * (rows - HALF)), (two, odd * (rows - WIDE), odd * (rows - HALF)))
        copies = [
            pltpu.make_async_copy(s_hbm.at[0, pl.ds(0, tall_n)], s, sems.at[0]),
            pltpu.make_async_copy(d_hbm.at[0, pl.ds(HALF, dens_n)], d, sems.at[1]),
        ]
        for k, (ref, s_row, d_row) in enumerate(ends):
            s_row, d_row = pl.multiple_of(s_row, HALF), pl.multiple_of(d_row, HALF)
            copies.append(pltpu.make_async_copy(s_hbm.at[0, pl.ds(s_row, WIDE)], ref.at[pl.ds(0, WIDE)], sems.at[2 + 2 * k]))
            copies.append(pltpu.make_async_copy(d_hbm.at[0, pl.ds(d_row, HALF)], ref.at[pl.ds(WIDE, HALF)], sems.at[3 + 2 * k]))
        for copy in copies:
            copy.start()
        tall = band(BLOCK, BLOCK + WIDE, -HALF)
        wide = band(512, 256, LANES)
        tall_ref[0], tall_ref[1] = tall
        wide_ref[0], wide_ref[1] = wide
        copies[0].wait()
        kv = cols_all(wide, rows_of(tall, s[...]))
        copies[1].wait()
        u = quotient(d[...], kv)
        k = cols_inner(wide, rows_of(tall, u))
        ku[...] = k
        term[...] = log_term(w[0], s[WIDE : 2 * WIDE, LANES:-LANES], k)
        for copy in copies[2:]:
            copy.wait()

    inner = (WIDE, cols - 2 * LANES)
    pack = (WIDE + HALF, cols)
    bands = [jax.ShapeDtypeStruct((2, BLOCK, BLOCK + WIDE), BF16), jax.ShapeDtypeStruct((2, 512, 256), BF16)]
    scratch = [pltpu.VMEM((tall_n, cols), F32), pltpu.VMEM((dens_n, cols), F32), pltpu.SemaphoreType.DMA((6,))]
    return call(body, [inner, inner, *bands, pack, pack], [smem(), hbm(), hbm()], "first", (), scratch)(
        weights, scaling, densities
    )


def inner_chunks(weights, scaling, densities, tall, wide, deps):
    rows, cols = scaling.shape[1:]
    count = rows // WIDE - 3

    def body(w, s, d, tall_ref, wide_ref, *outs):
        tall, wide = pair_of(tall_ref), pair_of(wide_ref)
        kv = cols_all(wide, rows_of(tall, s[0, WIDE:]))
        u = quotient(d[0, WIDE + HALF : rows - HALF], kv)
        k = cols_inner(wide, rows_of(tall, u))
        term = log_term(w[0], s[0, 2 * WIDE : rows - WIDE, LANES:-LANES], k)
        for p in range(count):
            outs[2 * p][...] = term[p * WIDE : (p + 1) * WIDE]
            outs[2 * p + 1][...] = k[p * WIDE : (p + 1) * WIDE]

    out = [(WIDE, cols - 2 * LANES)] * (2 * count)
    return call(body, out, [smem()] + [vmem()] * 4, "inner", deps)(weights, scaling, densities, tall, wide)


def halo_rows(one, two, cols=slice(None)):
    here, count = lax.axis_index("gx"), lax.axis_size("gx")
    odd = lax.rem(here, 2) == 1
    near, far = one[:, cols], two[:, cols]
    far = jnp.where((here == 0) | (here == count - 1), 0.0, far)
    return jnp.where(odd, near, far), jnp.where(odd, far, near)


def edge_chunks(weights, scaling, densities, tall, wide, one, two, deps):
    rows, cols = scaling.shape[1:]

    def body(w, s, d, tall_ref, wide_ref, one_ref, two_ref, *outs):
        tall, wide = pair_of(tall_ref), pair_of(wide_ref)
        up, down = halo_rows(one_ref, two_ref)
        scal = (
            jnp.concatenate([up[:WIDE], s[0, : 2 * WIDE]], axis=0),
            jnp.concatenate([s[0, rows - 2 * WIDE :], down[:WIDE]], axis=0),
        )
        dens = jnp.concatenate([up[WIDE:], d[0, : 3 * HALF], d[0, rows - 3 * HALF :], down[WIDE:]], axis=0)
        kv = cols_all(wide, jnp.concatenate([rows_of(tall, x) for x in scal], axis=0))
        u = quotient(dens, kv)
        k = cols_inner(wide, jnp.concatenate([rows_of(tall, x) for x in (u[: 2 * WIDE], u[2 * WIDE :])], axis=0))
        for p, start in enumerate((0, rows - WIDE)):
            kp = k[p * WIDE : (p + 1) * WIDE]
            outs[2 * p][...] = log_term(w[0], s[0, start : start + WIDE, LANES:-LANES], kp)
            outs[2 * p + 1][...] = kp

    out = [(WIDE, cols - 2 * LANES)] * 4
    return call(body, out, [smem()] + [vmem()] * 6, "edges", deps)(
        weights, scaling, densities, tall, wide, one, two
    )


def side_pack(scaling, densities, one, two, deps):
    rows, cols = scaling.shape[1:]
    tall = rows + 2 * WIDE
    pair = lax.axis_size("gy") == 2

    def body(s, d, one_ref, two_ref, *outs):
        lane = lax.broadcasted_iota(jnp.int32, (tall, LANES), 1)
        zero = jnp.zeros((HALF, LANES), F32)

        def tallest(which):
            up, down = halo_rows(one_ref, two_ref, which)
            scal = jnp.concatenate([up[:WIDE], s[0, :, which], down[:WIDE]], axis=0)
            dens = jnp.concatenate([zero, up[WIDE:], d[0, :, which], down[WIDE:], zero], axis=0)
            return scal, dens

        scal, dens = tallest(slice(cols - LANES, cols))
        last = jnp.where(lane >= WIDE, scal, pltpu.roll(dens, HALF, 1))
        scal, dens = tallest(slice(0, LANES))
        first = jnp.where(lane < WIDE, scal, pltpu.roll(dens, WIDE, 1))
        if pair:
            outs[0][...] = jnp.where(lax.axis_index("gy") == 0, last, first)
        else:
            outs[0][...] = last
            outs[1][...] = first

    out = [(tall, LANES)] * (1 if pair else 2)
    return call(body, out, [vmem()] * 4, "side_pack", deps)(scaling, densities, one, two)


def side_chunks(weights, scaling, densities, tall, one, two, from_left, from_right, deps):
    rows, cols = scaling.shape[1:]
    long = rows + 2 * WIDE
    width = cols - 2 * LANES
    count = rows * 2 * LANES // (WIDE * width)
    blocks = width // (2 * LANES)
    pair = lax.axis_size("gy") == 2

    def body(w, s, d, tall_ref, one_ref, two_ref, left_ref, right_ref, *outs):
        tall = pair_of(tall_ref)
        short = band(BLOCK + WIDE, BLOCK, HALF)
        here, last = lax.axis_index("gy"), lax.axis_size("gy") - 1
        left = jnp.where(here == 0, 0.0, left_ref[...])
        right = jnp.where(here == last, 0.0, right_ref[...])
        lane = lax.broadcasted_iota(jnp.int32, (long, LANES), 1)
        inner = slice(HALF, long - HALF)

        def block(which):
            up, down = halo_rows(one_ref, two_ref, which)
            scal = jnp.concatenate([up[:WIDE], s[0, :, which], down[:WIDE]], axis=0)
            dens = jnp.concatenate([up[WIDE:], d[0, :, which], down[WIDE:]], axis=0)
            return pltpu.roll(scal, WIDE, 1), dens

        def side(scal, dens):
            kv = times(split(rows_of(tall, scal)), short)
            u = quotient(dens, kv)
            r = split(rows_of(tall, u))
            return times(r, part(short, slice(BLOCK), slice(LANES)))

        small = lane[inner]
        (s0, d0), (s1, d1) = block(slice(0, LANES)), block(slice(LANES, 2 * LANES))
        scal = jnp.concatenate([jnp.where(lane < WIDE, pltpu.roll(left, WIDE, 1), s0), jnp.where(lane < WIDE, s0, s1)], axis=1)
        d0, d1 = pltpu.roll(d0, HALF, 1), pltpu.roll(d1, HALF, 1)
        dens = jnp.concatenate(
            [jnp.where(small < HALF, left[inner], d0), jnp.where(small < HALF, d0, d1)[:, :WIDE]], axis=1
        )
        k0 = side(scal, dens)
        (s0, d0), (s1, d1) = block(slice(cols - 2 * LANES, cols - LANES)), block(slice(cols - LANES, cols))
        scal = jnp.concatenate([jnp.where(lane < WIDE, s0, s1), jnp.where(lane < WIDE, s1, pltpu.roll(right, WIDE, 1))], axis=1)
        d0, d1 = pltpu.roll(d0, HALF, 1), pltpu.roll(d1, HALF, 1)
        halo = pltpu.roll(right, LANES - HALF, 1)[inner]
        dens = jnp.concatenate(
            [jnp.where(small < HALF, d0, d1), jnp.where(small < HALF, d1, halo)[:, :WIDE]], axis=1
        )
        k1 = side(scal, dens)
        for p in range(count):
            for b in range(blocks):
                r = slice((p * blocks + b) * WIDE, (p * blocks + b + 1) * WIDE)
                c = 2 * LANES * b
                outs[2 * p][:, c : c + LANES] = log_term(w[0], s[0, r, :LANES], k0[r])
                outs[2 * p][:, c + LANES : c + 2 * LANES] = log_term(w[0], s[0, r, cols - LANES :], k1[r])
                outs[2 * p + 1][:, c : c + LANES] = k0[r]
                outs[2 * p + 1][:, c + LANES : c + 2 * LANES] = k1[r]

    out = [(WIDE, width)] * (2 * count)
    return call(body, out, [smem()] + [vmem()] * 7, "sides", deps)(
        weights, scaling, densities, tall, one, two, from_left, from_right
    )


def add(a, b, deps):
    def body(a_ref, b_ref, out_ref):
        out_ref[...] = a_ref[...] + b_ref[...]

    return call(body, [a.shape], [vmem()] * 2, "add", deps)(a, b)[0]


def in_middle():
    z = lax.axis_index("map")
    return (z == 1) | (z == 2)


def add_and_pass(a, b, term, deps):
    def body(a_ref, b_ref, term_ref, out_ref, send_ref):
        total = a_ref[...] + b_ref[...]
        out_ref[...] = total
        send_ref[...] = jnp.where(in_middle(), total, term_ref[...])

    return call(body, [a.shape, a.shape], [vmem()] * 3, "add_and_pass", deps)(a, b, term)


def finish(held, landed, ku, mass, deps):
    inputs = [held] + ([] if landed is None else [landed]) + [ku] + ([] if mass is None else [mass])
    n = len(inputs)

    def body(*refs):
        raw_ref, quot_ref, mass_ref = refs[n:]
        logs = refs[0][...]
        if landed is not None:
            logs = jnp.where(in_middle(), logs, refs[1][...])
        raw = jnp.exp(logs)
        raw_ref[...] = raw
        quot_ref[...] = raw / refs[1 if landed is None else 2][...]
        rows, cols = raw.shape
        total = jnp.sum(raw.reshape(rows // 8, 8, cols), axis=0)
        total = sum(total[:, k : k + LANES] for k in range(0, cols, LANES))
        mass_ref[...] = total if mass is None else total + refs[n - 1][...]

    return call(body, [held.shape, held.shape, (8, LANES)], [vmem()] * n, "finish", deps)(*inputs)


def sum_grid(mass):
    for axis in ("gx", "gy"):
        count = lax.axis_size(axis)
        if count & (count - 1):
            mass = lax.psum(mass, axis)
            continue
        step = 1
        while step < count:
            mass = mass + lax.ppermute(mass, axis, [(i, i ^ step) for i in range(count)])
            step *= 2
    return mass


def assemble(mass, places, raws, quots, rows, cols, cells):
    n = len(places)

    def body(*refs):
        mass_ref, raw, quot = refs[0], refs[1 : 1 + n], refs[1 + n : 1 + 2 * n]
        bary, new = refs[-2:]
        scale = cells / jnp.sum(mass_ref[...])
        for k, place in enumerate(places):
            for r0, c0, width, from_col in place:
                piece = (slice(None), slice(from_col, from_col + width))
                bary[r0 : r0 + WIDE, c0 : c0 + width] = raw[k][piece] * scale
                new[0, r0 : r0 + WIDE, c0 : c0 + width] = quot[k][piece] * scale

    return call(body, [(rows, cols), (1, rows, cols)], [vmem()] * (1 + 2 * n), "assemble")(mass, *raws, *quots)


def chunk_places(rows, cols):
    width = cols - 2 * LANES
    starts = list(range(WIDE, rows - WIDE, WIDE)) + [0, rows - WIDE]
    places = [[(r, LANES, width, 0)] for r in starts]
    blocks = width // (2 * LANES)
    for p in range(rows * 2 * LANES // (WIDE * width)):
        place = []
        for b in range(blocks):
            r = (p * blocks + b) * WIDE
            place += [(r, 0, LANES, 2 * LANES * b), (r, cols - LANES, LANES, 2 * LANES * b + LANES)]
        places.append(place)
    return places


def local(densities, scaling, weights):
    rows, cols = scaling.shape[1:]
    places = chunk_places(rows, cols)
    n = len(places)
    gx, gy = lax.axis_size("gx"), lax.axis_size("gy")
    cells = float(rows * cols * gx * gy)
    maps = lax.axis_size("map")
    chain = [()]

    def done(*values):
        chain[0] = (values[0],)
        return values

    near = [(i, i ^ 1) for i in range(gx)]
    far = []
    for i in range(gx):
        for j in range(gy):
            other = ((i + 1) // 2 * 2 - (1 if i % 2 == 0 else 0)) if 0 < i < gx - 1 else i
            far.append((i * gy + j, other * gy + (j if other != i else j ^ 1)))
    outer = [(0, 1), (1, 0), (2, 3), (3, 2)]
    middle = []
    for g in range(gx):
        middle += [(gx + g, 2 * gx + g), (2 * gx + g, gx + g), (g, g ^ 1), (3 * gx + g, 3 * gx + (g ^ 1))]

    term, ku, sent, crossed, held, got = [None] * n, [None] * n, [None] * n, [None] * n, [None] * n, [None] * (n + LAG)
    raws, quots, mass = [None] * n, [None] * n, [None]

    def outward(k, value):
        if maps == 4 and k < n + LAG:
            got[k] = lax.ppermute(value, "map", outer)

    def receive(k):
        if maps == 4:
            (sent[k],) = done(add(term[k], got[k], chain[0]))
            crossed[k] = lax.ppermute(sent[k], ("map", "gx"), middle)

    def total(k):
        if maps == 4:
            later = term[min(k + LAG, n - 1)]
            held[k], passed = done(*add_and_pass(sent[k], crossed[k], later, chain[0]))
            outward(k + LAG, passed)
        else:
            held[k] = lax.psum(term[k], "map")

    def close(k):
        raws[k], quots[k], mass[0] = finish(held[k], got[k + LAG], ku[k], mass[0], chain[0])
        done(mass[0])

    def take(first, values):
        for k in range(len(values) // 2):
            term[first + k], ku[first + k] = values[2 * k : 2 * k + 2]
        done(values[0])

    *values, tall, wide, one, two = first_chunk(weights, scaling, densities)
    take(0, values)
    outward(0, term[0])
    one = lax.ppermute(one, "gx", near)
    two = lax.ppermute(two, ("gx", "gy"), far)
    take(1, inner_chunks(weights, scaling, densities, tall, wide, chain[0]))
    for k in range(1, LAG):
        outward(k, term[k])
    receive(0)
    packs = done(*side_pack(scaling, densities, one, two, chain[0]))
    if gy == 2:
        from_left = from_right = lax.ppermute(packs[0], "gy", [(0, 1), (1, 0)])
    else:
        from_left = lax.ppermute(packs[0], "gy", [(i, i + 1) for i in range(gy - 1)])
        from_right = lax.ppermute(packs[1], "gy", [(i + 1, i) for i in range(gy - 1)])
    receive(1)
    inner_count = rows // WIDE - 2
    take(inner_count, edge_chunks(weights, scaling, densities, tall, wide, one, two, chain[0]))
    total(0)
    receive(2)
    total(1)
    take(
        inner_count + 2,
        side_chunks(weights, scaling, densities, tall, one, two, from_left, from_right, chain[0]),
    )
    for k in range(3, n):
        receive(k)
        if k >= LAG:
            close_k = k - LAG
        total(k - 1)
        close(close_k)
    total(n - 1)
    for k in range(n - LAG, n):
        close(k)
    bary, new = assemble(sum_grid(mass[0]), places, raws, quots, rows, cols, cells)
    return bary, new


def solution(mesh):
    placed = (P("map", "gx", "gy"), P("map", "gx", "gy"), P("map"))
    return jax.shard_map(
        local,
        mesh=mesh,
        in_specs=placed,
        out_specs=(P("gx", "gy"), P("map", "gx", "gy")),
        check_vma=False,
    )
```

time: 197 us -> 78.5 us (0.40)
  waiting for transfers between devices: 87.6 us -> 23.6 us
  matrix products: 24.4 us -> 0 us
  local copies, waits for them, and re-layouts: 25.4 us -> 2.81 us
  starting transfers between devices: 16.7 us -> 36.6 us
  blocking collectives: 14.1 us -> 0 us
  Pallas kernels: 0 us -> 13.8 us
  between operations: 15 us -> 1.6 us
  other arithmetic: 13.2 us -> 0.01 us
    psum x1 -> x0, waiting for transfers between devices: 71.4 us -> none  [local(): logsum = lax.psum(partial_log, 'map')]
    dot_general x8 -> x0, matrix products: 24.4 us -> none  [the longest x4 12.8 us: smooth_axis(): jnp.einsum('ic,mbcj->mbij', small, piece, precision=lax.Precision.HIGHEST...]
    ppermute x8 -> x25, starting transfers between devices: 16.7 us -> 36.6 us  [the longest x11 31.9 us: outward(): got[k] = lax.ppermute(value, 'map', outer)]
    psum x1 -> x0, blocking collectives: 14.1 us -> none  [local(): mass = lax.psum(jnp.sum(raw), ('gx', 'gy'))]
    pallas_call x0 -> x30, Pallas kernels: none -> 13.8 us  [call(): return lambda *args: kernel(*args, *deps)]
    slice x12 -> x0, local copies, waits for them, and re-layouts: 11.6 us -> none  [the longest x8 10.3 us: smooth_axis(): lax.slice_in_dim(padded, index * block, index * block + length, axis=axis)]
    ppermute x8 -> x25, waiting for transfers between devices: 16.2 us -> 23.6 us  [the longest x11 14.8 us: outward(): got[k] = lax.ppermute(value, 'map', outer)]
    reduce_sum x3 -> x0, other arithmetic: 5.92 us -> none  [the longest x1 2.88 us: local(): jnp.sum(weights[:, None, None] * jnp.log(scaling * ku), axis=0)]
  transfers between devices with their start and end apart: 9 -> 25, of which waited for: 7 -> 12; matrix products, arithmetic and copies ran while one was open for 1% -> 0% of each run, Pallas kernels for 0% -> 11%
where the time goes in v2:
time: 78.5 us; the launch traced here: 78.3 us
  starting transfers between devices  36.6 us (47%)
  waiting for transfers between devices  23.6 us (30%)
  Pallas kernels  13.8 us (18%)
  local copies, waits for them, and re-layouts  2.81 us (4%)
  between operations  1.6 us (2%)
    ppermute x11, starting transfers between devices, outward(): got[k] = lax.ppermute(value, 'map', outer)  31.9 us
    ppermute x11, waiting for transfers between devices, outward(): got[k] = lax.ppermute(value, 'map', outer)  14.8 us
    pallas_call x30, Pallas kernels, call(): return lambda *args: kernel(*args, *deps)  13.8 us
    ppermute x3, waiting for transfers between devices, sum_grid(): lax.ppermute(mass, axis, [(i, i ^ step) for i in range(count)])  8.16 us
    unnamed x6, local copies, waits for them, and re-layouts  2.81 us
    ppermute x1, starting transfers between devices, local(): two = lax.ppermute(two, ('gx', 'gy'), far)  2.59 us
  transfers between devices with their start and end apart: 25, of which 12 were waited for; matrix products, arithmetic and copies ran while one was open for 0% of the time, Pallas kernels for 11%

profile of v2, /device:TPU:0, one launch (start us, length us, event | category | flops | bytes accessed | tf_op | source)
XLA Modules:
  0.0 78.3 jit_solution(12434169505870282731)
XLA Ops:
  1.3 1.4 %copy-done = f32[1,384,1024]{2,1,0:T(8,128)S(1)} copy-done((f32[1,384,1024]{2,1,0:T(8,128)S(1)}, f32[1,384,1024]{2,1,0:T(8,128)}, u32[]{:S(2)}) %copy-start) | copy-done | bytes 1572888
  2.7 1.4 %copy-done.2 = f32[1,384,1024]{2,1,0:T(8,128)S(1)} copy-done((f32[1,384,1024]{2,1,0:T(8,128)S(1)}, f32[1,384,1024]{2,1,0:T(8,128)}, u32[]{:S(2)}) %copy-start.2) | copy-done | bytes 1572888
  4.1 2.9 %first.1 = (f32[64,768]{1,0:T(8,128)S(1)}, f32[64,768]{1,0:T(8,128)S(1)}, bf16[2,192,256]{2,1,0:T(8,128)(2,1)S(1)}, bf16[2,512,256]{2,1,0:T(8,128)(2,1)S(1)}, f3...) custom-call(f32[1]{0:T(128)S(6)} %copy.5.refs_0_, f32[1,384,1024]{2,1,0:T(8,128)S(1)} %copy-done, f32[1,384,1024]{2,1,0:T(8,128)S(1)} %copy-done.2), custom_call_target="tpu_custom_call" | custom-call | tf_op jit(solution)/shard_map/first/pallas_call | solution.py:123
  7.0 0.5 collective-permute-start
  7.5 2.6 %collective-permute-start.1 = (f32[96,1024]{1,0:T(8,128)S(1)}, f32[96,1024]{1,0:T(8,128)S(1)}, u32[]{:S(2)}, u32[]{:S(2)}) collective-permute-start(f32[96,1024]{1,0:T(8,128)S(1)} %get-tuple-element.64), channel_id=1, source_target_pairs={{0,1},{1,0},{2,4},{3,5},{4,2},{5,3},{6,7},{7,6},{8,9},{9,8},{10,12... | collective-permute-start | bytes 1179656 | tf_op jit(solution)/shard_map/ppermute | solution.py:447
  10.1 1.6 %collective-permute-start.2 = (f32[64,768]{1,0:T(8,128)S(1)}, f32[64,768]{1,0:T(8,128)S(1)}, u32[]{:S(2)}, u32[]{:S(2)}) collective-permute-start(f32[64,768]{1,0:T(8,128)S(1)} %get-tuple-element.65.refs_5_.refs_0_), channel_id=1, source_target_pairs={{0,8},{8,0},{16,24},{24,16},{1,9},{9,1},{17,25},{25,17},{2,10},{10... | collective-permute-start | bytes 589832 | tf_op jit(solution)/shard_map/ppermute | solution.py:419
  11.7 2.6 %inner.1 = (f32[64,768]{1,0:T(8,128)S(1)}, f32[64,768]{1,0:T(8,128)S(1)}, f32[64,768]{1,0:T(8,128)S(1)}, f32[64,768]{1,0:T(8,128)S(1)}, f32[64,768]{1,0:T(8,128)S(1)}, /*index=5*/f32[64,768]{1,0:T(8,128)S(1)}) custom-call(f32[1]{0:T(128)S(6)} %copy.5.refs_0_, f32[1,384,1024]{2,1,0:T(8,128)S(1)} %copy-done, f32[1,384,1024]{2,1,0:T(8,128)S(1)} %copy-done.2, ...), custom_call_target="tpu_custom_call" | custom-call | tf_op jit(solution)/shard_map/inner/pallas_call | solution.py:123
  14.3 0.5 collective-permute-start.4
  14.8 2.3 %collective-permute-done.2.refs_1_ = f32[64,768]{1,0:T(8,128)S(1)} collective-permute-done((f32[64,768]{1,0:T(8,128)S(1)}, f32[64,768]{1,0:T(8,128)S(1)}, u32[]{:S(2)}, u32[]{:S(2)}) %collective-permute-start.2) | collective-permute-done | bytes 196640 | tf_op jit(solution)/shard_map/ppermute | solution.py:419
  17.1 0.1 collective-permute-start.7
  17.2 3.1 %collective-permute-start.6 = (f32[64,768]{1,0:T(8,128)S(1)}, f32[64,768]{1,0:T(8,128)S(1)}, u32[]{:S(2)}, u32[]{:S(2)}) collective-permute-start(f32[64,768]{1,0:T(8,128)S(1)} %get-tuple-element.69.refs_0_), channel_id=1, source_target_pairs={{0,8},{8,0},{16,24},{24,16},{1,9},{9,1},{17,25},{25,17},{2,10},{10... | collective-permute-start | bytes 589832 | tf_op jit(solution)/shard_map/ppermute | solution.py:419
  20.4 0.2 side_pack.1.refs_2_
  20.6 1.4 %collective-permute-done.4.refs_1_ = f32[64,768]{1,0:T(8,128)S(1)} collective-permute-done((f32[64,768]{1,0:T(8,128)S(1)}, f32[64,768]{1,0:T(8,128)S(1)}, u32[]{:S(2)}, u32[]{:S(2)}) %collective-permute-start.4) | collective-permute-done | bytes 196640 | tf_op jit(solution)/shard_map/ppermute | solution.py:419
  22.0 0.1 collective-permute-start.5
  22.1 0.7 collective-permute-start.3
  22.8 2.3 %edges.1 = (f32[64,768]{1,0:T(8,128)S(1)}, f32[64,768]{1,0:T(8,128)S(1)}, f32[64,768]{1,0:T(8,128)S(1)}, f32[64,768]{1,0:T(8,128)S(1)}) custom-call(f32[1]{0:T(128)S(6)} %copy.5.refs_0_, f32[1,384,1024]{2,1,0:T(8,128)S(1)} %copy-done.1, f32[1,384,1024]{2,1,0:T(8,128)S(1)} %copy-done.2, bf16[2,192,256]{2,1,0:T(8,128)(2,1)S(1)} %get-tuple-element.62.refs_3_, ...), custom_call_target="tpu_custom_call" | custom-call | tf_op jit(solution)/shard_map/edges/pallas_call | solution.py:123
  25.2 3.2 %collective-permute-start.9 = (f32[64,768]{1,0:T(8,128)S(1)}, f32[64,768]{1,0:T(8,128)S(1)}, u32[]{:S(2)}, u32[]{:S(2)}) collective-permute-start(f32[64,768]{1,0:T(8,128)S(1)} %get-tuple-element.75), channel_id=1, source_target_pairs={{0,8},{8,0},{16,24},{24,16},{1,9},{9,1},{17,25},{25,17},{2,10},{10... | collective-permute-start | bytes 589832 | tf_op jit(solution)/shard_map/ppermute | solution.py:419
  28.4 0.1 collective-permute-start.10
  28.5 1.7 %collective-permute-start.8 = (f32[64,768]{1,0:T(8,128)S(1)}, f32[64,768]{1,0:T(8,128)S(1)}, u32[]{:S(2)}, u32[]{:S(2)}) collective-permute-start(f32[64,768]{1,0:T(8,128)S(1)} %get-tuple-element.74), channel_id=1, source_target_pairs={{0,8},{8,0},{16,24},{24,16},{1,9},{9,1},{17,25},{25,17},{2,10},{10... | collective-permute-start | bytes 589832 | tf_op jit(solution)/shard_map/ppermute | solution.py:419
  30.3 0.5 collective-permute-done.3.refs_6_.refs_7_
  30.8 2.7 %sides.1 = (f32[64,768]{1,0:T(8,128)S(1)}, f32[64,768]{1,0:T(8,128)S(1)}, f32[64,768]{1,0:T(8,128)S(1)}, f32[64,768]{1,0:T(8,128)S(1)}) custom-call(f32[1]{0:T(128)S(6)} %copy.5.refs_0_, f32[1,384,1024]{2,1,0:T(8,128)S(1)} %copy-done.1, f32[1,384,1024]{2,1,0:T(8,128)S(1)} %copy-done.2, bf16[2,192,256]{2,1,0:T(8,128)(2,1)S(1)} %get-tuple-element.62.refs_3_, ...), custom_call_target="tpu_custom_call" | custom-call | tf_op jit(solution)/shard_map/sides/pallas_call | solution.py:123
  33.5 0.2 collective-permute-done.9.refs_1_
  33.8 0.1 collective-permute-start.13
  33.9 2.7 %collective-permute-start.12 = (f32[64,768]{1,0:T(8,128)S(1)}, f32[64,768]{1,0:T(8,128)S(1)}, u32[]{:S(2)}, u32[]{:S(2)}) collective-permute-start(f32[64,768]{1,0:T(8,128)S(1)} %get-tuple-element.81), channel_id=1, source_target_pairs={{0,8},{8,0},{16,24},{24,16},{1,9},{9,1},{17,25},{25,17},{2,10},{10... | collective-permute-start | bytes 589832 | tf_op jit(solution)/shard_map/ppermute | solution.py:419
  36.6 0.8 %collective-permute-done.8.refs_1_ = f32[64,768]{1,0:T(8,128)S(1)} collective-permute-done((f32[64,768]{1,0:T(8,128)S(1)}, f32[64,768]{1,0:T(8,128)S(1)}, u32[]{:S(2)}, u32[]{:S(2)}) %collective-permute-start.8) | collective-permute-done | bytes 196640 | tf_op jit(solution)/shard_map/ppermute | solution.py:419
  37.5 0.1 collective-permute-start.11
  37.6 6.4 %collective-permute-start.15 = (f32[64,768]{1,0:T(8,128)S(1)}, f32[64,768]{1,0:T(8,128)S(1)}, u32[]{:S(2)}, u32[]{:S(2)}) collective-permute-start(f32[64,768]{1,0:T(8,128)S(1)} %get-tuple-element.86), channel_id=1, source_target_pairs={{0,8},{8,0},{16,24},{24,16},{1,9},{9,1},{17,25},{25,17},{2,10},{10... | collective-permute-start | bytes 589832 | tf_op jit(solution)/shard_map/ppermute | solution.py:419
  44.1 0.1 collective-permute-start.16
  44.3 3.7 %collective-permute-start.14 = (f32[64,768]{1,0:T(8,128)S(1)}, f32[64,768]{1,0:T(8,128)S(1)}, u32[]{:S(2)}, u32[]{:S(2)}) collective-permute-start(f32[64,768]{1,0:T(8,128)S(1)} %get-tuple-element.85), channel_id=1, source_target_pairs={{0,8},{8,0},{16,24},{24,16},{1,9},{9,1},{17,25},{25,17},{2,10},{10... | collective-permute-start | bytes 589832 | tf_op jit(solution)/shard_map/ppermute | solution.py:419
  48.0 1.2 %collective-permute-done.15.refs_1_ = f32[64,768]{1,0:T(8,128)S(1)} collective-permute-done((f32[64,768]{1,0:T(8,128)S(1)}, f32[64,768]{1,0:T(8,128)S(1)}, u32[]{:S(2)}, u32[]{:S(2)}) %collective-permute-start.15) | collective-permute-done | bytes 196640 | tf_op jit(solution)/shard_map/ppermute | solution.py:419
  49.2 0.1 collective-permute-start.18
  49.4 0.1 finish.11
  49.5 2.4 %collective-permute-done.14.refs_1_ = f32[64,768]{1,0:T(8,128)S(1)} collective-permute-done((f32[64,768]{1,0:T(8,128)S(1)}, f32[64,768]{1,0:T(8,128)S(1)}, u32[]{:S(2)}, u32[]{:S(2)}) %collective-permute-start.14) | collective-permute-done | bytes 196640 | tf_op jit(solution)/shard_map/ppermute | solution.py:419
  51.9 0.1 collective-permute-start.17
  52.0 2.1 %collective-permute-start.21 = (f32[64,768]{1,0:T(8,128)S(1)}, f32[64,768]{1,0:T(8,128)S(1)}, u32[]{:S(2)}, u32[]{:S(2)}) collective-permute-start(f32[64,768]{1,0:T(8,128)S(1)} %get-tuple-element.101), channel_id=1, source_target_pairs={{0,8},{8,0},{16,24},{24,16},{1,9},{9,1},{17,25},{25,17},{2,10},{10... | collective-permute-start | bytes 589832 | tf_op jit(solution)/shard_map/ppermute | solution.py:419
  54.1 4.9 %collective-permute-start.20 = (f32[64,768]{1,0:T(8,128)S(1)}, f32[64,768]{1,0:T(8,128)S(1)}, u32[]{:S(2)}, u32[]{:S(2)}) collective-permute-start(f32[64,768]{1,0:T(8,128)S(1)} %get-tuple-element.99), channel_id=1, source_target_pairs={{0,8},{8,0},{16,24},{24,16},{1,9},{9,1},{17,25},{25,17},{2,10},{10... | collective-permute-start | bytes 589832 | tf_op jit(solution)/shard_map/ppermute | solution.py:419
  59.0 0.1 finish.12
  59.2 2.0 %collective-permute-start.19 = (f32[64,768]{1,0:T(8,128)S(1)}, f32[64,768]{1,0:T(8,128)S(1)}, u32[]{:S(2)}, u32[]{:S(2)}) collective-permute-start(f32[64,768]{1,0:T(8,128)S(1)} %get-tuple-element.97), channel_id=1, source_target_pairs={{0,8},{8,0},{16,24},{24,16},{1,9},{9,1},{17,25},{25,17},{2,10},{10... | collective-permute-start | bytes 589832 | tf_op jit(solution)/shard_map/ppermute | solution.py:419
  61.2 3.6 %collective-permute-done.20.refs_1_ = f32[64,768]{1,0:T(8,128)S(1)} collective-permute-done((f32[64,768]{1,0:T(8,128)S(1)}, f32[64,768]{1,0:T(8,128)S(1)}, u32[]{:S(2)}, u32[]{:S(2)}) %collective-permute-start.20) | collective-permute-done | bytes 196640 | tf_op jit(solution)/shard_map/ppermute | solution.py:419
  64.9 2.8 %collective-permute-done.19.refs_1_ = f32[64,768]{1,0:T(8,128)S(1)} collective-permute-done((f32[64,768]{1,0:T(8,128)S(1)}, f32[64,768]{1,0:T(8,128)S(1)}, u32[]{:S(2)}, u32[]{:S(2)}) %collective-permute-start.19) | collective-permute-done | bytes 196640 | tf_op jit(solution)/shard_map/ppermute | solution.py:419
  67.7 0.1 finish.15
  67.8 0.1 collective-permute-start.22
  67.9 1.2 %collective-permute-done.22 = f32[8,128]{1,0:T(8,128)S(1)} collective-permute-done((f32[8,128]{1,0:T(8,128)S(1)}, f32[8,128]{1,0:T(8,128)S(1)}, u32[]{:S(2)}, u32[]{:S(2)}) %collective-permute-start.22) | collective-permute-done | bytes 4128 | tf_op jit(solution)/shard_map/ppermute | solution.py:355
  69.1 0.1 collective-permute-start.23
  69.2 3.5 %collective-permute-done.23 = f32[8,128]{1,0:T(8,128)S(1)} collective-permute-done((f32[8,128]{1,0:T(8,128)S(1)}, f32[8,128]{1,0:T(8,128)S(1)}, u32[]{:S(2)}, u32[]{:S(2)}) %collective-permute-start.23) | collective-permute-done | bytes 4128 | tf_op jit(solution)/shard_map/ppermute | solution.py:355
  72.7 0.1 collective-permute-start.24
  72.8 3.5 %collective-permute-done.24 = f32[8,128]{1,0:T(8,128)S(1)} collective-permute-done((f32[8,128]{1,0:T(8,128)S(1)}, f32[8,128]{1,0:T(8,128)S(1)}, u32[]{:S(2)}, u32[]{:S(2)}) %collective-permute-start.24) | collective-permute-done | bytes 4128 | tf_op jit(solution)/shard_map/ppermute | solution.py:355
  76.3 2.1 %assemble.1 = (f32[384,1024]{1,0:T(8,128)}, f32[1,384,1024]{2,1,0:T(8,128)}) custom-call(f32[8,128]{1,0:T(8,128)S(1)} %add.19.refs_0_, f32[64,768]{1,0:T(8,128)S(1)} %get-tuple-element.106.refs_1_, f32[64,768]{1,0:T(8,128)S(1)} %get-tuple-element.107.refs_2_, f32[64,768]{1,0:T(8,128)S(1)} %get-tuple-element.108.refs_3_, ...), custom_call_target="tpu_custom_call" | custom-call | tf_op jit(solution)/shard_map/assemble/pallas_call | solution.py:123
  (41 shorter events, 0.9 us)
Async XLA Ops:
  1.3 1.4 %copy-start = (f32[1,384,1024]{2,1,0:T(8,128)S(1)}, f32[1,384,1024]{2,1,0:T(8,128)}, u32[]{:S(2)}) copy-start(f32[1,384,1024]{2,1,0:T(8,128)} %refs_1_.9) | copy-start | bytes 4718596
  2.7 1.4 %copy-start.2 = (f32[1,384,1024]{2,1,0:T(8,128)S(1)}, f32[1,384,1024]{2,1,0:T(8,128)}, u32[]{:S(2)}) copy-start(f32[1,384,1024]{2,1,0:T(8,128)} %refs_2_.7) | copy-start | bytes 4718596
  7.0 13.4 %collective-permute-start = (f32[96,1024]{1,0:T(8,128)S(1)}, f32[96,1024]{1,0:T(8,128)S(1)}, u32[]{:S(2)}, u32[]{:S(2)}) collective-permute-start(f32[96,1024]{1,0:T(8,128)S(1)} %get-tuple-element.63), channel_id=1, source_target_pairs={{0,2},{2,0},{4,6},{6,4},{1,3},{3,1},{5,7},{7,5},{8,10},{10,8},{12,... | collective-permute-start | bytes 1179656 | tf_op jit(solution)/shard_map/ppermute | solution.py:446
  7.5 12.9 %collective-permute-start.1 = (f32[96,1024]{1,0:T(8,128)S(1)}, f32[96,1024]{1,0:T(8,128)S(1)}, u32[]{:S(2)}, u32[]{:S(2)}) collective-permute-start(f32[96,1024]{1,0:T(8,128)S(1)} %get-tuple-element.64), channel_id=1, source_target_pairs={{0,1},{1,0},{2,4},{3,5},{4,2},{5,3},{6,7},{7,6},{8,9},{9,8},{10,12... | collective-permute-start | bytes 1179656 | tf_op jit(solution)/shard_map/ppermute | solution.py:447
  10.1 7.0 %collective-permute-start.2 = (f32[64,768]{1,0:T(8,128)S(1)}, f32[64,768]{1,0:T(8,128)S(1)}, u32[]{:S(2)}, u32[]{:S(2)}) collective-permute-start(f32[64,768]{1,0:T(8,128)S(1)} %get-tuple-element.65.refs_5_.refs_0_), channel_id=1, source_target_pairs={{0,8},{8,0},{16,24},{24,16},{1,9},{9,1},{17,25},{25,17},{2,10},{10... | collective-permute-start | bytes 589832 | tf_op jit(solution)/shard_map/ppermute | solution.py:419
  11.7 8.7 %copy-start.1 = (f32[1,384,1024]{2,1,0:T(8,128)S(1)}, f32[1,384,1024]{2,1,0:T(8,128)}, u32[]{:S(2)}) copy-start(f32[1,384,1024]{2,1,0:T(8,128)} %refs_1_.9) | copy-start | bytes 4718596
  14.3 7.7 %collective-permute-start.4 = (f32[64,768]{1,0:T(8,128)S(1)}, f32[64,768]{1,0:T(8,128)S(1)}, u32[]{:S(2)}, u32[]{:S(2)}) collective-permute-start(f32[64,768]{1,0:T(8,128)S(1)} %get-tuple-element.67.refs_2_.refs_0_), channel_id=1, source_target_pairs={{0,8},{8,0},{16,24},{24,16},{1,9},{9,1},{17,25},{25,17},{2,10},{10... | collective-permute-start | bytes 589832 | tf_op jit(solution)/shard_map/ppermute | solution.py:419
  17.1 8.0 %collective-permute-start.7 = (f32[64,768]{1,0:T(8,128)S(1)}, f32[64,768]{1,0:T(8,128)S(1)}, u32[]{:S(2)}, u32[]{:S(2)}) collective-permute-start(f32[64,768]{1,0:T(8,128)S(1)} %add.20.refs_4_.refs_0_), channel_id=1, source_target_pairs={{8,16},{16,8},{0,2},{24,26},{10,18},{18,10},{2,0},{26,24},{12,20},... | collective-permute-start | bytes 589832 | tf_op jit(solution)/shard_map/ppermute | solution.py:424
  17.2 11.2 %collective-permute-start.6 = (f32[64,768]{1,0:T(8,128)S(1)}, f32[64,768]{1,0:T(8,128)S(1)}, u32[]{:S(2)}, u32[]{:S(2)}) collective-permute-start(f32[64,768]{1,0:T(8,128)S(1)} %get-tuple-element.69.refs_0_), channel_id=1, source_target_pairs={{0,8},{8,0},{16,24},{24,16},{1,9},{9,1},{17,25},{25,17},{2,10},{10... | collective-permute-start | bytes 589832 | tf_op jit(solution)/shard_map/ppermute | solution.py:419
  22.0 6.5 %collective-permute-start.5 = (f32[64,768]{1,0:T(8,128)S(1)}, f32[64,768]{1,0:T(8,128)S(1)}, u32[]{:S(2)}, u32[]{:S(2)}) collective-permute-start(f32[64,768]{1,0:T(8,128)S(1)} %add.21.refs_7_.refs_0_), channel_id=1, source_target_pairs={{8,16},{16,8},{0,2},{24,26},{10,18},{18,10},{2,0},{26,24},{12,20},... | collective-permute-start | bytes 589832 | tf_op jit(solution)/shard_map/ppermute | solution.py:424
  22.1 8.7 %collective-permute-start.3 = (f32[512,128]{1,0:T(8,128)S(1)}, f32[512,128]{1,0:T(8,128)S(1)}, u32[]{:S(2)}, u32[]{:S(2)}) collective-permute-start(f32[512,128]{1,0:T(8,128)S(1)} %side_pack.1.refs_2_), channel_id=1, source_target_pairs={{0,1},{1,0},{2,3},{3,2},{4,5},{5,4},{6,7},{7,6},{8,9},{9,8},{10,11... | collective-permute-start | bytes 786440 | tf_op jit(solution)/shard_map/ppermute | solution.py:454
  25.2 8.6 %collective-permute-start.9 = (f32[64,768]{1,0:T(8,128)S(1)}, f32[64,768]{1,0:T(8,128)S(1)}, u32[]{:S(2)}, u32[]{:S(2)}) collective-permute-start(f32[64,768]{1,0:T(8,128)S(1)} %get-tuple-element.75), channel_id=1, source_target_pairs={{0,8},{8,0},{16,24},{24,16},{1,9},{9,1},{17,25},{25,17},{2,10},{10... | collective-permute-start | bytes 589832 | tf_op jit(solution)/shard_map/ppermute | solution.py:419
  28.4 5.4 %collective-permute-start.10 = (f32[64,768]{1,0:T(8,128)S(1)}, f32[64,768]{1,0:T(8,128)S(1)}, u32[]{:S(2)}, u32[]{:S(2)}) collective-permute-start(f32[64,768]{1,0:T(8,128)S(1)} %add.22.refs_3_.refs_0_), channel_id=1, source_target_pairs={{8,16},{16,8},{0,2},{24,26},{10,18},{18,10},{2,0},{26,24},{12,20},... | collective-permute-start | bytes 589832 | tf_op jit(solution)/shard_map/ppermute | solution.py:424
  28.5 8.9 %collective-permute-start.8 = (f32[64,768]{1,0:T(8,128)S(1)}, f32[64,768]{1,0:T(8,128)S(1)}, u32[]{:S(2)}, u32[]{:S(2)}) collective-permute-start(f32[64,768]{1,0:T(8,128)S(1)} %get-tuple-element.74), channel_id=1, source_target_pairs={{0,8},{8,0},{16,24},{24,16},{1,9},{9,1},{17,25},{25,17},{2,10},{10... | collective-permute-start | bytes 589832 | tf_op jit(solution)/shard_map/ppermute | solution.py:419
  33.8 3.8 %collective-permute-start.13 = (f32[64,768]{1,0:T(8,128)S(1)}, f32[64,768]{1,0:T(8,128)S(1)}, u32[]{:S(2)}, u32[]{:S(2)}) collective-permute-start(f32[64,768]{1,0:T(8,128)S(1)} %add.23.refs_3_.refs_0_), channel_id=1, source_target_pairs={{8,16},{16,8},{0,2},{24,26},{10,18},{18,10},{2,0},{26,24},{12,20},... | collective-permute-start | bytes 589832 | tf_op jit(solution)/shard_map/ppermute | solution.py:424
  33.9 10.2 %collective-permute-start.12 = (f32[64,768]{1,0:T(8,128)S(1)}, f32[64,768]{1,0:T(8,128)S(1)}, u32[]{:S(2)}, u32[]{:S(2)}) collective-permute-start(f32[64,768]{1,0:T(8,128)S(1)} %get-tuple-element.81), channel_id=1, source_target_pairs={{0,8},{8,0},{16,24},{24,16},{1,9},{9,1},{17,25},{25,17},{2,10},{10... | collective-permute-start | bytes 589832 | tf_op jit(solution)/shard_map/ppermute | solution.py:419
  37.5 6.7 %collective-permute-start.11 = (f32[64,768]{1,0:T(8,128)S(1)}, f32[64,768]{1,0:T(8,128)S(1)}, u32[]{:S(2)}, u32[]{:S(2)}) collective-permute-start(f32[64,768]{1,0:T(8,128)S(1)} %add.24.refs_3_.refs_0_), channel_id=1, source_target_pairs={{8,16},{16,8},{0,2},{24,26},{10,18},{18,10},{2,0},{26,24},{12,20},... | collective-permute-start | bytes 589832 | tf_op jit(solution)/shard_map/ppermute | solution.py:424
  37.6 11.6 %collective-permute-start.15 = (f32[64,768]{1,0:T(8,128)S(1)}, f32[64,768]{1,0:T(8,128)S(1)}, u32[]{:S(2)}, u32[]{:S(2)}) collective-permute-start(f32[64,768]{1,0:T(8,128)S(1)} %get-tuple-element.86), channel_id=1, source_target_pairs={{0,8},{8,0},{16,24},{24,16},{1,9},{9,1},{17,25},{25,17},{2,10},{10... | collective-permute-start | bytes 589832 | tf_op jit(solution)/shard_map/ppermute | solution.py:419
  44.1 5.2 %collective-permute-start.16 = (f32[64,768]{1,0:T(8,128)S(1)}, f32[64,768]{1,0:T(8,128)S(1)}, u32[]{:S(2)}, u32[]{:S(2)}) collective-permute-start(f32[64,768]{1,0:T(8,128)S(1)} %add.25.refs_3_.refs_0_), channel_id=1, source_target_pairs={{8,16},{16,8},{0,2},{24,26},{10,18},{18,10},{2,0},{26,24},{12,20},... | collective-permute-start | bytes 589832 | tf_op jit(solution)/shard_map/ppermute | solution.py:424
  44.3 7.6 %collective-permute-start.14 = (f32[64,768]{1,0:T(8,128)S(1)}, f32[64,768]{1,0:T(8,128)S(1)}, u32[]{:S(2)}, u32[]{:S(2)}) collective-permute-start(f32[64,768]{1,0:T(8,128)S(1)} %get-tuple-element.85), channel_id=1, source_target_pairs={{0,8},{8,0},{16,24},{24,16},{1,9},{9,1},{17,25},{25,17},{2,10},{10... | collective-permute-start | bytes 589832 | tf_op jit(solution)/shard_map/ppermute | solution.py:419
  49.2 4.9 %collective-permute-start.18 = (f32[64,768]{1,0:T(8,128)S(1)}, f32[64,768]{1,0:T(8,128)S(1)}, u32[]{:S(2)}, u32[]{:S(2)}) collective-permute-start(f32[64,768]{1,0:T(8,128)S(1)} %add.26.refs_3_.refs_0_), channel_id=1, source_target_pairs={{8,16},{16,8},{0,2},{24,26},{10,18},{18,10},{2,0},{26,24},{12,20},... | collective-permute-start | bytes 589832 | tf_op jit(solution)/shard_map/ppermute | solution.py:424
  51.9 7.2 %collective-permute-start.17 = (f32[64,768]{1,0:T(8,128)S(1)}, f32[64,768]{1,0:T(8,128)S(1)}, u32[]{:S(2)}, u32[]{:S(2)}) collective-permute-start(f32[64,768]{1,0:T(8,128)S(1)} %add.27.refs_3_.refs_0_), channel_id=1, source_target_pairs={{8,16},{16,8},{0,2},{24,26},{10,18},{18,10},{2,0},{26,24},{12,20},... | collective-permute-start | bytes 589832 | tf_op jit(solution)/shard_map/ppermute | solution.py:424
  52.0 9.2 %collective-permute-start.21 = (f32[64,768]{1,0:T(8,128)S(1)}, f32[64,768]{1,0:T(8,128)S(1)}, u32[]{:S(2)}, u32[]{:S(2)}) collective-permute-start(f32[64,768]{1,0:T(8,128)S(1)} %get-tuple-element.101), channel_id=1, source_target_pairs={{0,8},{8,0},{16,24},{24,16},{1,9},{9,1},{17,25},{25,17},{2,10},{10... | collective-permute-start | bytes 589832 | tf_op jit(solution)/shard_map/ppermute | solution.py:419
  54.1 10.7 %collective-permute-start.20 = (f32[64,768]{1,0:T(8,128)S(1)}, f32[64,768]{1,0:T(8,128)S(1)}, u32[]{:S(2)}, u32[]{:S(2)}) collective-permute-start(f32[64,768]{1,0:T(8,128)S(1)} %get-tuple-element.99), channel_id=1, source_target_pairs={{0,8},{8,0},{16,24},{24,16},{1,9},{9,1},{17,25},{25,17},{2,10},{10... | collective-permute-start | bytes 589832 | tf_op jit(solution)/shard_map/ppermute | solution.py:419
  59.2 8.6 %collective-permute-start.19 = (f32[64,768]{1,0:T(8,128)S(1)}, f32[64,768]{1,0:T(8,128)S(1)}, u32[]{:S(2)}, u32[]{:S(2)}) collective-permute-start(f32[64,768]{1,0:T(8,128)S(1)} %get-tuple-element.97), channel_id=1, source_target_pairs={{0,8},{8,0},{16,24},{24,16},{1,9},{9,1},{17,25},{25,17},{2,10},{10... | collective-permute-start | bytes 589832 | tf_op jit(solution)/shard_map/ppermute | solution.py:419
  67.8 1.2 %collective-permute-start.22 = (f32[8,128]{1,0:T(8,128)S(1)}, f32[8,128]{1,0:T(8,128)S(1)}, u32[]{:S(2)}, u32[]{:S(2)}) collective-permute-start(f32[8,128]{1,0:T(8,128)S(1)} %get-tuple-element.105), channel_id=1, source_target_pairs={{0,2},{2,0},{4,6},{6,4},{1,3},{3,1},{5,7},{7,5},{8,10},{10,8},{12,... | collective-permute-start | bytes 12296 | tf_op jit(solution)/shard_map/ppermute | solution.py:355
  69.1 3.6 %collective-permute-start.23 = (f32[8,128]{1,0:T(8,128)S(1)}, f32[8,128]{1,0:T(8,128)S(1)}, u32[]{:S(2)}, u32[]{:S(2)}) collective-permute-start(f32[8,128]{1,0:T(8,128)S(1)} %add.17), channel_id=1, source_target_pairs={{0,4},{2,6},{4,0},{6,2},{1,5},{3,7},{5,1},{7,3},{8,12},{10,14},{12... | collective-permute-start | bytes 12296 | tf_op jit(solution)/shard_map/ppermute | solution.py:355
  72.7 3.6 %collective-permute-start.24 = (f32[8,128]{1,0:T(8,128)S(1)}, f32[8,128]{1,0:T(8,128)S(1)}, u32[]{:S(2)}, u32[]{:S(2)}) collective-permute-start(f32[8,128]{1,0:T(8,128)S(1)} %add.18), channel_id=1, source_target_pairs={{0,1},{1,0},{2,3},{3,2},{4,5},{5,4},{6,7},{7,6},{8,9},{9,8},{10,11... | collective-permute-start | bytes 12296 | tf_op jit(solution)/shard_map/ppermute | solution.py:355

commit v3 on v2

--- a/solution.py
+++ b/solution.py
@@ -11,7 +11,7 @@
 WIDE = 2 * HALF
 LANES = 128
 BLOCK = 192
-LAG = 3
+LAG = 4
 F32 = jnp.float32
 BF16 = jnp.bfloat16
 
@@ -41,7 +41,7 @@
 
 def times(left, right):
     (lh, ll), (rh, rl) = left, right
-    return mm(lh, rh) + mm(ll, rh) + mm(lh, rl)
+    return mm(jnp.concatenate([lh, lh, ll], axis=1), jnp.concatenate([rh, rl, rh], axis=0))
 
 
 def part(pair, rows=slice(None), cols=slice(None)):
@@ -58,28 +58,18 @@
     return out[0] if len(out) == 1 else jnp.concatenate(out, axis=0)
 
 
-def cols_all(wide, x):
+def cols_of(wide, x, padded):
+    margin = 0 if padded else LANES
     width = x.shape[1]
     x = split(x)
     out = []
-    for start in range(0, width, 256):
+    for start in range(margin, width - margin, 256):
         lo, hi = max(start - LANES, 0), min(start + 256 + LANES, width)
         rows = slice(lo - (start - LANES), hi - (start - LANES))
         out.append(times(part(x, cols=slice(lo, hi)), part(wide, rows)))
     return jnp.concatenate(out, axis=1)
 
 
-def cols_inner(wide, x):
-    width = x.shape[1]
-    x = split(x)
-    out = []
-    for start in range(0, width - 2 * LANES, 256):
-        stop = min(start + 512, width)
-        band_part = part(wide, slice(stop - start), slice(stop - start - 2 * LANES))
-        out.append(times(part(x, cols=slice(start, stop)), band_part))
-    return jnp.concatenate(out, axis=1)
-
-
 def quotient(dens, kv):
     return jnp.where(dens > 0.0, dens / kv, 0.0)
 
@@ -104,7 +94,10 @@
     return pl.BlockSpec(memory_space=pltpu.HBM)
 
 
-def call(body, out, in_specs, name, deps=(), scratch=()):
+COST = {'finish_last': 2.0, 'add': 4.0, 'inner': 2.5, 'edges': 2.3, 'sides': 2.5}
+
+
+def call(body, out, in_specs, name, deps=(), scratch=(), out_specs=None):
     n = len(in_specs)
 
     def run(*refs):
@@ -114,52 +107,58 @@
         run,
         out_shape=[jax.ShapeDtypeStruct(s, F32) if isinstance(s, tuple) else s for s in out],
         in_specs=list(in_specs) + [pl.BlockSpec(memory_space=pl.ANY)] * len(deps),
-        out_specs=[vmem()] * len(out),
+        out_specs=out_specs or [vmem()] * len(out),
         scratch_shapes=list(scratch),
         compiler_params=pltpu.CompilerParams(vmem_limit_bytes=40 * 1024 * 1024),
-        cost_estimate=pl.CostEstimate(flops=0, bytes_accessed=0, transcendentals=0),
+        cost_estimate=pl.CostEstimate(flops=int(COST.get(name, 0) * 1e9), bytes_accessed=0, transcendentals=0),
         name=name,
     )
     return lambda *args: kernel(*args, *deps)
 
 
+def fill_pack(s, d, pack, last):
+    rows = s.shape[1]
+    for start, x, n in ((0, s, WIDE), (WIDE, d, HALF)):
+        pack[start : start + n] = jnp.where(last, x[0, rows - n :], x[0, :n])
+
+
 def first_chunk(weights, scaling, densities):
     rows, cols = scaling.shape[1:]
     tall_n, dens_n = 3 * WIDE, 2 * WIDE
 
-    def body(w, s_hbm, d_hbm, term, ku, tall_ref, wide_ref, one, two, s, d, sems):
-        odd = lax.rem(lax.axis_index("gx"), 2)
-        ends = ((one, (1 - odd) * (rows - WIDE), (1 - odd) * (rows - HALF)), (two, odd * (rows - WIDE), odd * (rows - HALF)))
-        copies = [
-            pltpu.make_async_copy(s_hbm.at[0, pl.ds(0, tall_n)], s, sems.at[0]),
-            pltpu.make_async_copy(d_hbm.at[0, pl.ds(HALF, dens_n)], d, sems.at[1]),
-        ]
-        for k, (ref, s_row, d_row) in enumerate(ends):
-            s_row, d_row = pl.multiple_of(s_row, HALF), pl.multiple_of(d_row, HALF)
-            copies.append(pltpu.make_async_copy(s_hbm.at[0, pl.ds(s_row, WIDE)], ref.at[pl.ds(0, WIDE)], sems.at[2 + 2 * k]))
-            copies.append(pltpu.make_async_copy(d_hbm.at[0, pl.ds(d_row, HALF)], ref.at[pl.ds(WIDE, HALF)], sems.at[3 + 2 * k]))
-        for copy in copies:
+    def body(w, s_hbm, d_hbm, term, ku, tall_ref, wide_ref, s, d, near, sems):
+        copies = []
+        for start, stop in ((0, tall_n), (tall_n, rows)):
+            for source, ref in ((s_hbm, s), (d_hbm, d)):
+                piece = (0, pl.ds(start, stop - start))
+                copies.append(pltpu.make_async_copy(source.at[piece], ref.at[piece], sems.at[len(copies)]))
+        for copy in copies[:2]:
             copy.start()
         tall = band(BLOCK, BLOCK + WIDE, -HALF)
         wide = band(512, 256, LANES)
         tall_ref[0], tall_ref[1] = tall
         wide_ref[0], wide_ref[1] = wide
         copies[0].wait()
-        kv = cols_all(wide, rows_of(tall, s[...]))
+        for copy in copies[2:]:
+            copy.start()
+        kv = cols_of(wide, rows_of(tall, s[0, :tall_n]), True)
         copies[1].wait()
-        u = quotient(d[...], kv)
-        k = cols_inner(wide, rows_of(tall, u))
+        u = quotient(d[0, HALF : HALF + dens_n], kv)
+        k = cols_of(wide, rows_of(tall, u), False)
         ku[...] = k
-        term[...] = log_term(w[0], s[WIDE : 2 * WIDE, LANES:-LANES], k)
+        term[...] = log_term(w[0], s[0, WIDE : 2 * WIDE, LANES:-LANES], k)
         for copy in copies[2:]:
             copy.wait()
+        fill_pack(s, d, near, lax.rem(lax.axis_index("gx"), 2) == 0)
 
     inner = (WIDE, cols - 2 * LANES)
-    pack = (WIDE + HALF, cols)
     bands = [jax.ShapeDtypeStruct((2, BLOCK, BLOCK + WIDE), BF16), jax.ShapeDtypeStruct((2, 512, 256), BF16)]
-    scratch = [pltpu.VMEM((tall_n, cols), F32), pltpu.VMEM((dens_n, cols), F32), pltpu.SemaphoreType.DMA((6,))]
-    return call(body, [inner, inner, *bands, pack, pack], [smem(), hbm(), hbm()], "first", (), scratch)(
-        weights, scaling, densities
+    whole, pack = (1, rows, cols), (WIDE + HALF, cols)
+    out = [inner, inner, *bands, whole, whole, pack]
+    return call(body, out, [smem(), hbm(), hbm()], "first", (), [pltpu.SemaphoreType.DMA((4,))])(
+        weights,
+        pltpu.with_memory_space_constraint(scaling, pltpu.HBM),
+        pltpu.with_memory_space_constraint(densities, pltpu.HBM),
     )
 
 
@@ -169,15 +168,16 @@
 
     def body(w, s, d, tall_ref, wide_ref, *outs):
         tall, wide = pair_of(tall_ref), pair_of(wide_ref)
-        kv = cols_all(wide, rows_of(tall, s[0, WIDE:]))
+        kv = cols_of(wide, rows_of(tall, s[0, WIDE:]), True)
         u = quotient(d[0, WIDE + HALF : rows - HALF], kv)
-        k = cols_inner(wide, rows_of(tall, u))
+        k = cols_of(wide, rows_of(tall, u), False)
         term = log_term(w[0], s[0, 2 * WIDE : rows - WIDE, LANES:-LANES], k)
         for p in range(count):
             outs[2 * p][...] = term[p * WIDE : (p + 1) * WIDE]
             outs[2 * p + 1][...] = k[p * WIDE : (p + 1) * WIDE]
-
-    out = [(WIDE, cols - 2 * LANES)] * (2 * count)
+        fill_pack(s, d, outs[2 * count], lax.rem(lax.axis_index("gx"), 2) == 1)
+
+    out = [(WIDE, cols - 2 * LANES)] * (2 * count) + [(WIDE + HALF, cols)]
     return call(body, out, [smem()] + [vmem()] * 4, "inner", deps)(weights, scaling, densities, tall, wide)
 
 
@@ -200,9 +200,9 @@
             jnp.concatenate([s[0, rows - 2 * WIDE :], down[:WIDE]], axis=0),
         )
         dens = jnp.concatenate([up[WIDE:], d[0, : 3 * HALF], d[0, rows - 3 * HALF :], down[WIDE:]], axis=0)
-        kv = cols_all(wide, jnp.concatenate([rows_of(tall, x) for x in scal], axis=0))
+        kv = cols_of(wide, jnp.concatenate([rows_of(tall, x) for x in scal], axis=0), True)
         u = quotient(dens, kv)
-        k = cols_inner(wide, jnp.concatenate([rows_of(tall, x) for x in (u[: 2 * WIDE], u[2 * WIDE :])], axis=0))
+        k = cols_of(wide, jnp.concatenate([rows_of(tall, x) for x in (u[: 2 * WIDE], u[2 * WIDE :])], axis=0), False)
         for p, start in enumerate((0, rows - WIDE)):
             kp = k[p * WIDE : (p + 1) * WIDE]
             outs[2 * p][...] = log_term(w[0], s[0, start : start + WIDE, LANES:-LANES], kp)
@@ -266,11 +266,10 @@
             dens = jnp.concatenate([up[WIDE:], d[0, :, which], down[WIDE:]], axis=0)
             return pltpu.roll(scal, WIDE, 1), dens
 
-        def side(scal, dens):
-            kv = times(split(rows_of(tall, scal)), short)
-            u = quotient(dens, kv)
-            r = split(rows_of(tall, u))
-            return times(r, part(short, slice(BLOCK), slice(LANES)))
+        def cols_of_both(sides, band):
+            y = times(split(jnp.concatenate(sides, axis=0)), band)
+            n = sides[0].shape[0]
+            return y[:n], y[n:]
 
         small = lane[inner]
         (s0, d0), (s1, d1) = block(slice(0, LANES)), block(slice(LANES, 2 * LANES))
@@ -279,7 +278,7 @@
         dens = jnp.concatenate(
             [jnp.where(small < HALF, left[inner], d0), jnp.where(small < HALF, d0, d1)[:, :WIDE]], axis=1
         )
-        k0 = side(scal, dens)
+        first = scal, dens
         (s0, d0), (s1, d1) = block(slice(cols - 2 * LANES, cols - LANES)), block(slice(cols - LANES, cols))
         scal = jnp.concatenate([jnp.where(lane < WIDE, s0, s1), jnp.where(lane < WIDE, s1, pltpu.roll(right, WIDE, 1))], axis=1)
         d0, d1 = pltpu.roll(d0, HALF, 1), pltpu.roll(d1, HALF, 1)
@@ -287,7 +286,10 @@
         dens = jnp.concatenate(
             [jnp.where(small < HALF, d0, d1), jnp.where(small < HALF, d1, halo)[:, :WIDE]], axis=1
         )
-        k1 = side(scal, dens)
+        both = first, (scal, dens)
+        kv = cols_of_both([rows_of(tall, scal) for scal, _ in both], short)
+        u = [quotient(dens, x) for (_, dens), x in zip(both, kv)]
+        k0, k1 = cols_of_both([rows_of(tall, x) for x in u], part(short, slice(BLOCK), slice(LANES)))
         for p in range(count):
             for b in range(blocks):
                 r = slice((p * blocks + b) * WIDE, (p * blocks + b + 1) * WIDE)
@@ -303,11 +305,11 @@
     )
 
 
-def add(a, b, deps):
+def add(a, b, deps, name="add"):
     def body(a_ref, b_ref, out_ref):
         out_ref[...] = a_ref[...] + b_ref[...]
 
-    return call(body, [a.shape], [vmem()] * 2, "add", deps)(a, b)[0]
+    return call(body, [a.shape], [vmem()] * 2, name, deps)(a, b)[0]
 
 
 def in_middle():
@@ -315,37 +317,55 @@
     return (z == 1) | (z == 2)
 
 
-def add_and_pass(a, b, term, deps):
-    def body(a_ref, b_ref, term_ref, out_ref, send_ref):
-        total = a_ref[...] + b_ref[...]
+def mass_of(raw, mass_ref):
+    rows, cols = raw.shape
+    total = jnp.sum(raw.reshape(rows // 8, 8, cols), axis=0)
+    total = sum(total[:, k : k + LANES] for k in range(0, cols, LANES))
+    return total if mass_ref is None else total + mass_ref[...]
+
+
+def add_and_pass(a, b, term, mass, deps):
+    inputs = [a, b, term] + ([] if mass is None else [mass])
+    n = len(inputs)
+
+    def body(*refs):
+        out_ref, send_ref, mass_ref = refs[n:]
+        total = refs[0][...] + refs[1][...]
         out_ref[...] = total
-        send_ref[...] = jnp.where(in_middle(), total, term_ref[...])
-
-    return call(body, [a.shape, a.shape], [vmem()] * 3, "add_and_pass", deps)(a, b, term)
-
-
-def finish(held, landed, ku, mass, deps):
-    inputs = [held] + ([] if landed is None else [landed]) + [ku] + ([] if mass is None else [mass])
+        send_ref[...] = jnp.where(in_middle(), total, refs[2][...])
+        mass_ref[...] = mass_of(jnp.exp(total), None if mass is None else refs[3])
+
+    return call(body, [a.shape, a.shape, (8, LANES)], [vmem()] * n, "add_and_pass", deps)(*inputs)
+
+
+def weigh(logs, mass, deps):
+    inputs = [logs] + ([] if mass is None else [mass])
     n = len(inputs)
 
     def body(*refs):
-        raw_ref, quot_ref, mass_ref = refs[n:]
+        refs[n][...] = mass_of(jnp.exp(refs[0][...]), None if mass is None else refs[1])
+
+    return call(body, [(8, LANES)], [vmem()] * n, "weigh", deps)(*inputs)
+
+
+def finish(held, landed, ku, deps, name="finish"):
+    inputs = [held] + ([] if landed is None else [landed]) + [ku]
+    n = len(inputs)
+
+    def body(*refs):
+        raw_ref, quot_ref = refs[n:]
         logs = refs[0][...]
         if landed is not None:
             logs = jnp.where(in_middle(), logs, refs[1][...])
         raw = jnp.exp(logs)
         raw_ref[...] = raw
-        quot_ref[...] = raw / refs[1 if landed is None else 2][...]
-        rows, cols = raw.shape
-        total = jnp.sum(raw.reshape(rows // 8, 8, cols), axis=0)
-        total = sum(total[:, k : k + LANES] for k in range(0, cols, LANES))
-        mass_ref[...] = total if mass is None else total + refs[n - 1][...]
-
-    return call(body, [held.shape, held.shape, (8, LANES)], [vmem()] * n, "finish", deps)(*inputs)
-
-
-def sum_grid(mass):
-    for axis in ("gx", "gy"):
+        quot_ref[...] = raw / refs[n - 1][...]
+
+    return call(body, [held.shape, held.shape], [vmem()] * n, name, deps)(*inputs)
+
+
+def sum_grid(mass, axes):
+    for axis in axes:
         count = lax.axis_size(axis)
         if count & (count - 1):
             mass = lax.psum(mass, axis)
@@ -357,20 +377,40 @@
     return mass
 
 
-def assemble(mass, places, raws, quots, rows, cols, cells):
-    n = len(places)
+def assemble(masses, places, raws, quots, rows, cols, cells):
+    n, m = len(places), len(masses)
 
     def body(*refs):
-        mass_ref, raw, quot = refs[0], refs[1 : 1 + n], refs[1 + n : 1 + 2 * n]
-        bary, new = refs[-2:]
-        scale = cells / jnp.sum(mass_ref[...])
-        for k, place in enumerate(places):
-            for r0, c0, width, from_col in place:
-                piece = (slice(None), slice(from_col, from_col + width))
-                bary[r0 : r0 + WIDE, c0 : c0 + width] = raw[k][piece] * scale
-                new[0, r0 : r0 + WIDE, c0 : c0 + width] = quot[k][piece] * scale
-
-    return call(body, [(rows, cols), (1, rows, cols)], [vmem()] * (1 + 2 * n), "assemble")(mass, *raws, *quots)
+        mass, raw, quot = refs[:m], refs[m : m + n], refs[m + n : m + 2 * n]
+        bary_hbm, new_hbm, bary, new, sems = refs[m + 2 * n :]
+        total = mass[0][...]
+        if m > 1:
+            total = jnp.where(in_middle(), total + mass[1][...], mass[2][...] + mass[3][...])
+        scale = cells / jnp.sum(total)
+        copies = []
+        for row in range(0, rows, WIDE):
+            band_rows = pl.ds(row, WIDE)
+            for k, place in enumerate(places):
+                for r0, c0, width, from_col in place:
+                    if r0 == row:
+                        piece = (slice(None), slice(from_col, from_col + width))
+                        bary[row : row + WIDE, c0 : c0 + width] = raw[k][piece] * scale
+                        new[row : row + WIDE, c0 : c0 + width] = quot[k][piece] * scale
+            for source, target in ((bary, bary_hbm.at[band_rows]), (new, new_hbm.at[0, band_rows])):
+                copies.append(pltpu.make_async_copy(source.at[band_rows], target, sems.at[len(copies)]))
+                copies[-1].start()
+        for copy in copies:
+            copy.wait()
+
+    tile = pltpu.VMEM((rows, cols), F32)
+    return call(
+        body,
+        [(rows, cols), (1, rows, cols)],
+        [vmem()] * (m + 2 * n),
+        "assemble",
+        scratch=[tile, tile, pltpu.SemaphoreType.DMA((2 * rows // WIDE,))],
+        out_specs=[pl.BlockSpec(memory_space=pl.ANY)] * 2,
+    )(*masses, *raws, *quots)
 
 
 def chunk_places(rows, cols):
@@ -426,28 +466,29 @@
     def total(k):
         if maps == 4:
             later = term[min(k + LAG, n - 1)]
-            held[k], passed = done(*add_and_pass(sent[k], crossed[k], later, chain[0]))
+            held[k], passed, mass[0] = done(*add_and_pass(sent[k], crossed[k], later, mass[0], chain[0]))
             outward(k + LAG, passed)
         else:
             held[k] = lax.psum(term[k], "map")
-
-    def close(k):
-        raws[k], quots[k], mass[0] = finish(held[k], got[k + LAG], ku[k], mass[0], chain[0])
-        done(mass[0])
+            (mass[0],) = done(*weigh(held[k], mass[0], chain[0]))
+
+    def close(k, name="finish"):
+        raws[k], quots[k] = done(*finish(held[k], got[k + LAG], ku[k], chain[0], name))
 
     def take(first, values):
         for k in range(len(values) // 2):
             term[first + k], ku[first + k] = values[2 * k : 2 * k + 2]
         done(values[0])
 
-    *values, tall, wide, one, two = first_chunk(weights, scaling, densities)
+    *values, tall, wide, scaling, densities, one = first_chunk(weights, scaling, densities)
     take(0, values)
     outward(0, term[0])
     one = lax.ppermute(one, "gx", near)
-    two = lax.ppermute(two, ("gx", "gy"), far)
-    take(1, inner_chunks(weights, scaling, densities, tall, wide, chain[0]))
+    *values, two = inner_chunks(weights, scaling, densities, tall, wide, (one,))
+    take(1, values)
     for k in range(1, LAG):
         outward(k, term[k])
+    two = lax.ppermute(two, ("gx", "gy"), far)
     receive(0)
     packs = done(*side_pack(scaling, densities, one, two, chain[0]))
     if gy == 2:
@@ -461,20 +502,36 @@
     total(0)
     receive(2)
     total(1)
+    receive(3)
     take(
         inner_count + 2,
         side_chunks(weights, scaling, densities, tall, one, two, from_left, from_right, chain[0]),
     )
-    for k in range(3, n):
+    total(2)
+    for k in range(4, n):
         receive(k)
-        if k >= LAG:
-            close_k = k - LAG
         total(k - 1)
-        close(close_k)
+        close(k - LAG)
+    close(n - LAG)
     total(n - 1)
-    for k in range(n - LAG, n):
-        close(k)
-    bary, new = assemble(sum_grid(mass[0]), places, raws, quots, rows, cols, cells)
+    if maps == 4 and gx == 4 and gy == 2:
+        own = sum_grid(mass[0], ("gx",))
+        swap = [(i * gy + j, (i ^ 1) * gy + 1 - j) for i in range(4) for j in range(gy)]
+        masses = [
+            own,
+            lax.ppermute(own, "gy", [(0, 1), (1, 0)]),
+            lax.ppermute(own, "map", outer),
+            lax.ppermute(own, ("map", "gy"), swap),
+        ]
+        for k in range(n - 3, n):
+            close(k, "finish_last")
+    else:
+        masses = [sum_grid(mass[0], ("gx", "gy"))]
+        if maps == 4:
+            masses = [jnp.where(in_middle(), masses[0], lax.ppermute(masses[0], "map", outer))]
+        for k in range(n - 3, n):
+            close(k)
+    bary, new = assemble(masses, places, raws, quots, rows, cols, cells)
     return bary, new
 
 

time: 78.5 us -> 65.1 us (0.83)
  waiting for transfers between devices: 23.6 us -> 11.9 us
  local copies, waits for them, and re-layouts: 2.81 us -> 0 us
  starting transfers between devices: 36.6 us -> 38 us
    ppermute x11 -> x12, waiting for transfers between devices: 14.8 us -> 7 us  [outward(): got[k] = lax.ppermute(value, 'map', outer)]
    ppermute x3 -> x2, waiting for transfers between devices: 8.16 us -> 2.61 us  [sum_grid(): lax.ppermute(mass, axis, [(i, i ^ step) for i in range(count)])]
    ppermute x0 -> x3, starting transfers between devices: none -> 3.49 us  [the longest x1 1.62 us: local(): lax.ppermute(own, ('map', 'gy'), swap)]
    unnamed x6 -> x0, local copies, waits for them, and re-layouts: 2.81 us -> none
    ppermute x11 -> x12, starting transfers between devices: 31.9 us -> 29.2 us  [outward(): got[k] = lax.ppermute(value, 'map', outer)]
    ppermute x1, waiting for transfers between devices: 0.01 us -> 1.27 us  [local(): two = lax.ppermute(two, ('gx', 'gy'), far)]
    ppermute x0 -> x3, waiting for transfers between devices: none -> 1 us  [the longest x1 1 us: local(): lax.ppermute(own, ('map', 'gy'), swap)]
    ppermute x1, starting transfers between devices: 2.59 us -> 1.64 us  [local(): two = lax.ppermute(two, ('gx', 'gy'), far)]
  transfers between devices with their start and end apart: 25 -> 28, of which waited for: 12 -> 8; matrix products, arithmetic and copies ran while one was open for 0% -> 0% of each run, Pallas kernels for 11% -> 13%
where the time goes in v3:
time: 65.1 us; the launch traced here: 64.9 us
  starting transfers between devices  38 us (58%)
  Pallas kernels  13.4 us (21%)
  waiting for transfers between devices  11.9 us (18%)
  between operations  1.58 us (2%)
    ppermute x12, starting transfers between devices, outward(): got[k] = lax.ppermute(value, 'map', outer)  29.2 us
    pallas_call x30, Pallas kernels, call(): return lambda *args: kernel(*args, *deps)  13.4 us
    ppermute x12, waiting for transfers between devices, outward(): got[k] = lax.ppermute(value, 'map', outer)  7 us
    ppermute x2, waiting for transfers between devices, sum_grid(): lax.ppermute(mass, axis, [(i, i ^ step) for i in range(count)])  2.61 us
    ppermute x1, starting transfers between devices, local(): two = lax.ppermute(two, ('gx', 'gy'), far)  1.64 us
    ppermute x1, starting transfers between devices, local(): from_left = from_right = lax.ppermute(packs[0], 'gy', [(0, 1), (1, 0)])  1.64 us
    ppermute x1, starting transfers between devices, local(): lax.ppermute(own, ('map', 'gy'), swap)  1.62 us
  transfers between devices with their start and end apart: 28, of which 8 were waited for; matrix products, arithmetic and copies ran while one was open for 0% of the time, Pallas kernels for 13%

profile of v3, /device:TPU:0, one launch (start us, length us, event | category | flops | bytes accessed | tf_op | source)
XLA Modules:
  0.0 64.9 jit_solution(15872656814994104441)
XLA Ops:
  1.3 2.9 %first.1 = (f32[64,768]{1,0:T(8,128)S(1)}, f32[64,768]{1,0:T(8,128)S(1)}, bf16[2,192,256]{2,1,0:T(8,128)(2,1)S(1)}, bf16[2,512,256]{2,1,0:T(8,128)(2,1)S(1)}, f3...) custom-call(f32[1]{0:T(128)S(6)} %copy.5.refs_0_, f32[1,384,1024]{2,1,0:T(8,128)} %refs_1_.1, ...), custom_call_target="tpu_custom_call" | custom-call | tf_op jit(solution)/shard_map/first/pallas_call | solution.py:116
  4.2 0.5 collective-permute-start
  4.7 2.6 %collective-permute-start.2 = (f32[64,768]{1,0:T(8,128)S(1)}, f32[64,768]{1,0:T(8,128)S(1)}, u32[]{:S(2)}, u32[]{:S(2)}) collective-permute-start(f32[64,768]{1,0:T(8,128)S(1)} %get-tuple-element.70.refs_0_), channel_id=1, source_target_pairs={{0,8},{8,0},{16,24},{24,16},{1,9},{9,1},{17,25},{25,17},{2,10},{10... | collective-permute-start | bytes 589832 | tf_op jit(solution)/shard_map/ppermute | solution.py:459
  7.4 2.4 %inner.1 = (f32[64,768]{1,0:T(8,128)S(1)}, f32[64,768]{1,0:T(8,128)S(1)}, f32[64,768]{1,0:T(8,128)S(1)}, f32[64,768]{1,0:T(8,128)S(1)}, f32[64,768]{1,0:T(8,128)...) custom-call(f32[1]{0:T(128)S(6)} %copy.5.refs_0_, f32[1,384,1024]{2,1,0:T(8,128)S(1)} %get-tuple-element.64.refs_1_.refs_0_, ...), custom_call_target="tpu_custom_call" | custom-call | flops 2500000000 | tf_op jit(solution)/shard_map/inner/pallas_call | solution.py:116
  9.7 1.6 %collective-permute-start.1 = (f32[96,1024]{1,0:T(8,128)S(1)}, f32[96,1024]{1,0:T(8,128)S(1)}, u32[]{:S(2)}, u32[]{:S(2)}) collective-permute-start(f32[96,1024]{1,0:T(8,128)S(1)} %get-tuple-element.69), channel_id=1, source_target_pairs={{0,1},{1,0},{2,4},{3,5},{4,2},{5,3},{6,7},{7,6},{8,9},{9,8},{10,12... | collective-permute-start | bytes 1179656 | tf_op jit(solution)/shard_map/ppermute | solution.py:491
  11.4 1.6 %collective-permute-start.5 = (f32[64,768]{1,0:T(8,128)S(1)}, f32[64,768]{1,0:T(8,128)S(1)}, u32[]{:S(2)}, u32[]{:S(2)}) collective-permute-start(f32[64,768]{1,0:T(8,128)S(1)} %get-tuple-element.71.refs_2_.refs_0_), channel_id=1, source_target_pairs={{0,8},{8,0},{16,24},{24,16},{1,9},{9,1},{17,25},{25,17},{2,10},{10... | collective-permute-start | bytes 589832 | tf_op jit(solution)/shard_map/ppermute | solution.py:459
  13.0 0.1 collective-permute-start.7
  13.1 3.2 %collective-permute-start.8 = (f32[64,768]{1,0:T(8,128)S(1)}, f32[64,768]{1,0:T(8,128)S(1)}, u32[]{:S(2)}, u32[]{:S(2)}) collective-permute-start(f32[64,768]{1,0:T(8,128)S(1)} %get-tuple-element.76.refs_0_), channel_id=1, source_target_pairs={{0,8},{8,0},{16,24},{24,16},{1,9},{9,1},{17,25},{25,17},{2,10},{10... | collective-permute-start | bytes 589832 | tf_op jit(solution)/shard_map/ppermute | solution.py:459
  16.3 1.3 %collective-permute-done.1.refs_3_.refs_6_.refs_5_ = f32[96,1024]{1,0:T(8,128)S(1)} collective-permute-done((f32[96,1024]{1,0:T(8,128)S(1)}, f32[96,1024]{1,0:T(8,128)S(1)}, u32[]{:S(2)}, u32[]{:S(2)}) %collective-permute-start.1) | collective-permute-done | bytes 393248 | tf_op jit(solution)/shard_map/ppermute | solution.py:491
  17.6 0.2 side_pack.1.refs_2_
  17.8 1.6 %collective-permute-start.3 = (f32[512,128]{1,0:T(8,128)S(1)}, f32[512,128]{1,0:T(8,128)S(1)}, u32[]{:S(2)}, u32[]{:S(2)}) collective-permute-start(f32[512,128]{1,0:T(8,128)S(1)} %side_pack.1.refs_2_), channel_id=1, source_target_pairs={{0,1},{1,0},{2,3},{3,2},{4,5},{5,4},{6,7},{7,6},{8,9},{9,8},{10,11... | collective-permute-start | bytes 786440 | tf_op jit(solution)/shard_map/ppermute | solution.py:495
  19.5 0.1 collective-permute-start.6
  19.5 2.2 %edges.1 = (f32[64,768]{1,0:T(8,128)S(1)}, f32[64,768]{1,0:T(8,128)S(1)}, f32[64,768]{1,0:T(8,128)S(1)}, f32[64,768]{1,0:T(8,128)S(1)}) custom-call(f32[1]{0:T(128)S(6)} %copy.5.refs_0_, f32[1,384,1024]{2,1,0:T(8,128)S(1)} %get-tuple-element.64.refs_1_.refs_0_, f32[1,384,1024]{2,1,0:T(8,128)S(1)} %get-tuple-element.65.refs_2_.refs_1_, ...), custom_call_target="tpu_custom_call" | custom-call | flops 2300000000 | tf_op jit(solution)/shard_map/edges/pallas_call | solution.py:116
  21.8 1.5 %collective-permute-done.8.refs_1_ = f32[64,768]{1,0:T(8,128)S(1)} collective-permute-done((f32[64,768]{1,0:T(8,128)S(1)}, f32[64,768]{1,0:T(8,128)S(1)}, u32[]{:S(2)}, u32[]{:S(2)}) %collective-permute-start.8) | collective-permute-done | bytes 196640 | tf_op jit(solution)/shard_map/ppermute | solution.py:459
  23.4 0.1 collective-permute-start.10
  23.5 3.1 %collective-permute-start.11 = (f32[64,768]{1,0:T(8,128)S(1)}, f32[64,768]{1,0:T(8,128)S(1)}, u32[]{:S(2)}, u32[]{:S(2)}) collective-permute-start(f32[64,768]{1,0:T(8,128)S(1)} %get-tuple-element.83), channel_id=1, source_target_pairs={{0,8},{8,0},{16,24},{24,16},{1,9},{9,1},{17,25},{25,17},{2,10},{10... | collective-permute-start | bytes 589832 | tf_op jit(solution)/shard_map/ppermute | solution.py:459
  26.7 0.1 collective-permute-done.4.refs_1_
  26.8 0.1 collective-permute-start.9
  26.9 3.8 %collective-permute-start.14 = (f32[64,768]{1,0:T(8,128)S(1)}, f32[64,768]{1,0:T(8,128)S(1)}, u32[]{:S(2)}, u32[]{:S(2)}) collective-permute-start(f32[64,768]{1,0:T(8,128)S(1)} %get-tuple-element.88), channel_id=1, source_target_pairs={{0,8},{8,0},{16,24},{24,16},{1,9},{9,1},{17,25},{25,17},{2,10},{10... | collective-permute-start | bytes 589832 | tf_op jit(solution)/shard_map/ppermute | solution.py:459
  30.7 2.5 %sides.1 = (f32[64,768]{1,0:T(8,128)S(1)}, f32[64,768]{1,0:T(8,128)S(1)}, f32[64,768]{1,0:T(8,128)S(1)}, f32[64,768]{1,0:T(8,128)S(1)}) custom-call(f32[1]{0:T(128)S(6)} %copy.5.refs_0_, f32[1,384,1024]{2,1,0:T(8,128)S(1)} %get-tuple-element.64.refs_1_.refs_0_, f32[1,384,1024]{2,1,0:T(8,128)S(1)} %get-tuple-element.65.refs_2_.refs_1_, ...), custom_call_target="tpu_custom_call" | custom-call | flops 2500000000 | tf_op jit(solution)/shard_map/sides/pallas_call | solution.py:116
  33.3 0.1 collective-permute-start.16
  33.4 1.6 %collective-permute-start.13 = (f32[64,768]{1,0:T(8,128)S(1)}, f32[64,768]{1,0:T(8,128)S(1)}, u32[]{:S(2)}, u32[]{:S(2)}) collective-permute-start(f32[64,768]{1,0:T(8,128)S(1)} %get-tuple-element.86), channel_id=1, source_target_pairs={{0,8},{8,0},{16,24},{24,16},{1,9},{9,1},{17,25},{25,17},{2,10},{10... | collective-permute-start | bytes 589832 | tf_op jit(solution)/shard_map/ppermute | solution.py:459
  35.1 0.1 finish.5
  35.2 0.1 collective-permute-start.15
  35.3 3.9 %collective-permute-start.12 = (f32[64,768]{1,0:T(8,128)S(1)}, f32[64,768]{1,0:T(8,128)S(1)}, u32[]{:S(2)}, u32[]{:S(2)}) collective-permute-start(f32[64,768]{1,0:T(8,128)S(1)} %get-tuple-element.85), channel_id=1, source_target_pairs={{0,8},{8,0},{16,24},{24,16},{1,9},{9,1},{17,25},{25,17},{2,10},{10... | collective-permute-start | bytes 589832 | tf_op jit(solution)/shard_map/ppermute | solution.py:459
  39.3 0.1 finish.6
  39.3 1.8 %collective-permute-done.13.refs_1_ = f32[64,768]{1,0:T(8,128)S(1)} collective-permute-done((f32[64,768]{1,0:T(8,128)S(1)}, f32[64,768]{1,0:T(8,128)S(1)}, u32[]{:S(2)}, u32[]{:S(2)}) %collective-permute-start.13) | collective-permute-done | bytes 196640 | tf_op jit(solution)/shard_map/ppermute | solution.py:459
  41.2 0.1 collective-permute-start.18
  41.3 2.2 %collective-permute-start.19 = (f32[64,768]{1,0:T(8,128)S(1)}, f32[64,768]{1,0:T(8,128)S(1)}, u32[]{:S(2)}, u32[]{:S(2)}) collective-permute-start(f32[64,768]{1,0:T(8,128)S(1)} %get-tuple-element.101), channel_id=1, source_target_pairs={{0,8},{8,0},{16,24},{24,16},{1,9},{9,1},{17,25},{25,17},{2,10},{10... | collective-permute-start | bytes 589832 | tf_op jit(solution)/shard_map/ppermute | solution.py:459
  43.5 0.1 finish.7
  43.6 1.8 %collective-permute-done.12.refs_1_ = f32[64,768]{1,0:T(8,128)S(1)} collective-permute-done((f32[64,768]{1,0:T(8,128)S(1)}, f32[64,768]{1,0:T(8,128)S(1)}, u32[]{:S(2)}, u32[]{:S(2)}) %collective-permute-start.12) | collective-permute-done | bytes 196640 | tf_op jit(solution)/shard_map/ppermute | solution.py:459
  45.4 0.1 collective-permute-start.17
  45.5 2.2 %collective-permute-start.25 = (f32[64,768]{1,0:T(8,128)S(1)}, f32[64,768]{1,0:T(8,128)S(1)}, u32[]{:S(2)}, u32[]{:S(2)}) collective-permute-start(f32[64,768]{1,0:T(8,128)S(1)} %get-tuple-element.108), channel_id=1, source_target_pairs={{0,8},{8,0},{16,24},{24,16},{1,9},{9,1},{17,25},{25,17},{2,10},{10... | collective-permute-start | bytes 589832 | tf_op jit(solution)/shard_map/ppermute | solution.py:459
  47.7 2.5 %collective-permute-start.26 = (f32[64,768]{1,0:T(8,128)S(1)}, f32[64,768]{1,0:T(8,128)S(1)}, u32[]{:S(2)}, u32[]{:S(2)}) collective-permute-start(f32[64,768]{1,0:T(8,128)S(1)} %get-tuple-element.112), channel_id=1, source_target_pairs={{0,8},{8,0},{16,24},{24,16},{1,9},{9,1},{17,25},{25,17},{2,10},{10... | collective-permute-start | bytes 589832 | tf_op jit(solution)/shard_map/ppermute | solution.py:459
  50.2 0.1 finish.8
  50.3 0.1 finish.9
  50.4 0.1 collective-permute-start.20
  50.5 2.5 %collective-permute-start.27 = (f32[64,768]{1,0:T(8,128)S(1)}, f32[64,768]{1,0:T(8,128)S(1)}, u32[]{:S(2)}, u32[]{:S(2)}) collective-permute-start(f32[64,768]{1,0:T(8,128)S(1)} %get-tuple-element.115), channel_id=1, source_target_pairs={{0,8},{8,0},{16,24},{24,16},{1,9},{9,1},{17,25},{25,17},{2,10},{10... | collective-permute-start | bytes 589832 | tf_op jit(solution)/shard_map/ppermute | solution.py:459
  53.0 0.9 %collective-permute-start.21 = (f32[8,128]{1,0:T(8,128)S(1)}, f32[8,128]{1,0:T(8,128)S(1)}, u32[]{:S(2)}, u32[]{:S(2)}) collective-permute-start(f32[8,128]{1,0:T(8,128)S(1)} %add.14), channel_id=1, source_target_pairs={{0,4},{2,6},{4,0},{6,2},{1,5},{3,7},{5,1},{7,3},{8,12},{10,14},{12... | collective-permute-start | bytes 12296 | tf_op jit(solution)/shard_map/ppermute | solution.py:375
  53.9 0.1 finish_last.3
  54.0 2.6 %collective-permute-done.21 = f32[8,128]{1,0:T(8,128)S(1)} collective-permute-done((f32[8,128]{1,0:T(8,128)S(1)}, f32[8,128]{1,0:T(8,128)S(1)}, u32[]{:S(2)}, u32[]{:S(2)}) %collective-permute-start.21) | collective-permute-done | bytes 4128 | tf_op jit(solution)/shard_map/ppermute | solution.py:375
  56.6 0.8 %collective-permute-start.22 = (f32[8,128]{1,0:T(8,128)S(1)}, f32[8,128]{1,0:T(8,128)S(1)}, u32[]{:S(2)}, u32[]{:S(2)}) collective-permute-start(f32[8,128]{1,0:T(8,128)S(1)} %add.15.refs_0_), channel_id=1, source_target_pairs={{0,1},{1,0},{2,3},{3,2},{4,5},{5,4},{6,7},{7,6},{8,9},{9,8},{10,11... | collective-permute-start | bytes 12296 | tf_op jit(solution)/shard_map/ppermute | solution.py:522
  57.4 1.1 %collective-permute-start.23 = (f32[8,128]{1,0:T(8,128)S(1)}, f32[8,128]{1,0:T(8,128)S(1)}, u32[]{:S(2)}, u32[]{:S(2)}) collective-permute-start(f32[8,128]{1,0:T(8,128)S(1)} %add.15.refs_0_), channel_id=1, source_target_pairs={{0,8},{8,0},{16,24},{24,16},{1,9},{9,1},{17,25},{25,17},{2,10},{10... | collective-permute-start | bytes 12296 | tf_op jit(solution)/shard_map/ppermute | solution.py:523
  58.4 1.6 %collective-permute-start.24 = (f32[8,128]{1,0:T(8,128)S(1)}, f32[8,128]{1,0:T(8,128)S(1)}, u32[]{:S(2)}, u32[]{:S(2)}) collective-permute-start(f32[8,128]{1,0:T(8,128)S(1)} %add.15.refs_0_), channel_id=1, source_target_pairs={{0,9},{1,8},{8,1},{9,0},{16,25},{17,24},{24,17},{25,16},{2,11},{3,... | collective-permute-start | bytes 12296 | tf_op jit(solution)/shard_map/ppermute | solution.py:524
  60.1 0.1 finish_last.4
  60.1 1.7 %collective-permute-done.27.refs_1_ = f32[64,768]{1,0:T(8,128)S(1)} collective-permute-done((f32[64,768]{1,0:T(8,128)S(1)}, f32[64,768]{1,0:T(8,128)S(1)}, u32[]{:S(2)}, u32[]{:S(2)}) %collective-permute-start.27) | collective-permute-done | bytes 196640 | tf_op jit(solution)/shard_map/ppermute | solution.py:459
  62.0 1.0 %collective-permute-done.24.refs_3_ = f32[8,128]{1,0:T(8,128)S(1)} collective-permute-done((f32[8,128]{1,0:T(8,128)S(1)}, f32[8,128]{1,0:T(8,128)S(1)}, u32[]{:S(2)}, u32[]{:S(2)}) %collective-permute-start.24) | collective-permute-done | bytes 4128 | tf_op jit(solution)/shard_map/ppermute | solution.py:524
  63.0 1.9 %assemble.1 = (f32[384,1024]{1,0:T(8,128)}, f32[1,384,1024]{2,1,0:T(8,128)}) custom-call(f32[8,128]{1,0:T(8,128)S(1)} %add.15.refs_0_, f32[8,128]{1,0:T(8,128)S(1)} %collective-permute-done.22.refs_1_, f32[8,128]{1,0:T(8,128)S(1)} %collective-permute-done.23.refs_2_, f32[8,128]{1,0:T(8,128)S(1)} %collective-permute-done.24.refs_3_, ...), custom_call_target="tpu_custom_call" | custom-call | tf_op jit(solution)/shard_map/assemble/pallas_call | solution.py:116
  (40 shorter events, 0.8 us)
Async XLA Ops:
  4.2 3.2 %collective-permute-start = (f32[96,1024]{1,0:T(8,128)S(1)}, f32[96,1024]{1,0:T(8,128)S(1)}, u32[]{:S(2)}, u32[]{:S(2)}) collective-permute-start(f32[96,1024]{1,0:T(8,128)S(1)} %get-tuple-element.67), channel_id=1, source_target_pairs={{0,2},{2,0},{4,6},{6,4},{1,3},{3,1},{5,7},{7,5},{8,10},{10,8},{12,... | collective-permute-start | bytes 1179656 | tf_op jit(solution)/shard_map/ppermute | solution.py:486
  4.7 8.2 %collective-permute-start.2 = (f32[64,768]{1,0:T(8,128)S(1)}, f32[64,768]{1,0:T(8,128)S(1)}, u32[]{:S(2)}, u32[]{:S(2)}) collective-permute-start(f32[64,768]{1,0:T(8,128)S(1)} %get-tuple-element.70.refs_0_), channel_id=1, source_target_pairs={{0,8},{8,0},{16,24},{24,16},{1,9},{9,1},{17,25},{25,17},{2,10},{10... | collective-permute-start | bytes 589832 | tf_op jit(solution)/shard_map/ppermute | solution.py:459
  9.7 7.8 %collective-permute-start.1 = (f32[96,1024]{1,0:T(8,128)S(1)}, f32[96,1024]{1,0:T(8,128)S(1)}, u32[]{:S(2)}, u32[]{:S(2)}) collective-permute-start(f32[96,1024]{1,0:T(8,128)S(1)} %get-tuple-element.69), channel_id=1, source_target_pairs={{0,1},{1,0},{2,4},{3,5},{4,2},{5,3},{6,7},{7,6},{8,9},{9,8},{10,12... | collective-permute-start | bytes 1179656 | tf_op jit(solution)/shard_map/ppermute | solution.py:491
  11.4 8.0 %collective-permute-start.5 = (f32[64,768]{1,0:T(8,128)S(1)}, f32[64,768]{1,0:T(8,128)S(1)}, u32[]{:S(2)}, u32[]{:S(2)}) collective-permute-start(f32[64,768]{1,0:T(8,128)S(1)} %get-tuple-element.71.refs_2_.refs_0_), channel_id=1, source_target_pairs={{0,8},{8,0},{16,24},{24,16},{1,9},{9,1},{17,25},{25,17},{2,10},{10... | collective-permute-start | bytes 589832 | tf_op jit(solution)/shard_map/ppermute | solution.py:459
  13.0 8.8 %collective-permute-start.7 = (f32[64,768]{1,0:T(8,128)S(1)}, f32[64,768]{1,0:T(8,128)S(1)}, u32[]{:S(2)}, u32[]{:S(2)}) collective-permute-start(f32[64,768]{1,0:T(8,128)S(1)} %add.16.refs_4_.refs_0_), channel_id=1, source_target_pairs={{8,16},{16,8},{0,2},{24,26},{10,18},{18,10},{2,0},{26,24},{12,20},... | collective-permute-start | bytes 589832 | tf_op jit(solution)/shard_map/ppermute | solution.py:464
  13.1 10.3 %collective-permute-start.8 = (f32[64,768]{1,0:T(8,128)S(1)}, f32[64,768]{1,0:T(8,128)S(1)}, u32[]{:S(2)}, u32[]{:S(2)}) collective-permute-start(f32[64,768]{1,0:T(8,128)S(1)} %get-tuple-element.76.refs_0_), channel_id=1, source_target_pairs={{0,8},{8,0},{16,24},{24,16},{1,9},{9,1},{17,25},{25,17},{2,10},{10... | collective-permute-start | bytes 589832 | tf_op jit(solution)/shard_map/ppermute | solution.py:459
  16.3 10.5 %collective-permute-start.4 = (f32[64,768]{1,0:T(8,128)S(1)}, f32[64,768]{1,0:T(8,128)S(1)}, u32[]{:S(2)}, u32[]{:S(2)}) collective-permute-start(f32[64,768]{1,0:T(8,128)S(1)} %get-tuple-element.72.refs_0_), channel_id=1, source_target_pairs={{0,8},{8,0},{16,24},{24,16},{1,9},{9,1},{17,25},{25,17},{2,10},{10... | collective-permute-start | bytes 589832 | tf_op jit(solution)/shard_map/ppermute | solution.py:459
  17.8 12.9 %collective-permute-start.3 = (f32[512,128]{1,0:T(8,128)S(1)}, f32[512,128]{1,0:T(8,128)S(1)}, u32[]{:S(2)}, u32[]{:S(2)}) collective-permute-start(f32[512,128]{1,0:T(8,128)S(1)} %side_pack.1.refs_2_), channel_id=1, source_target_pairs={{0,1},{1,0},{2,3},{3,2},{4,5},{5,4},{6,7},{7,6},{8,9},{9,8},{10,11... | collective-permute-start | bytes 786440 | tf_op jit(solution)/shard_map/ppermute | solution.py:495
  19.5 7.2 %collective-permute-start.6 = (f32[64,768]{1,0:T(8,128)S(1)}, f32[64,768]{1,0:T(8,128)S(1)}, u32[]{:S(2)}, u32[]{:S(2)}) collective-permute-start(f32[64,768]{1,0:T(8,128)S(1)} %add.17.refs_7_.refs_0_), channel_id=1, source_target_pairs={{8,16},{16,8},{0,2},{24,26},{10,18},{18,10},{2,0},{26,24},{12,20},... | collective-permute-start | bytes 589832 | tf_op jit(solution)/shard_map/ppermute | solution.py:464
  23.4 9.8 %collective-permute-start.10 = (f32[64,768]{1,0:T(8,128)S(1)}, f32[64,768]{1,0:T(8,128)S(1)}, u32[]{:S(2)}, u32[]{:S(2)}) collective-permute-start(f32[64,768]{1,0:T(8,128)S(1)} %add.18.refs_4_.refs_0_), channel_id=1, source_target_pairs={{8,16},{16,8},{0,2},{24,26},{10,18},{18,10},{2,0},{26,24},{12,20},... | collective-permute-start | bytes 589832 | tf_op jit(solution)/shard_map/ppermute | solution.py:464
  23.5 9.8 %collective-permute-start.11 = (f32[64,768]{1,0:T(8,128)S(1)}, f32[64,768]{1,0:T(8,128)S(1)}, u32[]{:S(2)}, u32[]{:S(2)}) collective-permute-start(f32[64,768]{1,0:T(8,128)S(1)} %get-tuple-element.83), channel_id=1, source_target_pairs={{0,8},{8,0},{16,24},{24,16},{1,9},{9,1},{17,25},{25,17},{2,10},{10... | collective-permute-start | bytes 589832 | tf_op jit(solution)/shard_map/ppermute | solution.py:459
  26.8 8.2 %collective-permute-start.9 = (f32[64,768]{1,0:T(8,128)S(1)}, f32[64,768]{1,0:T(8,128)S(1)}, u32[]{:S(2)}, u32[]{:S(2)}) collective-permute-start(f32[64,768]{1,0:T(8,128)S(1)} %add.19.refs_8_.refs_0_), channel_id=1, source_target_pairs={{8,16},{16,8},{0,2},{24,26},{10,18},{18,10},{2,0},{26,24},{12,20},... | collective-permute-start | bytes 589832 | tf_op jit(solution)/shard_map/ppermute | solution.py:464
  26.9 8.2 %collective-permute-start.14 = (f32[64,768]{1,0:T(8,128)S(1)}, f32[64,768]{1,0:T(8,128)S(1)}, u32[]{:S(2)}, u32[]{:S(2)}) collective-permute-start(f32[64,768]{1,0:T(8,128)S(1)} %get-tuple-element.88), channel_id=1, source_target_pairs={{0,8},{8,0},{16,24},{24,16},{1,9},{9,1},{17,25},{25,17},{2,10},{10... | collective-permute-start | bytes 589832 | tf_op jit(solution)/shard_map/ppermute | solution.py:459
  33.3 5.9 %collective-permute-start.16 = (f32[64,768]{1,0:T(8,128)S(1)}, f32[64,768]{1,0:T(8,128)S(1)}, u32[]{:S(2)}, u32[]{:S(2)}) collective-permute-start(f32[64,768]{1,0:T(8,128)S(1)} %add.20.refs_4_.refs_0_), channel_id=1, source_target_pairs={{8,16},{16,8},{0,2},{24,26},{10,18},{18,10},{2,0},{26,24},{12,20},... | collective-permute-start | bytes 589832 | tf_op jit(solution)/shard_map/ppermute | solution.py:464
  33.4 7.8 %collective-permute-start.13 = (f32[64,768]{1,0:T(8,128)S(1)}, f32[64,768]{1,0:T(8,128)S(1)}, u32[]{:S(2)}, u32[]{:S(2)}) collective-permute-start(f32[64,768]{1,0:T(8,128)S(1)} %get-tuple-element.86), channel_id=1, source_target_pairs={{0,8},{8,0},{16,24},{24,16},{1,9},{9,1},{17,25},{25,17},{2,10},{10... | collective-permute-start | bytes 589832 | tf_op jit(solution)/shard_map/ppermute | solution.py:459
  35.2 8.2 %collective-permute-start.15 = (f32[64,768]{1,0:T(8,128)S(1)}, f32[64,768]{1,0:T(8,128)S(1)}, u32[]{:S(2)}, u32[]{:S(2)}) collective-permute-start(f32[64,768]{1,0:T(8,128)S(1)} %add.21.refs_4_.refs_0_), channel_id=1, source_target_pairs={{8,16},{16,8},{0,2},{24,26},{10,18},{18,10},{2,0},{26,24},{12,20},... | collective-permute-start | bytes 589832 | tf_op jit(solution)/shard_map/ppermute | solution.py:464
  35.3 10.1 %collective-permute-start.12 = (f32[64,768]{1,0:T(8,128)S(1)}, f32[64,768]{1,0:T(8,128)S(1)}, u32[]{:S(2)}, u32[]{:S(2)}) collective-permute-start(f32[64,768]{1,0:T(8,128)S(1)} %get-tuple-element.85), channel_id=1, source_target_pairs={{0,8},{8,0},{16,24},{24,16},{1,9},{9,1},{17,25},{25,17},{2,10},{10... | collective-permute-start | bytes 589832 | tf_op jit(solution)/shard_map/ppermute | solution.py:459
  41.2 6.5 %collective-permute-start.18 = (f32[64,768]{1,0:T(8,128)S(1)}, f32[64,768]{1,0:T(8,128)S(1)}, u32[]{:S(2)}, u32[]{:S(2)}) collective-permute-start(f32[64,768]{1,0:T(8,128)S(1)} %add.22.refs_4_.refs_0_), channel_id=1, source_target_pairs={{8,16},{16,8},{0,2},{24,26},{10,18},{18,10},{2,0},{26,24},{12,20},... | collective-permute-start | bytes 589832 | tf_op jit(solution)/shard_map/ppermute | solution.py:464
  41.3 9.0 %collective-permute-start.19 = (f32[64,768]{1,0:T(8,128)S(1)}, f32[64,768]{1,0:T(8,128)S(1)}, u32[]{:S(2)}, u32[]{:S(2)}) collective-permute-start(f32[64,768]{1,0:T(8,128)S(1)} %get-tuple-element.101), channel_id=1, source_target_pairs={{0,8},{8,0},{16,24},{24,16},{1,9},{9,1},{17,25},{25,17},{2,10},{10... | collective-permute-start | bytes 589832 | tf_op jit(solution)/shard_map/ppermute | solution.py:459
  45.4 5.0 %collective-permute-start.17 = (f32[64,768]{1,0:T(8,128)S(1)}, f32[64,768]{1,0:T(8,128)S(1)}, u32[]{:S(2)}, u32[]{:S(2)}) collective-permute-start(f32[64,768]{1,0:T(8,128)S(1)} %add.23.refs_4_.refs_0_), channel_id=1, source_target_pairs={{8,16},{16,8},{0,2},{24,26},{10,18},{18,10},{2,0},{26,24},{12,20},... | collective-permute-start | bytes 589832 | tf_op jit(solution)/shard_map/ppermute | solution.py:464
  45.5 8.4 %collective-permute-start.25 = (f32[64,768]{1,0:T(8,128)S(1)}, f32[64,768]{1,0:T(8,128)S(1)}, u32[]{:S(2)}, u32[]{:S(2)}) collective-permute-start(f32[64,768]{1,0:T(8,128)S(1)} %get-tuple-element.108), channel_id=1, source_target_pairs={{0,8},{8,0},{16,24},{24,16},{1,9},{9,1},{17,25},{25,17},{2,10},{10... | collective-permute-start | bytes 589832 | tf_op jit(solution)/shard_map/ppermute | solution.py:459
  47.7 12.4 %collective-permute-start.26 = (f32[64,768]{1,0:T(8,128)S(1)}, f32[64,768]{1,0:T(8,128)S(1)}, u32[]{:S(2)}, u32[]{:S(2)}) collective-permute-start(f32[64,768]{1,0:T(8,128)S(1)} %get-tuple-element.112), channel_id=1, source_target_pairs={{0,8},{8,0},{16,24},{24,16},{1,9},{9,1},{17,25},{25,17},{2,10},{10... | collective-permute-start | bytes 589832 | tf_op jit(solution)/shard_map/ppermute | solution.py:459
  50.4 2.5 %collective-permute-start.20 = (f32[8,128]{1,0:T(8,128)S(1)}, f32[8,128]{1,0:T(8,128)S(1)}, u32[]{:S(2)}, u32[]{:S(2)}) collective-permute-start(f32[8,128]{1,0:T(8,128)S(1)} %get-tuple-element.107), channel_id=1, source_target_pairs={{0,2},{2,0},{4,6},{6,4},{1,3},{3,1},{5,7},{7,5},{8,10},{10,8},{12,... | collective-permute-start | bytes 12296 | tf_op jit(solution)/shard_map/ppermute | solution.py:375
  50.5 11.4 %collective-permute-start.27 = (f32[64,768]{1,0:T(8,128)S(1)}, f32[64,768]{1,0:T(8,128)S(1)}, u32[]{:S(2)}, u32[]{:S(2)}) collective-permute-start(f32[64,768]{1,0:T(8,128)S(1)} %get-tuple-element.115), channel_id=1, source_target_pairs={{0,8},{8,0},{16,24},{24,16},{1,9},{9,1},{17,25},{25,17},{2,10},{10... | collective-permute-start | bytes 589832 | tf_op jit(solution)/shard_map/ppermute | solution.py:459
  53.0 3.6 %collective-permute-start.21 = (f32[8,128]{1,0:T(8,128)S(1)}, f32[8,128]{1,0:T(8,128)S(1)}, u32[]{:S(2)}, u32[]{:S(2)}) collective-permute-start(f32[8,128]{1,0:T(8,128)S(1)} %add.14), channel_id=1, source_target_pairs={{0,4},{2,6},{4,0},{6,2},{1,5},{3,7},{5,1},{7,3},{8,12},{10,14},{12... | collective-permute-start | bytes 12296 | tf_op jit(solution)/shard_map/ppermute | solution.py:375
  56.6 5.4 %collective-permute-start.22 = (f32[8,128]{1,0:T(8,128)S(1)}, f32[8,128]{1,0:T(8,128)S(1)}, u32[]{:S(2)}, u32[]{:S(2)}) collective-permute-start(f32[8,128]{1,0:T(8,128)S(1)} %add.15.refs_0_), channel_id=1, source_target_pairs={{0,1},{1,0},{2,3},{3,2},{4,5},{5,4},{6,7},{7,6},{8,9},{9,8},{10,11... | collective-permute-start | bytes 12296 | tf_op jit(solution)/shard_map/ppermute | solution.py:522
  57.4 4.6 %collective-permute-start.23 = (f32[8,128]{1,0:T(8,128)S(1)}, f32[8,128]{1,0:T(8,128)S(1)}, u32[]{:S(2)}, u32[]{:S(2)}) collective-permute-start(f32[8,128]{1,0:T(8,128)S(1)} %add.15.refs_0_), channel_id=1, source_target_pairs={{0,8},{8,0},{16,24},{24,16},{1,9},{9,1},{17,25},{25,17},{2,10},{10... | collective-permute-start | bytes 12296 | tf_op jit(solution)/shard_map/ppermute | solution.py:523
  58.4 4.5 %collective-permute-start.24 = (f32[8,128]{1,0:T(8,128)S(1)}, f32[8,128]{1,0:T(8,128)S(1)}, u32[]{:S(2)}, u32[]{:S(2)}) collective-permute-start(f32[8,128]{1,0:T(8,128)S(1)} %add.15.refs_0_), channel_id=1, source_target_pairs={{0,9},{1,8},{8,1},{9,0},{16,25},{17,24},{24,17},{25,16},{2,11},{3,... | collective-permute-start | bytes 12296 | tf_op jit(solution)/shard_map/ppermute | solution.py:524

commit v4 on v3

--- a/solution.py
+++ b/solution.py
@@ -385,7 +385,7 @@
         bary_hbm, new_hbm, bary, new, sems = refs[m + 2 * n :]
         total = mass[0][...]
         if m > 1:
-            total = jnp.where(in_middle(), total + mass[1][...], mass[2][...] + mass[3][...])
+            total = jnp.where(in_middle(), total + mass[3][...], mass[2][...] + mass[1][...])
         scale = cells / jnp.sum(total)
         copies = []
         for row in range(0, rows, WIDE):
@@ -490,23 +490,21 @@
         outward(k, term[k])
     two = lax.ppermute(two, ("gx", "gy"), far)
     receive(0)
+    inner_count = rows // WIDE - 2
+    receive(1)
     packs = done(*side_pack(scaling, densities, one, two, chain[0]))
     if gy == 2:
         from_left = from_right = lax.ppermute(packs[0], "gy", [(0, 1), (1, 0)])
     else:
         from_left = lax.ppermute(packs[0], "gy", [(i, i + 1) for i in range(gy - 1)])
         from_right = lax.ppermute(packs[1], "gy", [(i + 1, i) for i in range(gy - 1)])
-    receive(1)
-    inner_count = rows // WIDE - 2
     take(inner_count, edge_chunks(weights, scaling, densities, tall, wide, one, two, chain[0]))
     total(0)
     receive(2)
     total(1)
     receive(3)
-    take(
-        inner_count + 2,
-        side_chunks(weights, scaling, densities, tall, one, two, from_left, from_right, chain[0]),
-    )
+    sides = side_chunks(weights, scaling, densities, tall, one, two, from_left, from_right, chain[0])
+    take(inner_count + 2, sides)
     total(2)
     for k in range(4, n):
         receive(k)
@@ -519,9 +517,9 @@
         swap = [(i * gy + j, (i ^ 1) * gy + 1 - j) for i in range(4) for j in range(gy)]
         masses = [
             own,
+            lax.ppermute(own, ("map", "gy"), swap),
+            lax.ppermute(own, "map", outer),
             lax.ppermute(own, "gy", [(0, 1), (1, 0)]),
-            lax.ppermute(own, "map", outer),
-            lax.ppermute(own, ("map", "gy"), swap),
         ]
         for k in range(n - 3, n):
             close(k, "finish_last")

time: 65.1 us -> 64.1 us (0.985)
  waiting for transfers between devices: 11.9 us -> 10.4 us
    ppermute x12, waiting for transfers between devices: 7 us -> 4.43 us  [outward(): got[k] = lax.ppermute(value, 'map', outer)]
  transfers between devices with their start and end apart: 28 -> 28, of which waited for: 8 -> 10; matrix products, arithmetic and copies ran while one was open for 0% -> 0% of each run, Pallas kernels for 13% -> 13%
where the time goes in v4:
time: 64.1 us; the launch traced here: 63.9 us
  starting transfers between devices  38.6 us (60%)
  Pallas kernels  13.4 us (21%)
  waiting for transfers between devices  10.4 us (16%)
  between operations  1.57 us (2%)
    ppermute x12, starting transfers between devices, outward(): got[k] = lax.ppermute(value, 'map', outer)  29.8 us
    pallas_call x30, Pallas kernels, call(): return lambda *args: kernel(*args, *deps)  13.4 us
    ppermute x12, waiting for transfers between devices, outward(): got[k] = lax.ppermute(value, 'map', outer)  4.43 us
    ppermute x2, waiting for transfers between devices, sum_grid(): lax.ppermute(mass, axis, [(i, i ^ step) for i in range(count)])  2.47 us
    ppermute x1, waiting for transfers between devices, local(): two = lax.ppermute(two, ('gx', 'gy'), far)  1.89 us
    ppermute x1, starting transfers between devices, local(): from_left = from_right = lax.ppermute(packs[0], 'gy', [(0, 1), (1, 0)])  1.58 us
    ppermute x1, starting transfers between devices, local(): two = lax.ppermute(two, ('gx', 'gy'), far)  1.52 us
    ppermute x1, starting transfers between devices, local(): lax.ppermute(own, ('map', 'gy'), swap)  1.36 us
  transfers between devices with their start and end apart: 28, of which 10 were waited for; matrix products, arithmetic and copies ran while one was open for 0% of the time, Pallas kernels for 13%

profile of v4, /device:TPU:0, one launch (start us, length us, event | category | flops | bytes accessed | tf_op | source)
XLA Modules:
  0.0 63.9 jit_solution(11892403758687018946)
XLA Ops:
  1.3 2.9 %first.1 = (f32[64,768]{1,0:T(8,128)S(1)}, f32[64,768]{1,0:T(8,128)S(1)}, bf16[2,192,256]{2,1,0:T(8,128)(2,1)S(1)}, bf16[2,512,256]{2,1,0:T(8,128)(2,1)S(1)}, f3...) custom-call(f32[1]{0:T(128)S(6)} %copy.5.refs_0_, f32[1,384,1024]{2,1,0:T(8,128)} %refs_1_.1, ...), custom_call_target="tpu_custom_call" | custom-call | tf_op jit(solution)/shard_map/first/pallas_call | solution.py:116
  4.2 0.5 collective-permute-start
  4.7 2.6 %collective-permute-start.3 = (f32[64,768]{1,0:T(8,128)S(1)}, f32[64,768]{1,0:T(8,128)S(1)}, u32[]{:S(2)}, u32[]{:S(2)}) collective-permute-start(f32[64,768]{1,0:T(8,128)S(1)} %get-tuple-element.71.refs_0_), channel_id=1, source_target_pairs={{0,8},{8,0},{16,24},{24,16},{1,9},{9,1},{17,25},{25,17},{2,10},{10... | collective-permute-start | bytes 589832 | tf_op jit(solution)/shard_map/ppermute | solution.py:459
  7.4 2.4 %inner.1 = (f32[64,768]{1,0:T(8,128)S(1)}, f32[64,768]{1,0:T(8,128)S(1)}, f32[64,768]{1,0:T(8,128)S(1)}, f32[64,768]{1,0:T(8,128)S(1)}, f32[64,768]{1,0:T(8,128)...) custom-call(f32[1]{0:T(128)S(6)} %copy.5.refs_0_, f32[1,384,1024]{2,1,0:T(8,128)S(1)} %get-tuple-element.64.refs_1_.refs_0_, ...), custom_call_target="tpu_custom_call" | custom-call | flops 2500000000 | tf_op jit(solution)/shard_map/inner/pallas_call | solution.py:116
  9.7 1.7 %collective-permute-start.2 = (f32[64,768]{1,0:T(8,128)S(1)}, f32[64,768]{1,0:T(8,128)S(1)}, u32[]{:S(2)}, u32[]{:S(2)}) collective-permute-start(f32[64,768]{1,0:T(8,128)S(1)} %get-tuple-element.70.refs_2_.refs_0_), channel_id=1, source_target_pairs={{0,8},{8,0},{16,24},{24,16},{1,9},{9,1},{17,25},{25,17},{2,10},{10... | collective-permute-start | bytes 589832 | tf_op jit(solution)/shard_map/ppermute | solution.py:459
  11.4 1.5 %collective-permute-start.1 = (f32[96,1024]{1,0:T(8,128)S(1)}, f32[96,1024]{1,0:T(8,128)S(1)}, u32[]{:S(2)}, u32[]{:S(2)}) collective-permute-start(f32[96,1024]{1,0:T(8,128)S(1)} %get-tuple-element.69), channel_id=1, source_target_pairs={{0,1},{1,0},{2,4},{3,5},{4,2},{5,3},{6,7},{7,6},{8,9},{9,8},{10,12... | collective-permute-start | bytes 1179656 | tf_op jit(solution)/shard_map/ppermute | solution.py:491
  13.0 0.2 collective-permute-done.3.refs_1_
  13.2 0.1 collective-permute-start.7
  13.2 3.4 %collective-permute-start.8 = (f32[64,768]{1,0:T(8,128)S(1)}, f32[64,768]{1,0:T(8,128)S(1)}, u32[]{:S(2)}, u32[]{:S(2)}) collective-permute-start(f32[64,768]{1,0:T(8,128)S(1)} %get-tuple-element.76.refs_0_), channel_id=1, source_target_pairs={{0,8},{8,0},{16,24},{24,16},{1,9},{9,1},{17,25},{25,17},{2,10},{10... | collective-permute-start | bytes 589832 | tf_op jit(solution)/shard_map/ppermute | solution.py:459
  16.7 0.5 collective-permute-done.2.refs_1_
  17.3 0.1 collective-permute-start.6
  17.3 1.9 %collective-permute-done.1.refs_3_.refs_6_.refs_5_ = f32[96,1024]{1,0:T(8,128)S(1)} collective-permute-done((f32[96,1024]{1,0:T(8,128)S(1)}, f32[96,1024]{1,0:T(8,128)S(1)}, u32[]{:S(2)}, u32[]{:S(2)}) %collective-permute-start.1) | collective-permute-done | bytes 393248 | tf_op jit(solution)/shard_map/ppermute | solution.py:491
  19.2 0.2 side_pack.1.refs_7_
  19.4 1.6 %collective-permute-start.4 = (f32[512,128]{1,0:T(8,128)S(1)}, f32[512,128]{1,0:T(8,128)S(1)}, u32[]{:S(2)}, u32[]{:S(2)}) collective-permute-start(f32[512,128]{1,0:T(8,128)S(1)} %side_pack.1.refs_7_), channel_id=1, source_target_pairs={{0,1},{1,0},{2,3},{3,2},{4,5},{5,4},{6,7},{7,6},{8,9},{9,8},{10,11... | collective-permute-start | bytes 786440 | tf_op jit(solution)/shard_map/ppermute | solution.py:497
  21.0 2.2 %edges.1 = (f32[64,768]{1,0:T(8,128)S(1)}, f32[64,768]{1,0:T(8,128)S(1)}, f32[64,768]{1,0:T(8,128)S(1)}, f32[64,768]{1,0:T(8,128)S(1)}) custom-call(f32[1]{0:T(128)S(6)} %copy.5.refs_0_, f32[1,384,1024]{2,1,0:T(8,128)S(1)} %get-tuple-element.64.refs_1_.refs_0_, f32[1,384,1024]{2,1,0:T(8,128)S(1)} %get-tuple-element.65.refs_2_.refs_1_, ...), custom_call_target="tpu_custom_call" | custom-call | flops 2300000000 | tf_op jit(solution)/shard_map/edges/pallas_call | solution.py:116
  23.3 0.1 collective-permute-start.10
  23.4 3.1 %collective-permute-start.11 = (f32[64,768]{1,0:T(8,128)S(1)}, f32[64,768]{1,0:T(8,128)S(1)}, u32[]{:S(2)}, u32[]{:S(2)}) collective-permute-start(f32[64,768]{1,0:T(8,128)S(1)} %get-tuple-element.83), channel_id=1, source_target_pairs={{0,8},{8,0},{16,24},{24,16},{1,9},{9,1},{17,25},{25,17},{2,10},{10... | collective-permute-start | bytes 589832 | tf_op jit(solution)/shard_map/ppermute | solution.py:459
  26.7 0.1 collective-permute-start.9
  26.7 2.4 %collective-permute-start.14 = (f32[64,768]{1,0:T(8,128)S(1)}, f32[64,768]{1,0:T(8,128)S(1)}, u32[]{:S(2)}, u32[]{:S(2)}) collective-permute-start(f32[64,768]{1,0:T(8,128)S(1)} %get-tuple-element.88), channel_id=1, source_target_pairs={{0,8},{8,0},{16,24},{24,16},{1,9},{9,1},{17,25},{25,17},{2,10},{10... | collective-permute-start | bytes 589832 | tf_op jit(solution)/shard_map/ppermute | solution.py:459
  29.2 2.5 %sides.1 = (f32[64,768]{1,0:T(8,128)S(1)}, f32[64,768]{1,0:T(8,128)S(1)}, f32[64,768]{1,0:T(8,128)S(1)}, f32[64,768]{1,0:T(8,128)S(1)}) custom-call(f32[1]{0:T(128)S(6)} %copy.5.refs_0_, f32[1,384,1024]{2,1,0:T(8,128)S(1)} %get-tuple-element.64.refs_1_.refs_0_, f32[1,384,1024]{2,1,0:T(8,128)S(1)} %get-tuple-element.65.refs_2_.refs_1_, ...), custom_call_target="tpu_custom_call" | custom-call | flops 2500000000 | tf_op jit(solution)/shard_map/sides/pallas_call | solution.py:116
  31.8 0.1 collective-permute-start.16
  31.9 2.4 %collective-permute-start.13 = (f32[64,768]{1,0:T(8,128)S(1)}, f32[64,768]{1,0:T(8,128)S(1)}, u32[]{:S(2)}, u32[]{:S(2)}) collective-permute-start(f32[64,768]{1,0:T(8,128)S(1)} %get-tuple-element.86), channel_id=1, source_target_pairs={{0,8},{8,0},{16,24},{24,16},{1,9},{9,1},{17,25},{25,17},{2,10},{10... | collective-permute-start | bytes 589832 | tf_op jit(solution)/shard_map/ppermute | solution.py:459
  34.3 0.1 finish.5
  34.4 0.6 collective-permute-done.14.refs_1_
  35.0 0.1 collective-permute-start.15
  35.1 3.2 %collective-permute-start.12 = (f32[64,768]{1,0:T(8,128)S(1)}, f32[64,768]{1,0:T(8,128)S(1)}, u32[]{:S(2)}, u32[]{:S(2)}) collective-permute-start(f32[64,768]{1,0:T(8,128)S(1)} %get-tuple-element.85), channel_id=1, source_target_pairs={{0,8},{8,0},{16,24},{24,16},{1,9},{9,1},{17,25},{25,17},{2,10},{10... | collective-permute-start | bytes 589832 | tf_op jit(solution)/shard_map/ppermute | solution.py:459
  38.3 0.1 finish.6
  38.4 1.5 %collective-permute-done.13.refs_1_ = f32[64,768]{1,0:T(8,128)S(1)} collective-permute-done((f32[64,768]{1,0:T(8,128)S(1)}, f32[64,768]{1,0:T(8,128)S(1)}, u32[]{:S(2)}, u32[]{:S(2)}) %collective-permute-start.13) | collective-permute-done | bytes 196640 | tf_op jit(solution)/shard_map/ppermute | solution.py:459
  40.0 0.1 collective-permute-start.18
  40.0 2.7 %collective-permute-start.19 = (f32[64,768]{1,0:T(8,128)S(1)}, f32[64,768]{1,0:T(8,128)S(1)}, u32[]{:S(2)}, u32[]{:S(2)}) collective-permute-start(f32[64,768]{1,0:T(8,128)S(1)} %get-tuple-element.101), channel_id=1, source_target_pairs={{0,8},{8,0},{16,24},{24,16},{1,9},{9,1},{17,25},{25,17},{2,10},{10... | collective-permute-start | bytes 589832 | tf_op jit(solution)/shard_map/ppermute | solution.py:459
  42.8 0.1 finish.7
  42.9 0.9 %collective-permute-done.12.refs_1_ = f32[64,768]{1,0:T(8,128)S(1)} collective-permute-done((f32[64,768]{1,0:T(8,128)S(1)}, f32[64,768]{1,0:T(8,128)S(1)}, u32[]{:S(2)}, u32[]{:S(2)}) %collective-permute-start.12) | collective-permute-done | bytes 196640 | tf_op jit(solution)/shard_map/ppermute | solution.py:459
  43.8 0.1 collective-permute-start.17
  43.9 2.6 %collective-permute-start.25 = (f32[64,768]{1,0:T(8,128)S(1)}, f32[64,768]{1,0:T(8,128)S(1)}, u32[]{:S(2)}, u32[]{:S(2)}) collective-permute-start(f32[64,768]{1,0:T(8,128)S(1)} %get-tuple-element.108), channel_id=1, source_target_pairs={{0,8},{8,0},{16,24},{24,16},{1,9},{9,1},{17,25},{25,17},{2,10},{10... | collective-permute-start | bytes 589832 | tf_op jit(solution)/shard_map/ppermute | solution.py:459
  46.6 3.0 %collective-permute-start.26 = (f32[64,768]{1,0:T(8,128)S(1)}, f32[64,768]{1,0:T(8,128)S(1)}, u32[]{:S(2)}, u32[]{:S(2)}) collective-permute-start(f32[64,768]{1,0:T(8,128)S(1)} %get-tuple-element.112), channel_id=1, source_target_pairs={{0,8},{8,0},{16,24},{24,16},{1,9},{9,1},{17,25},{25,17},{2,10},{10... | collective-permute-start | bytes 589832 | tf_op jit(solution)/shard_map/ppermute | solution.py:459
  49.6 0.1 finish.8
  49.6 0.1 finish.9
  49.8 0.1 collective-permute-start.20
  49.9 2.6 %collective-permute-start.27 = (f32[64,768]{1,0:T(8,128)S(1)}, f32[64,768]{1,0:T(8,128)S(1)}, u32[]{:S(2)}, u32[]{:S(2)}) collective-permute-start(f32[64,768]{1,0:T(8,128)S(1)} %get-tuple-element.115), channel_id=1, source_target_pairs={{0,8},{8,0},{16,24},{24,16},{1,9},{9,1},{17,25},{25,17},{2,10},{10... | collective-permute-start | bytes 589832 | tf_op jit(solution)/shard_map/ppermute | solution.py:459
  52.4 1.1 %collective-permute-start.21 = (f32[8,128]{1,0:T(8,128)S(1)}, f32[8,128]{1,0:T(8,128)S(1)}, u32[]{:S(2)}, u32[]{:S(2)}) collective-permute-start(f32[8,128]{1,0:T(8,128)S(1)} %add.14), channel_id=1, source_target_pairs={{0,4},{2,6},{4,0},{6,2},{1,5},{3,7},{5,1},{7,3},{8,12},{10,14},{12... | collective-permute-start | bytes 12296 | tf_op jit(solution)/shard_map/ppermute | solution.py:375
  53.6 2.5 %collective-permute-done.21 = f32[8,128]{1,0:T(8,128)S(1)} collective-permute-done((f32[8,128]{1,0:T(8,128)S(1)}, f32[8,128]{1,0:T(8,128)S(1)}, u32[]{:S(2)}, u32[]{:S(2)}) %collective-permute-start.21) | collective-permute-done | bytes 4128 | tf_op jit(solution)/shard_map/ppermute | solution.py:375
  56.0 1.4 %collective-permute-start.22 = (f32[8,128]{1,0:T(8,128)S(1)}, f32[8,128]{1,0:T(8,128)S(1)}, u32[]{:S(2)}, u32[]{:S(2)}) collective-permute-start(f32[8,128]{1,0:T(8,128)S(1)} %add.15.refs_0_), channel_id=1, source_target_pairs={{0,9},{1,8},{8,1},{9,0},{16,25},{17,24},{24,17},{25,16},{2,11},{3,... | collective-permute-start | bytes 12296 | tf_op jit(solution)/shard_map/ppermute | solution.py:520
  57.4 0.9 %collective-permute-start.23 = (f32[8,128]{1,0:T(8,128)S(1)}, f32[8,128]{1,0:T(8,128)S(1)}, u32[]{:S(2)}, u32[]{:S(2)}) collective-permute-start(f32[8,128]{1,0:T(8,128)S(1)} %add.15.refs_0_), channel_id=1, source_target_pairs={{0,8},{8,0},{16,24},{24,16},{1,9},{9,1},{17,25},{25,17},{2,10},{10... | collective-permute-start | bytes 12296 | tf_op jit(solution)/shard_map/ppermute | solution.py:521
  58.3 1.2 %collective-permute-start.24 = (f32[8,128]{1,0:T(8,128)S(1)}, f32[8,128]{1,0:T(8,128)S(1)}, u32[]{:S(2)}, u32[]{:S(2)}) collective-permute-start(f32[8,128]{1,0:T(8,128)S(1)} %add.15.refs_0_), channel_id=1, source_target_pairs={{0,1},{1,0},{2,3},{3,2},{4,5},{5,4},{6,7},{7,6},{8,9},{9,8},{10,11... | collective-permute-start | bytes 12296 | tf_op jit(solution)/shard_map/ppermute | solution.py:522
  59.6 0.7 %collective-permute-done.27.refs_1_ = f32[64,768]{1,0:T(8,128)S(1)} collective-permute-done((f32[64,768]{1,0:T(8,128)S(1)}, f32[64,768]{1,0:T(8,128)S(1)}, u32[]{:S(2)}, u32[]{:S(2)}) %collective-permute-start.27) | collective-permute-done | bytes 196640 | tf_op jit(solution)/shard_map/ppermute | solution.py:459
  60.4 1.1 %collective-permute-done.22.refs_1_ = f32[8,128]{1,0:T(8,128)S(1)} collective-permute-done((f32[8,128]{1,0:T(8,128)S(1)}, f32[8,128]{1,0:T(8,128)S(1)}, u32[]{:S(2)}, u32[]{:S(2)}) %collective-permute-start.22) | collective-permute-done | bytes 4128 | tf_op jit(solution)/shard_map/ppermute | solution.py:520
  61.5 0.5 collective-permute-done.24.refs_3_
  61.9 1.9 %assemble.1 = (f32[384,1024]{1,0:T(8,128)}, f32[1,384,1024]{2,1,0:T(8,128)}) custom-call(f32[8,128]{1,0:T(8,128)S(1)} %add.15.refs_0_, f32[8,128]{1,0:T(8,128)S(1)} %collective-permute-done.22.refs_1_, f32[8,128]{1,0:T(8,128)S(1)} %collective-permute-done.23.refs_2_, f32[8,128]{1,0:T(8,128)S(1)} %collective-permute-done.24.refs_3_, ...), custom_call_target="tpu_custom_call" | custom-call | tf_op jit(solution)/shard_map/assemble/pallas_call | solution.py:116
  (40 shorter events, 0.9 us)
Async XLA Ops:
  4.2 3.2 %collective-permute-start = (f32[96,1024]{1,0:T(8,128)S(1)}, f32[96,1024]{1,0:T(8,128)S(1)}, u32[]{:S(2)}, u32[]{:S(2)}) collective-permute-start(f32[96,1024]{1,0:T(8,128)S(1)} %get-tuple-element.67), channel_id=1, source_target_pairs={{0,2},{2,0},{4,6},{6,4},{1,3},{3,1},{5,7},{7,5},{8,10},{10,8},{12,... | collective-permute-start | bytes 1179656 | tf_op jit(solution)/shard_map/ppermute | solution.py:486
  4.7 8.4 %collective-permute-start.3 = (f32[64,768]{1,0:T(8,128)S(1)}, f32[64,768]{1,0:T(8,128)S(1)}, u32[]{:S(2)}, u32[]{:S(2)}) collective-permute-start(f32[64,768]{1,0:T(8,128)S(1)} %get-tuple-element.71.refs_0_), channel_id=1, source_target_pairs={{0,8},{8,0},{16,24},{24,16},{1,9},{9,1},{17,25},{25,17},{2,10},{10... | collective-permute-start | bytes 589832 | tf_op jit(solution)/shard_map/ppermute | solution.py:459
  9.7 7.5 %collective-permute-start.2 = (f32[64,768]{1,0:T(8,128)S(1)}, f32[64,768]{1,0:T(8,128)S(1)}, u32[]{:S(2)}, u32[]{:S(2)}) collective-permute-start(f32[64,768]{1,0:T(8,128)S(1)} %get-tuple-element.70.refs_2_.refs_0_), channel_id=1, source_target_pairs={{0,8},{8,0},{16,24},{24,16},{1,9},{9,1},{17,25},{25,17},{2,10},{10... | collective-permute-start | bytes 589832 | tf_op jit(solution)/shard_map/ppermute | solution.py:459
  11.4 7.8 %collective-permute-start.1 = (f32[96,1024]{1,0:T(8,128)S(1)}, f32[96,1024]{1,0:T(8,128)S(1)}, u32[]{:S(2)}, u32[]{:S(2)}) collective-permute-start(f32[96,1024]{1,0:T(8,128)S(1)} %get-tuple-element.69), channel_id=1, source_target_pairs={{0,1},{1,0},{2,4},{3,5},{4,2},{5,3},{6,7},{7,6},{8,9},{9,8},{10,12... | collective-permute-start | bytes 1179656 | tf_op jit(solution)/shard_map/ppermute | solution.py:491
  13.2 10.1 %collective-permute-start.7 = (f32[64,768]{1,0:T(8,128)S(1)}, f32[64,768]{1,0:T(8,128)S(1)}, u32[]{:S(2)}, u32[]{:S(2)}) collective-permute-start(f32[64,768]{1,0:T(8,128)S(1)} %add.16.refs_2_.refs_0_), channel_id=1, source_target_pairs={{8,16},{16,8},{0,2},{24,26},{10,18},{18,10},{2,0},{26,24},{12,20},... | collective-permute-start | bytes 589832 | tf_op jit(solution)/shard_map/ppermute | solution.py:464
  13.2 10.1 %collective-permute-start.8 = (f32[64,768]{1,0:T(8,128)S(1)}, f32[64,768]{1,0:T(8,128)S(1)}, u32[]{:S(2)}, u32[]{:S(2)}) collective-permute-start(f32[64,768]{1,0:T(8,128)S(1)} %get-tuple-element.76.refs_0_), channel_id=1, source_target_pairs={{0,8},{8,0},{16,24},{24,16},{1,9},{9,1},{17,25},{25,17},{2,10},{10... | collective-permute-start | bytes 589832 | tf_op jit(solution)/shard_map/ppermute | solution.py:459
  16.7 10.0 %collective-permute-start.5 = (f32[64,768]{1,0:T(8,128)S(1)}, f32[64,768]{1,0:T(8,128)S(1)}, u32[]{:S(2)}, u32[]{:S(2)}) collective-permute-start(f32[64,768]{1,0:T(8,128)S(1)} %get-tuple-element.72.refs_0_), channel_id=1, source_target_pairs={{0,8},{8,0},{16,24},{24,16},{1,9},{9,1},{17,25},{25,17},{2,10},{10... | collective-permute-start | bytes 589832 | tf_op jit(solution)/shard_map/ppermute | solution.py:459
  17.3 9.3 %collective-permute-start.6 = (f32[64,768]{1,0:T(8,128)S(1)}, f32[64,768]{1,0:T(8,128)S(1)}, u32[]{:S(2)}, u32[]{:S(2)}) collective-permute-start(f32[64,768]{1,0:T(8,128)S(1)} %add.17.refs_4_.refs_0_), channel_id=1, source_target_pairs={{8,16},{16,8},{0,2},{24,26},{10,18},{18,10},{2,0},{26,24},{12,20},... | collective-permute-start | bytes 589832 | tf_op jit(solution)/shard_map/ppermute | solution.py:464
  19.4 9.7 %collective-permute-start.4 = (f32[512,128]{1,0:T(8,128)S(1)}, f32[512,128]{1,0:T(8,128)S(1)}, u32[]{:S(2)}, u32[]{:S(2)}) collective-permute-start(f32[512,128]{1,0:T(8,128)S(1)} %side_pack.1.refs_7_), channel_id=1, source_target_pairs={{0,1},{1,0},{2,3},{3,2},{4,5},{5,4},{6,7},{7,6},{8,9},{9,8},{10,11... | collective-permute-start | bytes 786440 | tf_op jit(solution)/shard_map/ppermute | solution.py:497
  23.3 8.3 %collective-permute-start.10 = (f32[64,768]{1,0:T(8,128)S(1)}, f32[64,768]{1,0:T(8,128)S(1)}, u32[]{:S(2)}, u32[]{:S(2)}) collective-permute-start(f32[64,768]{1,0:T(8,128)S(1)} %add.18.refs_4_.refs_0_), channel_id=1, source_target_pairs={{8,16},{16,8},{0,2},{24,26},{10,18},{18,10},{2,0},{26,24},{12,20},... | collective-permute-start | bytes 589832 | tf_op jit(solution)/shard_map/ppermute | solution.py:464
  23.4 8.3 %collective-permute-start.11 = (f32[64,768]{1,0:T(8,128)S(1)}, f32[64,768]{1,0:T(8,128)S(1)}, u32[]{:S(2)}, u32[]{:S(2)}) collective-permute-start(f32[64,768]{1,0:T(8,128)S(1)} %get-tuple-element.83), channel_id=1, source_target_pairs={{0,8},{8,0},{16,24},{24,16},{1,9},{9,1},{17,25},{25,17},{2,10},{10... | collective-permute-start | bytes 589832 | tf_op jit(solution)/shard_map/ppermute | solution.py:459
  26.7 7.6 %collective-permute-start.9 = (f32[64,768]{1,0:T(8,128)S(1)}, f32[64,768]{1,0:T(8,128)S(1)}, u32[]{:S(2)}, u32[]{:S(2)}) collective-permute-start(f32[64,768]{1,0:T(8,128)S(1)} %add.19.refs_8_.refs_0_), channel_id=1, source_target_pairs={{8,16},{16,8},{0,2},{24,26},{10,18},{18,10},{2,0},{26,24},{12,20},... | collective-permute-start | bytes 589832 | tf_op jit(solution)/shard_map/ppermute | solution.py:464
  26.7 8.2 %collective-permute-start.14 = (f32[64,768]{1,0:T(8,128)S(1)}, f32[64,768]{1,0:T(8,128)S(1)}, u32[]{:S(2)}, u32[]{:S(2)}) collective-permute-start(f32[64,768]{1,0:T(8,128)S(1)} %get-tuple-element.88), channel_id=1, source_target_pairs={{0,8},{8,0},{16,24},{24,16},{1,9},{9,1},{17,25},{25,17},{2,10},{10... | collective-permute-start | bytes 589832 | tf_op jit(solution)/shard_map/ppermute | solution.py:459
  31.8 6.5 %collective-permute-start.16 = (f32[64,768]{1,0:T(8,128)S(1)}, f32[64,768]{1,0:T(8,128)S(1)}, u32[]{:S(2)}, u32[]{:S(2)}) collective-permute-start(f32[64,768]{1,0:T(8,128)S(1)} %add.20.refs_4_.refs_0_), channel_id=1, source_target_pairs={{8,16},{16,8},{0,2},{24,26},{10,18},{18,10},{2,0},{26,24},{12,20},... | collective-permute-start | bytes 589832 | tf_op jit(solution)/shard_map/ppermute | solution.py:464
  31.9 8.1 %collective-permute-start.13 = (f32[64,768]{1,0:T(8,128)S(1)}, f32[64,768]{1,0:T(8,128)S(1)}, u32[]{:S(2)}, u32[]{:S(2)}) collective-permute-start(f32[64,768]{1,0:T(8,128)S(1)} %get-tuple-element.86), channel_id=1, source_target_pairs={{0,8},{8,0},{16,24},{24,16},{1,9},{9,1},{17,25},{25,17},{2,10},{10... | collective-permute-start | bytes 589832 | tf_op jit(solution)/shard_map/ppermute | solution.py:459
  35.0 7.8 %collective-permute-start.15 = (f32[64,768]{1,0:T(8,128)S(1)}, f32[64,768]{1,0:T(8,128)S(1)}, u32[]{:S(2)}, u32[]{:S(2)}) collective-permute-start(f32[64,768]{1,0:T(8,128)S(1)} %add.21.refs_4_.refs_0_), channel_id=1, source_target_pairs={{8,16},{16,8},{0,2},{24,26},{10,18},{18,10},{2,0},{26,24},{12,20},... | collective-permute-start | bytes 589832 | tf_op jit(solution)/shard_map/ppermute | solution.py:464
  35.1 8.7 %collective-permute-start.12 = (f32[64,768]{1,0:T(8,128)S(1)}, f32[64,768]{1,0:T(8,128)S(1)}, u32[]{:S(2)}, u32[]{:S(2)}) collective-permute-start(f32[64,768]{1,0:T(8,128)S(1)} %get-tuple-element.85), channel_id=1, source_target_pairs={{0,8},{8,0},{16,24},{24,16},{1,9},{9,1},{17,25},{25,17},{2,10},{10... | collective-permute-start | bytes 589832 | tf_op jit(solution)/shard_map/ppermute | solution.py:459
  40.0 6.6 %collective-permute-start.18 = (f32[64,768]{1,0:T(8,128)S(1)}, f32[64,768]{1,0:T(8,128)S(1)}, u32[]{:S(2)}, u32[]{:S(2)}) collective-permute-start(f32[64,768]{1,0:T(8,128)S(1)} %add.22.refs_4_.refs_0_), channel_id=1, source_target_pairs={{8,16},{16,8},{0,2},{24,26},{10,18},{18,10},{2,0},{26,24},{12,20},... | collective-permute-start | bytes 589832 | tf_op jit(solution)/shard_map/ppermute | solution.py:464
  40.0 9.6 %collective-permute-start.19 = (f32[64,768]{1,0:T(8,128)S(1)}, f32[64,768]{1,0:T(8,128)S(1)}, u32[]{:S(2)}, u32[]{:S(2)}) collective-permute-start(f32[64,768]{1,0:T(8,128)S(1)} %get-tuple-element.101), channel_id=1, source_target_pairs={{0,8},{8,0},{16,24},{24,16},{1,9},{9,1},{17,25},{25,17},{2,10},{10... | collective-permute-start | bytes 589832 | tf_op jit(solution)/shard_map/ppermute | solution.py:459
  43.8 5.9 %collective-permute-start.17 = (f32[64,768]{1,0:T(8,128)S(1)}, f32[64,768]{1,0:T(8,128)S(1)}, u32[]{:S(2)}, u32[]{:S(2)}) collective-permute-start(f32[64,768]{1,0:T(8,128)S(1)} %add.23.refs_4_.refs_0_), channel_id=1, source_target_pairs={{8,16},{16,8},{0,2},{24,26},{10,18},{18,10},{2,0},{26,24},{12,20},... | collective-permute-start | bytes 589832 | tf_op jit(solution)/shard_map/ppermute | solution.py:464
  43.9 9.6 %collective-permute-start.25 = (f32[64,768]{1,0:T(8,128)S(1)}, f32[64,768]{1,0:T(8,128)S(1)}, u32[]{:S(2)}, u32[]{:S(2)}) collective-permute-start(f32[64,768]{1,0:T(8,128)S(1)} %get-tuple-element.108), channel_id=1, source_target_pairs={{0,8},{8,0},{16,24},{24,16},{1,9},{9,1},{17,25},{25,17},{2,10},{10... | collective-permute-start | bytes 589832 | tf_op jit(solution)/shard_map/ppermute | solution.py:459
  46.6 12.9 %collective-permute-start.26 = (f32[64,768]{1,0:T(8,128)S(1)}, f32[64,768]{1,0:T(8,128)S(1)}, u32[]{:S(2)}, u32[]{:S(2)}) collective-permute-start(f32[64,768]{1,0:T(8,128)S(1)} %get-tuple-element.112), channel_id=1, source_target_pairs={{0,8},{8,0},{16,24},{24,16},{1,9},{9,1},{17,25},{25,17},{2,10},{10... | collective-permute-start | bytes 589832 | tf_op jit(solution)/shard_map/ppermute | solution.py:459
  49.8 2.6 %collective-permute-start.20 = (f32[8,128]{1,0:T(8,128)S(1)}, f32[8,128]{1,0:T(8,128)S(1)}, u32[]{:S(2)}, u32[]{:S(2)}) collective-permute-start(f32[8,128]{1,0:T(8,128)S(1)} %get-tuple-element.107), channel_id=1, source_target_pairs={{0,2},{2,0},{4,6},{6,4},{1,3},{3,1},{5,7},{7,5},{8,10},{10,8},{12,... | collective-permute-start | bytes 12296 | tf_op jit(solution)/shard_map/ppermute | solution.py:375
  49.9 10.5 %collective-permute-start.27 = (f32[64,768]{1,0:T(8,128)S(1)}, f32[64,768]{1,0:T(8,128)S(1)}, u32[]{:S(2)}, u32[]{:S(2)}) collective-permute-start(f32[64,768]{1,0:T(8,128)S(1)} %get-tuple-element.115), channel_id=1, source_target_pairs={{0,8},{8,0},{16,24},{24,16},{1,9},{9,1},{17,25},{25,17},{2,10},{10... | collective-permute-start | bytes 589832 | tf_op jit(solution)/shard_map/ppermute | solution.py:459
  52.4 3.6 %collective-permute-start.21 = (f32[8,128]{1,0:T(8,128)S(1)}, f32[8,128]{1,0:T(8,128)S(1)}, u32[]{:S(2)}, u32[]{:S(2)}) collective-permute-start(f32[8,128]{1,0:T(8,128)S(1)} %add.14), channel_id=1, source_target_pairs={{0,4},{2,6},{4,0},{6,2},{1,5},{3,7},{5,1},{7,3},{8,12},{10,14},{12... | collective-permute-start | bytes 12296 | tf_op jit(solution)/shard_map/ppermute | solution.py:375
  56.0 5.4 %collective-permute-start.22 = (f32[8,128]{1,0:T(8,128)S(1)}, f32[8,128]{1,0:T(8,128)S(1)}, u32[]{:S(2)}, u32[]{:S(2)}) collective-permute-start(f32[8,128]{1,0:T(8,128)S(1)} %add.15.refs_0_), channel_id=1, source_target_pairs={{0,9},{1,8},{8,1},{9,0},{16,25},{17,24},{24,17},{25,16},{2,11},{3,... | collective-permute-start | bytes 12296 | tf_op jit(solution)/shard_map/ppermute | solution.py:520
  57.4 4.1 %collective-permute-start.23 = (f32[8,128]{1,0:T(8,128)S(1)}, f32[8,128]{1,0:T(8,128)S(1)}, u32[]{:S(2)}, u32[]{:S(2)}) collective-permute-start(f32[8,128]{1,0:T(8,128)S(1)} %add.15.refs_0_), channel_id=1, source_target_pairs={{0,8},{8,0},{16,24},{24,16},{1,9},{9,1},{17,25},{25,17},{2,10},{10... | collective-permute-start | bytes 12296 | tf_op jit(solution)/shard_map/ppermute | solution.py:521
  58.3 3.6 %collective-permute-start.24 = (f32[8,128]{1,0:T(8,128)S(1)}, f32[8,128]{1,0:T(8,128)S(1)}, u32[]{:S(2)}, u32[]{:S(2)}) collective-permute-start(f32[8,128]{1,0:T(8,128)S(1)} %add.15.refs_0_), channel_id=1, source_target_pairs={{0,1},{1,0},{2,3},{3,2},{4,5},{5,4},{6,7},{7,6},{8,9},{9,8},{10,11... | collective-permute-start | bytes 12296 | tf_op jit(solution)/shard_map/ppermute | solution.py:522

commit v5 on v4

--- a/solution.py
+++ b/solution.py
@@ -513,13 +513,14 @@
     close(n - LAG)
     total(n - 1)
     if maps == 4 and gx == 4 and gy == 2:
-        own = sum_grid(mass[0], ("gx",))
-        swap = [(i * gy + j, (i ^ 1) * gy + 1 - j) for i in range(4) for j in range(gy)]
+        own = mass[0] + lax.ppermute(mass[0], "gy", [(0, 1), (1, 0)])
+        own = own + lax.ppermute(own, "gx", near)
+        swap = [(i * gx + j, (i ^ 1) * gx + (j ^ 2)) for i in range(4) for j in range(gx)]
         masses = [
             own,
-            lax.ppermute(own, ("map", "gy"), swap),
+            lax.ppermute(own, ("map", "gx"), swap),
             lax.ppermute(own, "map", outer),
-            lax.ppermute(own, "gy", [(0, 1), (1, 0)]),
+            lax.ppermute(own, "gx", [(i, i ^ 2) for i in range(gx)]),
         ]
         for k in range(n - 3, n):
             close(k, "finish_last")

time: 64.1 us -> 63.6 us (level)
  waiting for transfers between devices: 10.4 us -> 9.69 us
    ppermute x4, waiting for transfers between devices: 4 us -> 2.4 us  [the longest x1 1.08 us: local(): own = own + lax.ppermute(own, 'gx', near)]
    ppermute x4, starting transfers between devices: 3.68 us -> 4.81 us  [the longest x1 2.98 us: local(): lax.ppermute(own, ('map', 'gx'), swap)]
    ppermute x1, starting transfers between devices: 0.94 us -> 0.01 us  [local(): lax.ppermute(own, 'map', outer)]
    ppermute x12, waiting for transfers between devices: 4.43 us -> 5.37 us  [outward(): got[k] = lax.ppermute(value, 'map', outer)]
where the time goes in v5:
time: 63.6 us; the launch traced here: 63.4 us
  starting transfers between devices  38.8 us (61%)
  Pallas kernels  13.4 us (21%)
  waiting for transfers between devices  9.69 us (15%)
  between operations  1.56 us (2%)
    ppermute x12, starting transfers between devices, outward(): got[k] = lax.ppermute(value, 'map', outer)  29.8 us
    pallas_call x30, Pallas kernels, call(): return lambda *args: kernel(*args, *deps)  13.4 us
    ppermute x12, waiting for transfers between devices, outward(): got[k] = lax.ppermute(value, 'map', outer)  5.37 us
    ppermute x1, starting transfers between devices, local(): lax.ppermute(own, ('map', 'gx'), swap)  2.98 us
    ppermute x1, waiting for transfers between devices, local(): two = lax.ppermute(two, ('gx', 'gy'), far)  1.89 us
    ppermute x1, starting transfers between devices, local(): from_left = from_right = lax.ppermute(packs[0], 'gy', [(0, 1), (1, 0)])  1.58 us
    ppermute x1, starting transfers between devices, local(): two = lax.ppermute(two, ('gx', 'gy'), far)  1.52 us
  transfers between devices with their start and end apart: 28, of which 10 were waited for; matrix products, arithmetic and copies ran while one was open for 0% of the time, Pallas kernels for 13%

profile of v5, /device:TPU:0, one launch (start us, length us, event | category | flops | bytes accessed | tf_op | source)
XLA Modules:
  0.0 63.4 jit_solution(10779196714016246196)
XLA Ops:
  1.3 2.9 %first.1 = (f32[64,768]{1,0:T(8,128)S(1)}, f32[64,768]{1,0:T(8,128)S(1)}, bf16[2,192,256]{2,1,0:T(8,128)(2,1)S(1)}, bf16[2,512,256]{2,1,0:T(8,128)(2,1)S(1)}, f3...) custom-call(f32[1]{0:T(128)S(6)} %copy.5.refs_0_, f32[1,384,1024]{2,1,0:T(8,128)} %refs_1_.1, ...), custom_call_target="tpu_custom_call" | custom-call | tf_op jit(solution)/shard_map/first/pallas_call | solution.py:116
  4.2 0.5 collective-permute-start
  4.7 2.6 %collective-permute-start.3 = (f32[64,768]{1,0:T(8,128)S(1)}, f32[64,768]{1,0:T(8,128)S(1)}, u32[]{:S(2)}, u32[]{:S(2)}) collective-permute-start(f32[64,768]{1,0:T(8,128)S(1)} %get-tuple-element.71.refs_0_), channel_id=1, source_target_pairs={{0,8},{8,0},{16,24},{24,16},{1,9},{9,1},{17,25},{25,17},{2,10},{10... | collective-permute-start | bytes 589832 | tf_op jit(solution)/shard_map/ppermute | solution.py:459
  7.4 2.4 %inner.1 = (f32[64,768]{1,0:T(8,128)S(1)}, f32[64,768]{1,0:T(8,128)S(1)}, f32[64,768]{1,0:T(8,128)S(1)}, f32[64,768]{1,0:T(8,128)S(1)}, f32[64,768]{1,0:T(8,128)...) custom-call(f32[1]{0:T(128)S(6)} %copy.5.refs_0_, f32[1,384,1024]{2,1,0:T(8,128)S(1)} %get-tuple-element.64.refs_1_.refs_0_, ...), custom_call_target="tpu_custom_call" | custom-call | flops 2500000000 | tf_op jit(solution)/shard_map/inner/pallas_call | solution.py:116
  9.7 1.7 %collective-permute-start.2 = (f32[64,768]{1,0:T(8,128)S(1)}, f32[64,768]{1,0:T(8,128)S(1)}, u32[]{:S(2)}, u32[]{:S(2)}) collective-permute-start(f32[64,768]{1,0:T(8,128)S(1)} %get-tuple-element.70.refs_2_.refs_0_), channel_id=1, source_target_pairs={{0,8},{8,0},{16,24},{24,16},{1,9},{9,1},{17,25},{25,17},{2,10},{10... | collective-permute-start | bytes 589832 | tf_op jit(solution)/shard_map/ppermute | solution.py:459
  11.4 1.5 %collective-permute-start.1 = (f32[96,1024]{1,0:T(8,128)S(1)}, f32[96,1024]{1,0:T(8,128)S(1)}, u32[]{:S(2)}, u32[]{:S(2)}) collective-permute-start(f32[96,1024]{1,0:T(8,128)S(1)} %get-tuple-element.69), channel_id=1, source_target_pairs={{0,1},{1,0},{2,4},{3,5},{4,2},{5,3},{6,7},{7,6},{8,9},{9,8},{10,12... | collective-permute-start | bytes 1179656 | tf_op jit(solution)/shard_map/ppermute | solution.py:491
  13.0 0.2 collective-permute-done.3.refs_1_
  13.2 0.1 collective-permute-start.7
  13.2 3.4 %collective-permute-start.8 = (f32[64,768]{1,0:T(8,128)S(1)}, f32[64,768]{1,0:T(8,128)S(1)}, u32[]{:S(2)}, u32[]{:S(2)}) collective-permute-start(f32[64,768]{1,0:T(8,128)S(1)} %get-tuple-element.76.refs_0_), channel_id=1, source_target_pairs={{0,8},{8,0},{16,24},{24,16},{1,9},{9,1},{17,25},{25,17},{2,10},{10... | collective-permute-start | bytes 589832 | tf_op jit(solution)/shard_map/ppermute | solution.py:459
  16.7 0.5 collective-permute-done.2.refs_1_
  17.3 0.1 collective-permute-start.6
  17.3 1.9 %collective-permute-done.1.refs_3_.refs_6_.refs_5_ = f32[96,1024]{1,0:T(8,128)S(1)} collective-permute-done((f32[96,1024]{1,0:T(8,128)S(1)}, f32[96,1024]{1,0:T(8,128)S(1)}, u32[]{:S(2)}, u32[]{:S(2)}) %collective-permute-start.1) | collective-permute-done | bytes 393248 | tf_op jit(solution)/shard_map/ppermute | solution.py:491
  19.2 0.2 side_pack.1.refs_7_
  19.4 1.6 %collective-permute-start.4 = (f32[512,128]{1,0:T(8,128)S(1)}, f32[512,128]{1,0:T(8,128)S(1)}, u32[]{:S(2)}, u32[]{:S(2)}) collective-permute-start(f32[512,128]{1,0:T(8,128)S(1)} %side_pack.1.refs_7_), channel_id=1, source_target_pairs={{0,1},{1,0},{2,3},{3,2},{4,5},{5,4},{6,7},{7,6},{8,9},{9,8},{10,11... | collective-permute-start | bytes 786440 | tf_op jit(solution)/shard_map/ppermute | solution.py:497
  21.0 2.2 %edges.1 = (f32[64,768]{1,0:T(8,128)S(1)}, f32[64,768]{1,0:T(8,128)S(1)}, f32[64,768]{1,0:T(8,128)S(1)}, f32[64,768]{1,0:T(8,128)S(1)}) custom-call(f32[1]{0:T(128)S(6)} %copy.5.refs_0_, f32[1,384,1024]{2,1,0:T(8,128)S(1)} %get-tuple-element.64.refs_1_.refs_0_, f32[1,384,1024]{2,1,0:T(8,128)S(1)} %get-tuple-element.65.refs_2_.refs_1_, ...), custom_call_target="tpu_custom_call" | custom-call | flops 2300000000 | tf_op jit(solution)/shard_map/edges/pallas_call | solution.py:116
  23.3 0.1 collective-permute-start.10
  23.4 3.1 %collective-permute-start.11 = (f32[64,768]{1,0:T(8,128)S(1)}, f32[64,768]{1,0:T(8,128)S(1)}, u32[]{:S(2)}, u32[]{:S(2)}) collective-permute-start(f32[64,768]{1,0:T(8,128)S(1)} %get-tuple-element.83), channel_id=1, source_target_pairs={{0,8},{8,0},{16,24},{24,16},{1,9},{9,1},{17,25},{25,17},{2,10},{10... | collective-permute-start | bytes 589832 | tf_op jit(solution)/shard_map/ppermute | solution.py:459
  26.7 0.1 collective-permute-start.9
  26.7 2.4 %collective-permute-start.14 = (f32[64,768]{1,0:T(8,128)S(1)}, f32[64,768]{1,0:T(8,128)S(1)}, u32[]{:S(2)}, u32[]{:S(2)}) collective-permute-start(f32[64,768]{1,0:T(8,128)S(1)} %get-tuple-element.88), channel_id=1, source_target_pairs={{0,8},{8,0},{16,24},{24,16},{1,9},{9,1},{17,25},{25,17},{2,10},{10... | collective-permute-start | bytes 589832 | tf_op jit(solution)/shard_map/ppermute | solution.py:459
  29.2 2.5 %sides.1 = (f32[64,768]{1,0:T(8,128)S(1)}, f32[64,768]{1,0:T(8,128)S(1)}, f32[64,768]{1,0:T(8,128)S(1)}, f32[64,768]{1,0:T(8,128)S(1)}) custom-call(f32[1]{0:T(128)S(6)} %copy.5.refs_0_, f32[1,384,1024]{2,1,0:T(8,128)S(1)} %get-tuple-element.64.refs_1_.refs_0_, f32[1,384,1024]{2,1,0:T(8,128)S(1)} %get-tuple-element.65.refs_2_.refs_1_, ...), custom_call_target="tpu_custom_call" | custom-call | flops 2500000000 | tf_op jit(solution)/shard_map/sides/pallas_call | solution.py:116
  31.8 0.1 collective-permute-start.16
  31.9 2.4 %collective-permute-start.13 = (f32[64,768]{1,0:T(8,128)S(1)}, f32[64,768]{1,0:T(8,128)S(1)}, u32[]{:S(2)}, u32[]{:S(2)}) collective-permute-start(f32[64,768]{1,0:T(8,128)S(1)} %get-tuple-element.86), channel_id=1, source_target_pairs={{0,8},{8,0},{16,24},{24,16},{1,9},{9,1},{17,25},{25,17},{2,10},{10... | collective-permute-start | bytes 589832 | tf_op jit(solution)/shard_map/ppermute | solution.py:459
  34.3 0.1 finish.5
  34.4 0.6 collective-permute-done.14.refs_1_
  35.0 0.1 collective-permute-start.15
  35.1 3.2 %collective-permute-start.12 = (f32[64,768]{1,0:T(8,128)S(1)}, f32[64,768]{1,0:T(8,128)S(1)}, u32[]{:S(2)}, u32[]{:S(2)}) collective-permute-start(f32[64,768]{1,0:T(8,128)S(1)} %get-tuple-element.85), channel_id=1, source_target_pairs={{0,8},{8,0},{16,24},{24,16},{1,9},{9,1},{17,25},{25,17},{2,10},{10... | collective-permute-start | bytes 589832 | tf_op jit(solution)/shard_map/ppermute | solution.py:459
  38.3 0.1 finish.6
  38.4 1.5 %collective-permute-done.13.refs_1_ = f32[64,768]{1,0:T(8,128)S(1)} collective-permute-done((f32[64,768]{1,0:T(8,128)S(1)}, f32[64,768]{1,0:T(8,128)S(1)}, u32[]{:S(2)}, u32[]{:S(2)}) %collective-permute-start.13) | collective-permute-done | bytes 196640 | tf_op jit(solution)/shard_map/ppermute | solution.py:459
  40.0 0.1 collective-permute-start.18
  40.0 2.7 %collective-permute-start.19 = (f32[64,768]{1,0:T(8,128)S(1)}, f32[64,768]{1,0:T(8,128)S(1)}, u32[]{:S(2)}, u32[]{:S(2)}) collective-permute-start(f32[64,768]{1,0:T(8,128)S(1)} %get-tuple-element.101), channel_id=1, source_target_pairs={{0,8},{8,0},{16,24},{24,16},{1,9},{9,1},{17,25},{25,17},{2,10},{10... | collective-permute-start | bytes 589832 | tf_op jit(solution)/shard_map/ppermute | solution.py:459
  42.8 0.1 finish.7
  42.9 0.9 %collective-permute-done.12.refs_1_ = f32[64,768]{1,0:T(8,128)S(1)} collective-permute-done((f32[64,768]{1,0:T(8,128)S(1)}, f32[64,768]{1,0:T(8,128)S(1)}, u32[]{:S(2)}, u32[]{:S(2)}) %collective-permute-start.12) | collective-permute-done | bytes 196640 | tf_op jit(solution)/shard_map/ppermute | solution.py:459
  43.8 0.1 collective-permute-start.17
  43.9 2.6 %collective-permute-start.25 = (f32[64,768]{1,0:T(8,128)S(1)}, f32[64,768]{1,0:T(8,128)S(1)}, u32[]{:S(2)}, u32[]{:S(2)}) collective-permute-start(f32[64,768]{1,0:T(8,128)S(1)} %get-tuple-element.108), channel_id=1, source_target_pairs={{0,8},{8,0},{16,24},{24,16},{1,9},{9,1},{17,25},{25,17},{2,10},{10... | collective-permute-start | bytes 589832 | tf_op jit(solution)/shard_map/ppermute | solution.py:459
  46.6 3.0 %collective-permute-start.26 = (f32[64,768]{1,0:T(8,128)S(1)}, f32[64,768]{1,0:T(8,128)S(1)}, u32[]{:S(2)}, u32[]{:S(2)}) collective-permute-start(f32[64,768]{1,0:T(8,128)S(1)} %get-tuple-element.112), channel_id=1, source_target_pairs={{0,8},{8,0},{16,24},{24,16},{1,9},{9,1},{17,25},{25,17},{2,10},{10... | collective-permute-start | bytes 589832 | tf_op jit(solution)/shard_map/ppermute | solution.py:459
  49.6 0.1 finish.8
  49.6 0.1 finish.9
  49.8 0.9 %collective-permute-start.20 = (f32[8,128]{1,0:T(8,128)S(1)}, f32[8,128]{1,0:T(8,128)S(1)}, u32[]{:S(2)}, u32[]{:S(2)}) collective-permute-start(f32[8,128]{1,0:T(8,128)S(1)} %get-tuple-element.107), channel_id=1, source_target_pairs={{0,1},{1,0},{2,3},{3,2},{4,5},{5,4},{6,7},{7,6},{8,9},{9,8},{10,11... | collective-permute-start | bytes 12296 | tf_op jit(solution)/shard_map/ppermute | solution.py:516
  50.6 2.5 %collective-permute-start.27 = (f32[64,768]{1,0:T(8,128)S(1)}, f32[64,768]{1,0:T(8,128)S(1)}, u32[]{:S(2)}, u32[]{:S(2)}) collective-permute-start(f32[64,768]{1,0:T(8,128)S(1)} %get-tuple-element.115), channel_id=1, source_target_pairs={{0,8},{8,0},{16,24},{24,16},{1,9},{9,1},{17,25},{25,17},{2,10},{10... | collective-permute-start | bytes 589832 | tf_op jit(solution)/shard_map/ppermute | solution.py:459
  53.2 0.3 collective-permute-done.20
  53.5 0.1 finish_last.3
  53.6 1.1 %collective-permute-done.21 = f32[8,128]{1,0:T(8,128)S(1)} collective-permute-done((f32[8,128]{1,0:T(8,128)S(1)}, f32[8,128]{1,0:T(8,128)S(1)}, u32[]{:S(2)}, u32[]{:S(2)}) %collective-permute-start.21) | collective-permute-done | bytes 4128 | tf_op jit(solution)/shard_map/ppermute | solution.py:517
  54.6 3.0 %collective-permute-start.22 = (f32[8,128]{1,0:T(8,128)S(1)}, f32[8,128]{1,0:T(8,128)S(1)}, u32[]{:S(2)}, u32[]{:S(2)}) collective-permute-start(f32[8,128]{1,0:T(8,128)S(1)} %add.15.refs_0_), channel_id=1, source_target_pairs={{0,12},{2,14},{4,8},{6,10},{8,4},{10,6},{12,0},{14,2},{16,28},{18,... | collective-permute-start | bytes 12296 | tf_op jit(solution)/shard_map/ppermute | solution.py:521
  57.6 1.0 %collective-permute-start.24 = (f32[8,128]{1,0:T(8,128)S(1)}, f32[8,128]{1,0:T(8,128)S(1)}, u32[]{:S(2)}, u32[]{:S(2)}) collective-permute-start(f32[8,128]{1,0:T(8,128)S(1)} %add.15.refs_0_), channel_id=1, source_target_pairs={{0,4},{2,6},{4,0},{6,2},{1,5},{3,7},{5,1},{7,3},{8,12},{10,14},{12... | collective-permute-start | bytes 12296 | tf_op jit(solution)/shard_map/ppermute | solution.py:523
  58.7 1.7 %collective-permute-done.27.refs_1_ = f32[64,768]{1,0:T(8,128)S(1)} collective-permute-done((f32[64,768]{1,0:T(8,128)S(1)}, f32[64,768]{1,0:T(8,128)S(1)}, u32[]{:S(2)}, u32[]{:S(2)}) %collective-permute-start.27) | collective-permute-done | bytes 196640 | tf_op jit(solution)/shard_map/ppermute | solution.py:459
  60.3 0.1 finish_last.5
  60.4 1.0 %collective-permute-done.22.refs_1_ = f32[8,128]{1,0:T(8,128)S(1)} collective-permute-done((f32[8,128]{1,0:T(8,128)S(1)}, f32[8,128]{1,0:T(8,128)S(1)}, u32[]{:S(2)}, u32[]{:S(2)}) %collective-permute-start.22) | collective-permute-done | bytes 4128 | tf_op jit(solution)/shard_map/ppermute | solution.py:521
  61.5 2.0 %assemble.1 = (f32[384,1024]{1,0:T(8,128)}, f32[1,384,1024]{2,1,0:T(8,128)}) custom-call(f32[8,128]{1,0:T(8,128)S(1)} %add.15.refs_0_, f32[8,128]{1,0:T(8,128)S(1)} %collective-permute-done.22.refs_1_, f32[8,128]{1,0:T(8,128)S(1)} %collective-permute-done.23.refs_2_, f32[8,128]{1,0:T(8,128)S(1)} %collective-permute-done.24.refs_3_, ...), custom_call_target="tpu_custom_call" | custom-call | tf_op jit(solution)/shard_map/assemble/pallas_call | solution.py:116
  (40 shorter events, 0.8 us)
Async XLA Ops:
  4.2 3.2 %collective-permute-start = (f32[96,1024]{1,0:T(8,128)S(1)}, f32[96,1024]{1,0:T(8,128)S(1)}, u32[]{:S(2)}, u32[]{:S(2)}) collective-permute-start(f32[96,1024]{1,0:T(8,128)S(1)} %get-tuple-element.67), channel_id=1, source_target_pairs={{0,2},{2,0},{4,6},{6,4},{1,3},{3,1},{5,7},{7,5},{8,10},{10,8},{12,... | collective-permute-start | bytes 1179656 | tf_op jit(solution)/shard_map/ppermute | solution.py:486
  4.7 8.4 %collective-permute-start.3 = (f32[64,768]{1,0:T(8,128)S(1)}, f32[64,768]{1,0:T(8,128)S(1)}, u32[]{:S(2)}, u32[]{:S(2)}) collective-permute-start(f32[64,768]{1,0:T(8,128)S(1)} %get-tuple-element.71.refs_0_), channel_id=1, source_target_pairs={{0,8},{8,0},{16,24},{24,16},{1,9},{9,1},{17,25},{25,17},{2,10},{10... | collective-permute-start | bytes 589832 | tf_op jit(solution)/shard_map/ppermute | solution.py:459
  9.7 7.5 %collective-permute-start.2 = (f32[64,768]{1,0:T(8,128)S(1)}, f32[64,768]{1,0:T(8,128)S(1)}, u32[]{:S(2)}, u32[]{:S(2)}) collective-permute-start(f32[64,768]{1,0:T(8,128)S(1)} %get-tuple-element.70.refs_2_.refs_0_), channel_id=1, source_target_pairs={{0,8},{8,0},{16,24},{24,16},{1,9},{9,1},{17,25},{25,17},{2,10},{10... | collective-permute-start | bytes 589832 | tf_op jit(solution)/shard_map/ppermute | solution.py:459
  11.4 7.8 %collective-permute-start.1 = (f32[96,1024]{1,0:T(8,128)S(1)}, f32[96,1024]{1,0:T(8,128)S(1)}, u32[]{:S(2)}, u32[]{:S(2)}) collective-permute-start(f32[96,1024]{1,0:T(8,128)S(1)} %get-tuple-element.69), channel_id=1, source_target_pairs={{0,1},{1,0},{2,4},{3,5},{4,2},{5,3},{6,7},{7,6},{8,9},{9,8},{10,12... | collective-permute-start | bytes 1179656 | tf_op jit(solution)/shard_map/ppermute | solution.py:491
  13.2 10.1 %collective-permute-start.7 = (f32[64,768]{1,0:T(8,128)S(1)}, f32[64,768]{1,0:T(8,128)S(1)}, u32[]{:S(2)}, u32[]{:S(2)}) collective-permute-start(f32[64,768]{1,0:T(8,128)S(1)} %add.16.refs_2_.refs_0_), channel_id=1, source_target_pairs={{8,16},{16,8},{0,2},{24,26},{10,18},{18,10},{2,0},{26,24},{12,20},... | collective-permute-start | bytes 589832 | tf_op jit(solution)/shard_map/ppermute | solution.py:464
  13.2 10.1 %collective-permute-start.8 = (f32[64,768]{1,0:T(8,128)S(1)}, f32[64,768]{1,0:T(8,128)S(1)}, u32[]{:S(2)}, u32[]{:S(2)}) collective-permute-start(f32[64,768]{1,0:T(8,128)S(1)} %get-tuple-element.76.refs_0_), channel_id=1, source_target_pairs={{0,8},{8,0},{16,24},{24,16},{1,9},{9,1},{17,25},{25,17},{2,10},{10... | collective-permute-start | bytes 589832 | tf_op jit(solution)/shard_map/ppermute | solution.py:459
  16.7 10.0 %collective-permute-start.5 = (f32[64,768]{1,0:T(8,128)S(1)}, f32[64,768]{1,0:T(8,128)S(1)}, u32[]{:S(2)}, u32[]{:S(2)}) collective-permute-start(f32[64,768]{1,0:T(8,128)S(1)} %get-tuple-element.72.refs_0_), channel_id=1, source_target_pairs={{0,8},{8,0},{16,24},{24,16},{1,9},{9,1},{17,25},{25,17},{2,10},{10... | collective-permute-start | bytes 589832 | tf_op jit(solution)/shard_map/ppermute | solution.py:459
  17.3 9.3 %collective-permute-start.6 = (f32[64,768]{1,0:T(8,128)S(1)}, f32[64,768]{1,0:T(8,128)S(1)}, u32[]{:S(2)}, u32[]{:S(2)}) collective-permute-start(f32[64,768]{1,0:T(8,128)S(1)} %add.17.refs_4_.refs_0_), channel_id=1, source_target_pairs={{8,16},{16,8},{0,2},{24,26},{10,18},{18,10},{2,0},{26,24},{12,20},... | collective-permute-start | bytes 589832 | tf_op jit(solution)/shard_map/ppermute | solution.py:464
  19.4 9.7 %collective-permute-start.4 = (f32[512,128]{1,0:T(8,128)S(1)}, f32[512,128]{1,0:T(8,128)S(1)}, u32[]{:S(2)}, u32[]{:S(2)}) collective-permute-start(f32[512,128]{1,0:T(8,128)S(1)} %side_pack.1.refs_7_), channel_id=1, source_target_pairs={{0,1},{1,0},{2,3},{3,2},{4,5},{5,4},{6,7},{7,6},{8,9},{9,8},{10,11... | collective-permute-start | bytes 786440 | tf_op jit(solution)/shard_map/ppermute | solution.py:497
  23.3 8.3 %collective-permute-start.10 = (f32[64,768]{1,0:T(8,128)S(1)}, f32[64,768]{1,0:T(8,128)S(1)}, u32[]{:S(2)}, u32[]{:S(2)}) collective-permute-start(f32[64,768]{1,0:T(8,128)S(1)} %add.18.refs_4_.refs_0_), channel_id=1, source_target_pairs={{8,16},{16,8},{0,2},{24,26},{10,18},{18,10},{2,0},{26,24},{12,20},... | collective-permute-start | bytes 589832 | tf_op jit(solution)/shard_map/ppermute | solution.py:464
  23.4 8.3 %collective-permute-start.11 = (f32[64,768]{1,0:T(8,128)S(1)}, f32[64,768]{1,0:T(8,128)S(1)}, u32[]{:S(2)}, u32[]{:S(2)}) collective-permute-start(f32[64,768]{1,0:T(8,128)S(1)} %get-tuple-element.83), channel_id=1, source_target_pairs={{0,8},{8,0},{16,24},{24,16},{1,9},{9,1},{17,25},{25,17},{2,10},{10... | collective-permute-start | bytes 589832 | tf_op jit(solution)/shard_map/ppermute | solution.py:459
  26.7 7.6 %collective-permute-start.9 = (f32[64,768]{1,0:T(8,128)S(1)}, f32[64,768]{1,0:T(8,128)S(1)}, u32[]{:S(2)}, u32[]{:S(2)}) collective-permute-start(f32[64,768]{1,0:T(8,128)S(1)} %add.19.refs_8_.refs_0_), channel_id=1, source_target_pairs={{8,16},{16,8},{0,2},{24,26},{10,18},{18,10},{2,0},{26,24},{12,20},... | collective-permute-start | bytes 589832 | tf_op jit(solution)/shard_map/ppermute | solution.py:464
  26.7 8.2 %collective-permute-start.14 = (f32[64,768]{1,0:T(8,128)S(1)}, f32[64,768]{1,0:T(8,128)S(1)}, u32[]{:S(2)}, u32[]{:S(2)}) collective-permute-start(f32[64,768]{1,0:T(8,128)S(1)} %get-tuple-element.88), channel_id=1, source_target_pairs={{0,8},{8,0},{16,24},{24,16},{1,9},{9,1},{17,25},{25,17},{2,10},{10... | collective-permute-start | bytes 589832 | tf_op jit(solution)/shard_map/ppermute | solution.py:459
  31.8 6.5 %collective-permute-start.16 = (f32[64,768]{1,0:T(8,128)S(1)}, f32[64,768]{1,0:T(8,128)S(1)}, u32[]{:S(2)}, u32[]{:S(2)}) collective-permute-start(f32[64,768]{1,0:T(8,128)S(1)} %add.20.refs_4_.refs_0_), channel_id=1, source_target_pairs={{8,16},{16,8},{0,2},{24,26},{10,18},{18,10},{2,0},{26,24},{12,20},... | collective-permute-start | bytes 589832 | tf_op jit(solution)/shard_map/ppermute | solution.py:464
  31.9 8.1 %collective-permute-start.13 = (f32[64,768]{1,0:T(8,128)S(1)}, f32[64,768]{1,0:T(8,128)S(1)}, u32[]{:S(2)}, u32[]{:S(2)}) collective-permute-start(f32[64,768]{1,0:T(8,128)S(1)} %get-tuple-element.86), channel_id=1, source_target_pairs={{0,8},{8,0},{16,24},{24,16},{1,9},{9,1},{17,25},{25,17},{2,10},{10... | collective-permute-start | bytes 589832 | tf_op jit(solution)/shard_map/ppermute | solution.py:459
  35.0 7.8 %collective-permute-start.15 = (f32[64,768]{1,0:T(8,128)S(1)}, f32[64,768]{1,0:T(8,128)S(1)}, u32[]{:S(2)}, u32[]{:S(2)}) collective-permute-start(f32[64,768]{1,0:T(8,128)S(1)} %add.21.refs_4_.refs_0_), channel_id=1, source_target_pairs={{8,16},{16,8},{0,2},{24,26},{10,18},{18,10},{2,0},{26,24},{12,20},... | collective-permute-start | bytes 589832 | tf_op jit(solution)/shard_map/ppermute | solution.py:464
  35.1 8.7 %collective-permute-start.12 = (f32[64,768]{1,0:T(8,128)S(1)}, f32[64,768]{1,0:T(8,128)S(1)}, u32[]{:S(2)}, u32[]{:S(2)}) collective-permute-start(f32[64,768]{1,0:T(8,128)S(1)} %get-tuple-element.85), channel_id=1, source_target_pairs={{0,8},{8,0},{16,24},{24,16},{1,9},{9,1},{17,25},{25,17},{2,10},{10... | collective-permute-start | bytes 589832 | tf_op jit(solution)/shard_map/ppermute | solution.py:459
  40.0 6.6 %collective-permute-start.18 = (f32[64,768]{1,0:T(8,128)S(1)}, f32[64,768]{1,0:T(8,128)S(1)}, u32[]{:S(2)}, u32[]{:S(2)}) collective-permute-start(f32[64,768]{1,0:T(8,128)S(1)} %add.22.refs_4_.refs_0_), channel_id=1, source_target_pairs={{8,16},{16,8},{0,2},{24,26},{10,18},{18,10},{2,0},{26,24},{12,20},... | collective-permute-start | bytes 589832 | tf_op jit(solution)/shard_map/ppermute | solution.py:464
  40.0 9.6 %collective-permute-start.19 = (f32[64,768]{1,0:T(8,128)S(1)}, f32[64,768]{1,0:T(8,128)S(1)}, u32[]{:S(2)}, u32[]{:S(2)}) collective-permute-start(f32[64,768]{1,0:T(8,128)S(1)} %get-tuple-element.101), channel_id=1, source_target_pairs={{0,8},{8,0},{16,24},{24,16},{1,9},{9,1},{17,25},{25,17},{2,10},{10... | collective-permute-start | bytes 589832 | tf_op jit(solution)/shard_map/ppermute | solution.py:459
  43.8 5.9 %collective-permute-start.17 = (f32[64,768]{1,0:T(8,128)S(1)}, f32[64,768]{1,0:T(8,128)S(1)}, u32[]{:S(2)}, u32[]{:S(2)}) collective-permute-start(f32[64,768]{1,0:T(8,128)S(1)} %add.23.refs_4_.refs_0_), channel_id=1, source_target_pairs={{8,16},{16,8},{0,2},{24,26},{10,18},{18,10},{2,0},{26,24},{12,20},... | collective-permute-start | bytes 589832 | tf_op jit(solution)/shard_map/ppermute | solution.py:464
  43.9 9.6 %collective-permute-start.25 = (f32[64,768]{1,0:T(8,128)S(1)}, f32[64,768]{1,0:T(8,128)S(1)}, u32[]{:S(2)}, u32[]{:S(2)}) collective-permute-start(f32[64,768]{1,0:T(8,128)S(1)} %get-tuple-element.108), channel_id=1, source_target_pairs={{0,8},{8,0},{16,24},{24,16},{1,9},{9,1},{17,25},{25,17},{2,10},{10... | collective-permute-start | bytes 589832 | tf_op jit(solution)/shard_map/ppermute | solution.py:459
  46.6 12.0 %collective-permute-start.26 = (f32[64,768]{1,0:T(8,128)S(1)}, f32[64,768]{1,0:T(8,128)S(1)}, u32[]{:S(2)}, u32[]{:S(2)}) collective-permute-start(f32[64,768]{1,0:T(8,128)S(1)} %get-tuple-element.112), channel_id=1, source_target_pairs={{0,8},{8,0},{16,24},{24,16},{1,9},{9,1},{17,25},{25,17},{2,10},{10... | collective-permute-start | bytes 589832 | tf_op jit(solution)/shard_map/ppermute | solution.py:459
  49.8 3.7 %collective-permute-start.20 = (f32[8,128]{1,0:T(8,128)S(1)}, f32[8,128]{1,0:T(8,128)S(1)}, u32[]{:S(2)}, u32[]{:S(2)}) collective-permute-start(f32[8,128]{1,0:T(8,128)S(1)} %get-tuple-element.107), channel_id=1, source_target_pairs={{0,1},{1,0},{2,3},{3,2},{4,5},{5,4},{6,7},{7,6},{8,9},{9,8},{10,11... | collective-permute-start | bytes 12296 | tf_op jit(solution)/shard_map/ppermute | solution.py:516
  50.6 9.7 %collective-permute-start.27 = (f32[64,768]{1,0:T(8,128)S(1)}, f32[64,768]{1,0:T(8,128)S(1)}, u32[]{:S(2)}, u32[]{:S(2)}) collective-permute-start(f32[64,768]{1,0:T(8,128)S(1)} %get-tuple-element.115), channel_id=1, source_target_pairs={{0,8},{8,0},{16,24},{24,16},{1,9},{9,1},{17,25},{25,17},{2,10},{10... | collective-permute-start | bytes 589832 | tf_op jit(solution)/shard_map/ppermute | solution.py:459
  53.5 1.2 %collective-permute-start.21 = (f32[8,128]{1,0:T(8,128)S(1)}, f32[8,128]{1,0:T(8,128)S(1)}, u32[]{:S(2)}, u32[]{:S(2)}) collective-permute-start(f32[8,128]{1,0:T(8,128)S(1)} %add.14), channel_id=1, source_target_pairs={{0,2},{2,0},{4,6},{6,4},{1,3},{3,1},{5,7},{7,5},{8,10},{10,8},{12,... | collective-permute-start | bytes 12296 | tf_op jit(solution)/shard_map/ppermute | solution.py:517
  54.6 6.8 %collective-permute-start.22 = (f32[8,128]{1,0:T(8,128)S(1)}, f32[8,128]{1,0:T(8,128)S(1)}, u32[]{:S(2)}, u32[]{:S(2)}) collective-permute-start(f32[8,128]{1,0:T(8,128)S(1)} %add.15.refs_0_), channel_id=1, source_target_pairs={{0,12},{2,14},{4,8},{6,10},{8,4},{10,6},{12,0},{14,2},{16,28},{18,... | collective-permute-start | bytes 12296 | tf_op jit(solution)/shard_map/ppermute | solution.py:521
  57.6 3.8 %collective-permute-start.23 = (f32[8,128]{1,0:T(8,128)S(1)}, f32[8,128]{1,0:T(8,128)S(1)}, u32[]{:S(2)}, u32[]{:S(2)}) collective-permute-start(f32[8,128]{1,0:T(8,128)S(1)} %add.15.refs_0_), channel_id=1, source_target_pairs={{0,8},{8,0},{16,24},{24,16},{1,9},{9,1},{17,25},{25,17},{2,10},{10... | collective-permute-start | bytes 12296 | tf_op jit(solution)/shard_map/ppermute | solution.py:522
  57.6 3.8 %collective-permute-start.24 = (f32[8,128]{1,0:T(8,128)S(1)}, f32[8,128]{1,0:T(8,128)S(1)}, u32[]{:S(2)}, u32[]{:S(2)}) collective-permute-start(f32[8,128]{1,0:T(8,128)S(1)} %add.15.refs_0_), channel_id=1, source_target_pairs={{0,4},{2,6},{4,0},{6,2},{1,5},{3,7},{5,1},{7,3},{8,12},{10,14},{12... | collective-permute-start | bytes 12296 | tf_op jit(solution)/shard_map/ppermute | solution.py:523

commit v6 on v5

--- a/solution.py
+++ b/solution.py
@@ -132,15 +132,13 @@
             for source, ref in ((s_hbm, s), (d_hbm, d)):
                 piece = (0, pl.ds(start, stop - start))
                 copies.append(pltpu.make_async_copy(source.at[piece], ref.at[piece], sems.at[len(copies)]))
-        for copy in copies[:2]:
+        for copy in copies:
             copy.start()
         tall = band(BLOCK, BLOCK + WIDE, -HALF)
         wide = band(512, 256, LANES)
         tall_ref[0], tall_ref[1] = tall
         wide_ref[0], wide_ref[1] = wide
         copies[0].wait()
-        for copy in copies[2:]:
-            copy.start()
         kv = cols_of(wide, rows_of(tall, s[0, :tall_n]), True)
         copies[1].wait()
         u = quotient(d[0, HALF : HALF + dens_n], kv)
@@ -386,7 +384,7 @@
         total = mass[0][...]
         if m > 1:
             total = jnp.where(in_middle(), total + mass[3][...], mass[2][...] + mass[1][...])
-        scale = cells / jnp.sum(total)
+        scale = cells / jnp.sum(jnp.sum(total, axis=0, keepdims=True), axis=1, keepdims=True)
         copies = []
         for row in range(0, rows, WIDE):
             band_rows = pl.ds(row, WIDE)

time: 63.6 us -> 63.5 us (level)
  no operation moved by 1% of the time
where the time goes in v6:
time: 63.5 us; the launch traced here: 63.3 us
  starting transfers between devices  38.8 us (61%)
  Pallas kernels  13.3 us (21%)
  waiting for transfers between devices  9.65 us (15%)
  between operations  1.56 us (2%)
    ppermute x12, starting transfers between devices, outward(): got[k] = lax.ppermute(value, 'map', outer)  29.8 us
    pallas_call x30, Pallas kernels, call(): return lambda *args: kernel(*args, *deps)  13.3 us
    ppermute x12, waiting for transfers between devices, outward(): got[k] = lax.ppermute(value, 'map', outer)  5.37 us
    ppermute x1, starting transfers between devices, local(): lax.ppermute(own, ('map', 'gx'), swap)  3 us
    ppermute x1, waiting for transfers between devices, local(): two = lax.ppermute(two, ('gx', 'gy'), far)  1.89 us
    ppermute x1, starting transfers between devices, local(): from_left = from_right = lax.ppermute(packs[0], 'gy', [(0, 1), (1, 0)])  1.58 us
    ppermute x1, starting transfers between devices, local(): two = lax.ppermute(two, ('gx', 'gy'), far)  1.52 us
  transfers between devices with their start and end apart: 28, of which 10 were waited for; matrix products, arithmetic and copies ran while one was open for 0% of the time, Pallas kernels for 13%

profile of v6, /device:TPU:0, one launch (start us, length us, event | category | flops | bytes accessed | tf_op | source)
XLA Modules:
  0.0 63.3 jit_solution(18186844498545851035)
XLA Ops:
  1.3 2.9 %first.1 = (f32[64,768]{1,0:T(8,128)S(1)}, f32[64,768]{1,0:T(8,128)S(1)}, bf16[2,192,256]{2,1,0:T(8,128)(2,1)S(1)}, bf16[2,512,256]{2,1,0:T(8,128)(2,1)S(1)}, f3...) custom-call(f32[1]{0:T(128)S(6)} %copy.5.refs_0_, f32[1,384,1024]{2,1,0:T(8,128)} %refs_1_.1, ...), custom_call_target="tpu_custom_call" | custom-call | tf_op jit(solution)/shard_map/first/pallas_call | solution.py:116
  4.2 0.5 collective-permute-start
  4.7 2.7 %collective-permute-start.3 = (f32[64,768]{1,0:T(8,128)S(1)}, f32[64,768]{1,0:T(8,128)S(1)}, u32[]{:S(2)}, u32[]{:S(2)}) collective-permute-start(f32[64,768]{1,0:T(8,128)S(1)} %get-tuple-element.71.refs_0_), channel_id=1, source_target_pairs={{0,8},{8,0},{16,24},{24,16},{1,9},{9,1},{17,25},{25,17},{2,10},{10... | collective-permute-start | bytes 589832 | tf_op jit(solution)/shard_map/ppermute | solution.py:457
  7.4 2.4 %inner.1 = (f32[64,768]{1,0:T(8,128)S(1)}, f32[64,768]{1,0:T(8,128)S(1)}, f32[64,768]{1,0:T(8,128)S(1)}, f32[64,768]{1,0:T(8,128)S(1)}, f32[64,768]{1,0:T(8,128)...) custom-call(f32[1]{0:T(128)S(6)} %copy.5.refs_0_, f32[1,384,1024]{2,1,0:T(8,128)S(1)} %get-tuple-element.64.refs_1_.refs_0_, ...), custom_call_target="tpu_custom_call" | custom-call | flops 2500000000 | tf_op jit(solution)/shard_map/inner/pallas_call | solution.py:116
  9.7 1.7 %collective-permute-start.2 = (f32[64,768]{1,0:T(8,128)S(1)}, f32[64,768]{1,0:T(8,128)S(1)}, u32[]{:S(2)}, u32[]{:S(2)}) collective-permute-start(f32[64,768]{1,0:T(8,128)S(1)} %get-tuple-element.70.refs_2_.refs_0_), channel_id=1, source_target_pairs={{0,8},{8,0},{16,24},{24,16},{1,9},{9,1},{17,25},{25,17},{2,10},{10... | collective-permute-start | bytes 589832 | tf_op jit(solution)/shard_map/ppermute | solution.py:457
  11.4 1.5 %collective-permute-start.1 = (f32[96,1024]{1,0:T(8,128)S(1)}, f32[96,1024]{1,0:T(8,128)S(1)}, u32[]{:S(2)}, u32[]{:S(2)}) collective-permute-start(f32[96,1024]{1,0:T(8,128)S(1)} %get-tuple-element.69), channel_id=1, source_target_pairs={{0,1},{1,0},{2,4},{3,5},{4,2},{5,3},{6,7},{7,6},{8,9},{9,8},{10,12... | collective-permute-start | bytes 1179656 | tf_op jit(solution)/shard_map/ppermute | solution.py:489
  13.0 0.2 collective-permute-done.3.refs_1_
  13.2 0.1 collective-permute-start.7
  13.2 3.4 %collective-permute-start.8 = (f32[64,768]{1,0:T(8,128)S(1)}, f32[64,768]{1,0:T(8,128)S(1)}, u32[]{:S(2)}, u32[]{:S(2)}) collective-permute-start(f32[64,768]{1,0:T(8,128)S(1)} %get-tuple-element.76.refs_0_), channel_id=1, source_target_pairs={{0,8},{8,0},{16,24},{24,16},{1,9},{9,1},{17,25},{25,17},{2,10},{10... | collective-permute-start | bytes 589832 | tf_op jit(solution)/shard_map/ppermute | solution.py:457
  16.7 0.5 collective-permute-done.2.refs_1_
  17.3 0.1 collective-permute-start.6
  17.3 1.9 %collective-permute-done.1.refs_3_.refs_6_.refs_5_ = f32[96,1024]{1,0:T(8,128)S(1)} collective-permute-done((f32[96,1024]{1,0:T(8,128)S(1)}, f32[96,1024]{1,0:T(8,128)S(1)}, u32[]{:S(2)}, u32[]{:S(2)}) %collective-permute-start.1) | collective-permute-done | bytes 393248 | tf_op jit(solution)/shard_map/ppermute | solution.py:489
  19.2 0.2 side_pack.1.refs_7_
  19.4 1.6 %collective-permute-start.4 = (f32[512,128]{1,0:T(8,128)S(1)}, f32[512,128]{1,0:T(8,128)S(1)}, u32[]{:S(2)}, u32[]{:S(2)}) collective-permute-start(f32[512,128]{1,0:T(8,128)S(1)} %side_pack.1.refs_7_), channel_id=1, source_target_pairs={{0,1},{1,0},{2,3},{3,2},{4,5},{5,4},{6,7},{7,6},{8,9},{9,8},{10,11... | collective-permute-start | bytes 786440 | tf_op jit(solution)/shard_map/ppermute | solution.py:495
  21.0 2.2 %edges.1 = (f32[64,768]{1,0:T(8,128)S(1)}, f32[64,768]{1,0:T(8,128)S(1)}, f32[64,768]{1,0:T(8,128)S(1)}, f32[64,768]{1,0:T(8,128)S(1)}) custom-call(f32[1]{0:T(128)S(6)} %copy.5.refs_0_, f32[1,384,1024]{2,1,0:T(8,128)S(1)} %get-tuple-element.64.refs_1_.refs_0_, f32[1,384,1024]{2,1,0:T(8,128)S(1)} %get-tuple-element.65.refs_2_.refs_1_, ...), custom_call_target="tpu_custom_call" | custom-call | flops 2300000000 | tf_op jit(solution)/shard_map/edges/pallas_call | solution.py:116
  23.3 0.1 collective-permute-start.10
  23.4 3.1 %collective-permute-start.11 = (f32[64,768]{1,0:T(8,128)S(1)}, f32[64,768]{1,0:T(8,128)S(1)}, u32[]{:S(2)}, u32[]{:S(2)}) collective-permute-start(f32[64,768]{1,0:T(8,128)S(1)} %get-tuple-element.83), channel_id=1, source_target_pairs={{0,8},{8,0},{16,24},{24,16},{1,9},{9,1},{17,25},{25,17},{2,10},{10... | collective-permute-start | bytes 589832 | tf_op jit(solution)/shard_map/ppermute | solution.py:457
  26.7 0.1 collective-permute-start.9
  26.7 2.4 %collective-permute-start.14 = (f32[64,768]{1,0:T(8,128)S(1)}, f32[64,768]{1,0:T(8,128)S(1)}, u32[]{:S(2)}, u32[]{:S(2)}) collective-permute-start(f32[64,768]{1,0:T(8,128)S(1)} %get-tuple-element.88), channel_id=1, source_target_pairs={{0,8},{8,0},{16,24},{24,16},{1,9},{9,1},{17,25},{25,17},{2,10},{10... | collective-permute-start | bytes 589832 | tf_op jit(solution)/shard_map/ppermute | solution.py:457
  29.2 2.5 %sides.1 = (f32[64,768]{1,0:T(8,128)S(1)}, f32[64,768]{1,0:T(8,128)S(1)}, f32[64,768]{1,0:T(8,128)S(1)}, f32[64,768]{1,0:T(8,128)S(1)}) custom-call(f32[1]{0:T(128)S(6)} %copy.5.refs_0_, f32[1,384,1024]{2,1,0:T(8,128)S(1)} %get-tuple-element.64.refs_1_.refs_0_, f32[1,384,1024]{2,1,0:T(8,128)S(1)} %get-tuple-element.65.refs_2_.refs_1_, ...), custom_call_target="tpu_custom_call" | custom-call | flops 2500000000 | tf_op jit(solution)/shard_map/sides/pallas_call | solution.py:116
  31.8 0.1 collective-permute-start.16
  31.9 2.3 %collective-permute-start.13 = (f32[64,768]{1,0:T(8,128)S(1)}, f32[64,768]{1,0:T(8,128)S(1)}, u32[]{:S(2)}, u32[]{:S(2)}) collective-permute-start(f32[64,768]{1,0:T(8,128)S(1)} %get-tuple-element.86), channel_id=1, source_target_pairs={{0,8},{8,0},{16,24},{24,16},{1,9},{9,1},{17,25},{25,17},{2,10},{10... | collective-permute-start | bytes 589832 | tf_op jit(solution)/shard_map/ppermute | solution.py:457
  34.3 0.1 finish.5
  34.4 0.6 collective-permute-done.14.refs_1_
  35.0 0.1 collective-permute-start.15
  35.1 3.2 %collective-permute-start.12 = (f32[64,768]{1,0:T(8,128)S(1)}, f32[64,768]{1,0:T(8,128)S(1)}, u32[]{:S(2)}, u32[]{:S(2)}) collective-permute-start(f32[64,768]{1,0:T(8,128)S(1)} %get-tuple-element.85), channel_id=1, source_target_pairs={{0,8},{8,0},{16,24},{24,16},{1,9},{9,1},{17,25},{25,17},{2,10},{10... | collective-permute-start | bytes 589832 | tf_op jit(solution)/shard_map/ppermute | solution.py:457
  38.3 0.1 finish.6
  38.4 1.5 %collective-permute-done.13.refs_1_ = f32[64,768]{1,0:T(8,128)S(1)} collective-permute-done((f32[64,768]{1,0:T(8,128)S(1)}, f32[64,768]{1,0:T(8,128)S(1)}, u32[]{:S(2)}, u32[]{:S(2)}) %collective-permute-start.13) | collective-permute-done | bytes 196640 | tf_op jit(solution)/shard_map/ppermute | solution.py:457
  40.0 0.1 collective-permute-start.18
  40.0 2.7 %collective-permute-start.19 = (f32[64,768]{1,0:T(8,128)S(1)}, f32[64,768]{1,0:T(8,128)S(1)}, u32[]{:S(2)}, u32[]{:S(2)}) collective-permute-start(f32[64,768]{1,0:T(8,128)S(1)} %get-tuple-element.101), channel_id=1, source_target_pairs={{0,8},{8,0},{16,24},{24,16},{1,9},{9,1},{17,25},{25,17},{2,10},{10... | collective-permute-start | bytes 589832 | tf_op jit(solution)/shard_map/ppermute | solution.py:457
  42.8 0.1 finish.7
  42.9 0.9 %collective-permute-done.12.refs_1_ = f32[64,768]{1,0:T(8,128)S(1)} collective-permute-done((f32[64,768]{1,0:T(8,128)S(1)}, f32[64,768]{1,0:T(8,128)S(1)}, u32[]{:S(2)}, u32[]{:S(2)}) %collective-permute-start.12) | collective-permute-done | bytes 196640 | tf_op jit(solution)/shard_map/ppermute | solution.py:457
  43.8 0.1 collective-permute-start.17
  43.9 2.6 %collective-permute-start.25 = (f32[64,768]{1,0:T(8,128)S(1)}, f32[64,768]{1,0:T(8,128)S(1)}, u32[]{:S(2)}, u32[]{:S(2)}) collective-permute-start(f32[64,768]{1,0:T(8,128)S(1)} %get-tuple-element.108), channel_id=1, source_target_pairs={{0,8},{8,0},{16,24},{24,16},{1,9},{9,1},{17,25},{25,17},{2,10},{10... | collective-permute-start | bytes 589832 | tf_op jit(solution)/shard_map/ppermute | solution.py:457
  46.6 3.0 %collective-permute-start.26 = (f32[64,768]{1,0:T(8,128)S(1)}, f32[64,768]{1,0:T(8,128)S(1)}, u32[]{:S(2)}, u32[]{:S(2)}) collective-permute-start(f32[64,768]{1,0:T(8,128)S(1)} %get-tuple-element.112), channel_id=1, source_target_pairs={{0,8},{8,0},{16,24},{24,16},{1,9},{9,1},{17,25},{25,17},{2,10},{10... | collective-permute-start | bytes 589832 | tf_op jit(solution)/shard_map/ppermute | solution.py:457
  49.5 0.1 finish.8
  49.6 0.1 finish.9
  49.8 0.9 %collective-permute-start.20 = (f32[8,128]{1,0:T(8,128)S(1)}, f32[8,128]{1,0:T(8,128)S(1)}, u32[]{:S(2)}, u32[]{:S(2)}) collective-permute-start(f32[8,128]{1,0:T(8,128)S(1)} %get-tuple-element.107), channel_id=1, source_target_pairs={{0,1},{1,0},{2,3},{3,2},{4,5},{5,4},{6,7},{7,6},{8,9},{9,8},{10,11... | collective-permute-start | bytes 12296 | tf_op jit(solution)/shard_map/ppermute | solution.py:514
  50.7 2.5 %collective-permute-start.27 = (f32[64,768]{1,0:T(8,128)S(1)}, f32[64,768]{1,0:T(8,128)S(1)}, u32[]{:S(2)}, u32[]{:S(2)}) collective-permute-start(f32[64,768]{1,0:T(8,128)S(1)} %get-tuple-element.115), channel_id=1, source_target_pairs={{0,8},{8,0},{16,24},{24,16},{1,9},{9,1},{17,25},{25,17},{2,10},{10... | collective-permute-start | bytes 589832 | tf_op jit(solution)/shard_map/ppermute | solution.py:457
  53.2 0.3 collective-permute-done.20
  53.5 0.1 finish_last.3
  53.5 1.1 %collective-permute-done.21 = f32[8,128]{1,0:T(8,128)S(1)} collective-permute-done((f32[8,128]{1,0:T(8,128)S(1)}, f32[8,128]{1,0:T(8,128)S(1)}, u32[]{:S(2)}, u32[]{:S(2)}) %collective-permute-start.21) | collective-permute-done | bytes 4128 | tf_op jit(solution)/shard_map/ppermute | solution.py:515
  54.6 3.0 %collective-permute-start.22 = (f32[8,128]{1,0:T(8,128)S(1)}, f32[8,128]{1,0:T(8,128)S(1)}, u32[]{:S(2)}, u32[]{:S(2)}) collective-permute-start(f32[8,128]{1,0:T(8,128)S(1)} %add.15.refs_0_), channel_id=1, source_target_pairs={{0,12},{2,14},{4,8},{6,10},{8,4},{10,6},{12,0},{14,2},{16,28},{18,... | collective-permute-start | bytes 12296 | tf_op jit(solution)/shard_map/ppermute | solution.py:519
  57.6 1.0 %collective-permute-start.24 = (f32[8,128]{1,0:T(8,128)S(1)}, f32[8,128]{1,0:T(8,128)S(1)}, u32[]{:S(2)}, u32[]{:S(2)}) collective-permute-start(f32[8,128]{1,0:T(8,128)S(1)} %add.15.refs_0_), channel_id=1, source_target_pairs={{0,4},{2,6},{4,0},{6,2},{1,5},{3,7},{5,1},{7,3},{8,12},{10,14},{12... | collective-permute-start | bytes 12296 | tf_op jit(solution)/shard_map/ppermute | solution.py:521
  58.7 1.7 %collective-permute-done.27.refs_1_ = f32[64,768]{1,0:T(8,128)S(1)} collective-permute-done((f32[64,768]{1,0:T(8,128)S(1)}, f32[64,768]{1,0:T(8,128)S(1)}, u32[]{:S(2)}, u32[]{:S(2)}) %collective-permute-start.27) | collective-permute-done | bytes 196640 | tf_op jit(solution)/shard_map/ppermute | solution.py:457
  60.3 0.1 finish_last.5
  60.4 1.0 %collective-permute-done.22.refs_1_ = f32[8,128]{1,0:T(8,128)S(1)} collective-permute-done((f32[8,128]{1,0:T(8,128)S(1)}, f32[8,128]{1,0:T(8,128)S(1)}, u32[]{:S(2)}, u32[]{:S(2)}) %collective-permute-start.22) | collective-permute-done | bytes 4128 | tf_op jit(solution)/shard_map/ppermute | solution.py:519
  61.5 1.9 %assemble.1 = (f32[384,1024]{1,0:T(8,128)}, f32[1,384,1024]{2,1,0:T(8,128)}) custom-call(f32[8,128]{1,0:T(8,128)S(1)} %add.15.refs_0_, f32[8,128]{1,0:T(8,128)S(1)} %collective-permute-done.22.refs_1_, f32[8,128]{1,0:T(8,128)S(1)} %collective-permute-done.23.refs_2_, f32[8,128]{1,0:T(8,128)S(1)} %collective-permute-done.24.refs_3_, ...), custom_call_target="tpu_custom_call" | custom-call | tf_op jit(solution)/shard_map/assemble/pallas_call | solution.py:116
  (40 shorter events, 0.8 us)
Async XLA Ops:
  4.2 3.2 %collective-permute-start = (f32[96,1024]{1,0:T(8,128)S(1)}, f32[96,1024]{1,0:T(8,128)S(1)}, u32[]{:S(2)}, u32[]{:S(2)}) collective-permute-start(f32[96,1024]{1,0:T(8,128)S(1)} %get-tuple-element.67), channel_id=1, source_target_pairs={{0,2},{2,0},{4,6},{6,4},{1,3},{3,1},{5,7},{7,5},{8,10},{10,8},{12,... | collective-permute-start | bytes 1179656 | tf_op jit(solution)/shard_map/ppermute | solution.py:484
  4.7 8.4 %collective-permute-start.3 = (f32[64,768]{1,0:T(8,128)S(1)}, f32[64,768]{1,0:T(8,128)S(1)}, u32[]{:S(2)}, u32[]{:S(2)}) collective-permute-start(f32[64,768]{1,0:T(8,128)S(1)} %get-tuple-element.71.refs_0_), channel_id=1, source_target_pairs={{0,8},{8,0},{16,24},{24,16},{1,9},{9,1},{17,25},{25,17},{2,10},{10... | collective-permute-start | bytes 589832 | tf_op jit(solution)/shard_map/ppermute | solution.py:457
  9.7 7.5 %collective-permute-start.2 = (f32[64,768]{1,0:T(8,128)S(1)}, f32[64,768]{1,0:T(8,128)S(1)}, u32[]{:S(2)}, u32[]{:S(2)}) collective-permute-start(f32[64,768]{1,0:T(8,128)S(1)} %get-tuple-element.70.refs_2_.refs_0_), channel_id=1, source_target_pairs={{0,8},{8,0},{16,24},{24,16},{1,9},{9,1},{17,25},{25,17},{2,10},{10... | collective-permute-start | bytes 589832 | tf_op jit(solution)/shard_map/ppermute | solution.py:457
  11.4 7.8 %collective-permute-start.1 = (f32[96,1024]{1,0:T(8,128)S(1)}, f32[96,1024]{1,0:T(8,128)S(1)}, u32[]{:S(2)}, u32[]{:S(2)}) collective-permute-start(f32[96,1024]{1,0:T(8,128)S(1)} %get-tuple-element.69), channel_id=1, source_target_pairs={{0,1},{1,0},{2,4},{3,5},{4,2},{5,3},{6,7},{7,6},{8,9},{9,8},{10,12... | collective-permute-start | bytes 1179656 | tf_op jit(solution)/shard_map/ppermute | solution.py:489
  13.2 10.1 %collective-permute-start.7 = (f32[64,768]{1,0:T(8,128)S(1)}, f32[64,768]{1,0:T(8,128)S(1)}, u32[]{:S(2)}, u32[]{:S(2)}) collective-permute-start(f32[64,768]{1,0:T(8,128)S(1)} %add.16.refs_2_.refs_0_), channel_id=1, source_target_pairs={{8,16},{16,8},{0,2},{24,26},{10,18},{18,10},{2,0},{26,24},{12,20},... | collective-permute-start | bytes 589832 | tf_op jit(solution)/shard_map/ppermute | solution.py:462
  13.2 10.1 %collective-permute-start.8 = (f32[64,768]{1,0:T(8,128)S(1)}, f32[64,768]{1,0:T(8,128)S(1)}, u32[]{:S(2)}, u32[]{:S(2)}) collective-permute-start(f32[64,768]{1,0:T(8,128)S(1)} %get-tuple-element.76.refs_0_), channel_id=1, source_target_pairs={{0,8},{8,0},{16,24},{24,16},{1,9},{9,1},{17,25},{25,17},{2,10},{10... | collective-permute-start | bytes 589832 | tf_op jit(solution)/shard_map/ppermute | solution.py:457
  16.7 10.0 %collective-permute-start.5 = (f32[64,768]{1,0:T(8,128)S(1)}, f32[64,768]{1,0:T(8,128)S(1)}, u32[]{:S(2)}, u32[]{:S(2)}) collective-permute-start(f32[64,768]{1,0:T(8,128)S(1)} %get-tuple-element.72.refs_0_), channel_id=1, source_target_pairs={{0,8},{8,0},{16,24},{24,16},{1,9},{9,1},{17,25},{25,17},{2,10},{10... | collective-permute-start | bytes 589832 | tf_op jit(solution)/shard_map/ppermute | solution.py:457
  17.3 9.3 %collective-permute-start.6 = (f32[64,768]{1,0:T(8,128)S(1)}, f32[64,768]{1,0:T(8,128)S(1)}, u32[]{:S(2)}, u32[]{:S(2)}) collective-permute-start(f32[64,768]{1,0:T(8,128)S(1)} %add.17.refs_4_.refs_0_), channel_id=1, source_target_pairs={{8,16},{16,8},{0,2},{24,26},{10,18},{18,10},{2,0},{26,24},{12,20},... | collective-permute-start | bytes 589832 | tf_op jit(solution)/shard_map/ppermute | solution.py:462
  19.4 9.7 %collective-permute-start.4 = (f32[512,128]{1,0:T(8,128)S(1)}, f32[512,128]{1,0:T(8,128)S(1)}, u32[]{:S(2)}, u32[]{:S(2)}) collective-permute-start(f32[512,128]{1,0:T(8,128)S(1)} %side_pack.1.refs_7_), channel_id=1, source_target_pairs={{0,1},{1,0},{2,3},{3,2},{4,5},{5,4},{6,7},{7,6},{8,9},{9,8},{10,11... | collective-permute-start | bytes 786440 | tf_op jit(solution)/shard_map/ppermute | solution.py:495
  23.3 8.3 %collective-permute-start.10 = (f32[64,768]{1,0:T(8,128)S(1)}, f32[64,768]{1,0:T(8,128)S(1)}, u32[]{:S(2)}, u32[]{:S(2)}) collective-permute-start(f32[64,768]{1,0:T(8,128)S(1)} %add.18.refs_4_.refs_0_), channel_id=1, source_target_pairs={{8,16},{16,8},{0,2},{24,26},{10,18},{18,10},{2,0},{26,24},{12,20},... | collective-permute-start | bytes 589832 | tf_op jit(solution)/shard_map/ppermute | solution.py:462
  23.4 8.3 %collective-permute-start.11 = (f32[64,768]{1,0:T(8,128)S(1)}, f32[64,768]{1,0:T(8,128)S(1)}, u32[]{:S(2)}, u32[]{:S(2)}) collective-permute-start(f32[64,768]{1,0:T(8,128)S(1)} %get-tuple-element.83), channel_id=1, source_target_pairs={{0,8},{8,0},{16,24},{24,16},{1,9},{9,1},{17,25},{25,17},{2,10},{10... | collective-permute-start | bytes 589832 | tf_op jit(solution)/shard_map/ppermute | solution.py:457
  26.7 7.5 %collective-permute-start.9 = (f32[64,768]{1,0:T(8,128)S(1)}, f32[64,768]{1,0:T(8,128)S(1)}, u32[]{:S(2)}, u32[]{:S(2)}) collective-permute-start(f32[64,768]{1,0:T(8,128)S(1)} %add.19.refs_8_.refs_0_), channel_id=1, source_target_pairs={{8,16},{16,8},{0,2},{24,26},{10,18},{18,10},{2,0},{26,24},{12,20},... | collective-permute-start | bytes 589832 | tf_op jit(solution)/shard_map/ppermute | solution.py:462
  26.7 8.2 %collective-permute-start.14 = (f32[64,768]{1,0:T(8,128)S(1)}, f32[64,768]{1,0:T(8,128)S(1)}, u32[]{:S(2)}, u32[]{:S(2)}) collective-permute-start(f32[64,768]{1,0:T(8,128)S(1)} %get-tuple-element.88), channel_id=1, source_target_pairs={{0,8},{8,0},{16,24},{24,16},{1,9},{9,1},{17,25},{25,17},{2,10},{10... | collective-permute-start | bytes 589832 | tf_op jit(solution)/shard_map/ppermute | solution.py:457
  31.8 6.5 %collective-permute-start.16 = (f32[64,768]{1,0:T(8,128)S(1)}, f32[64,768]{1,0:T(8,128)S(1)}, u32[]{:S(2)}, u32[]{:S(2)}) collective-permute-start(f32[64,768]{1,0:T(8,128)S(1)} %add.20.refs_4_.refs_0_), channel_id=1, source_target_pairs={{8,16},{16,8},{0,2},{24,26},{10,18},{18,10},{2,0},{26,24},{12,20},... | collective-permute-start | bytes 589832 | tf_op jit(solution)/shard_map/ppermute | solution.py:462
  31.9 8.1 %collective-permute-start.13 = (f32[64,768]{1,0:T(8,128)S(1)}, f32[64,768]{1,0:T(8,128)S(1)}, u32[]{:S(2)}, u32[]{:S(2)}) collective-permute-start(f32[64,768]{1,0:T(8,128)S(1)} %get-tuple-element.86), channel_id=1, source_target_pairs={{0,8},{8,0},{16,24},{24,16},{1,9},{9,1},{17,25},{25,17},{2,10},{10... | collective-permute-start | bytes 589832 | tf_op jit(solution)/shard_map/ppermute | solution.py:457
  35.0 7.8 %collective-permute-start.15 = (f32[64,768]{1,0:T(8,128)S(1)}, f32[64,768]{1,0:T(8,128)S(1)}, u32[]{:S(2)}, u32[]{:S(2)}) collective-permute-start(f32[64,768]{1,0:T(8,128)S(1)} %add.21.refs_4_.refs_0_), channel_id=1, source_target_pairs={{8,16},{16,8},{0,2},{24,26},{10,18},{18,10},{2,0},{26,24},{12,20},... | collective-permute-start | bytes 589832 | tf_op jit(solution)/shard_map/ppermute | solution.py:462
  35.1 8.7 %collective-permute-start.12 = (f32[64,768]{1,0:T(8,128)S(1)}, f32[64,768]{1,0:T(8,128)S(1)}, u32[]{:S(2)}, u32[]{:S(2)}) collective-permute-start(f32[64,768]{1,0:T(8,128)S(1)} %get-tuple-element.85), channel_id=1, source_target_pairs={{0,8},{8,0},{16,24},{24,16},{1,9},{9,1},{17,25},{25,17},{2,10},{10... | collective-permute-start | bytes 589832 | tf_op jit(solution)/shard_map/ppermute | solution.py:457
  40.0 6.6 %collective-permute-start.18 = (f32[64,768]{1,0:T(8,128)S(1)}, f32[64,768]{1,0:T(8,128)S(1)}, u32[]{:S(2)}, u32[]{:S(2)}) collective-permute-start(f32[64,768]{1,0:T(8,128)S(1)} %add.22.refs_4_.refs_0_), channel_id=1, source_target_pairs={{8,16},{16,8},{0,2},{24,26},{10,18},{18,10},{2,0},{26,24},{12,20},... | collective-permute-start | bytes 589832 | tf_op jit(solution)/shard_map/ppermute | solution.py:462
  40.0 9.6 %collective-permute-start.19 = (f32[64,768]{1,0:T(8,128)S(1)}, f32[64,768]{1,0:T(8,128)S(1)}, u32[]{:S(2)}, u32[]{:S(2)}) collective-permute-start(f32[64,768]{1,0:T(8,128)S(1)} %get-tuple-element.101), channel_id=1, source_target_pairs={{0,8},{8,0},{16,24},{24,16},{1,9},{9,1},{17,25},{25,17},{2,10},{10... | collective-permute-start | bytes 589832 | tf_op jit(solution)/shard_map/ppermute | solution.py:457
  43.8 5.9 %collective-permute-start.17 = (f32[64,768]{1,0:T(8,128)S(1)}, f32[64,768]{1,0:T(8,128)S(1)}, u32[]{:S(2)}, u32[]{:S(2)}) collective-permute-start(f32[64,768]{1,0:T(8,128)S(1)} %add.23.refs_4_.refs_0_), channel_id=1, source_target_pairs={{8,16},{16,8},{0,2},{24,26},{10,18},{18,10},{2,0},{26,24},{12,20},... | collective-permute-start | bytes 589832 | tf_op jit(solution)/shard_map/ppermute | solution.py:462
  43.9 9.6 %collective-permute-start.25 = (f32[64,768]{1,0:T(8,128)S(1)}, f32[64,768]{1,0:T(8,128)S(1)}, u32[]{:S(2)}, u32[]{:S(2)}) collective-permute-start(f32[64,768]{1,0:T(8,128)S(1)} %get-tuple-element.108), channel_id=1, source_target_pairs={{0,8},{8,0},{16,24},{24,16},{1,9},{9,1},{17,25},{25,17},{2,10},{10... | collective-permute-start | bytes 589832 | tf_op jit(solution)/shard_map/ppermute | solution.py:457
  46.6 12.0 %collective-permute-start.26 = (f32[64,768]{1,0:T(8,128)S(1)}, f32[64,768]{1,0:T(8,128)S(1)}, u32[]{:S(2)}, u32[]{:S(2)}) collective-permute-start(f32[64,768]{1,0:T(8,128)S(1)} %get-tuple-element.112), channel_id=1, source_target_pairs={{0,8},{8,0},{16,24},{24,16},{1,9},{9,1},{17,25},{25,17},{2,10},{10... | collective-permute-start | bytes 589832 | tf_op jit(solution)/shard_map/ppermute | solution.py:457
  49.8 3.7 %collective-permute-start.20 = (f32[8,128]{1,0:T(8,128)S(1)}, f32[8,128]{1,0:T(8,128)S(1)}, u32[]{:S(2)}, u32[]{:S(2)}) collective-permute-start(f32[8,128]{1,0:T(8,128)S(1)} %get-tuple-element.107), channel_id=1, source_target_pairs={{0,1},{1,0},{2,3},{3,2},{4,5},{5,4},{6,7},{7,6},{8,9},{9,8},{10,11... | collective-permute-start | bytes 12296 | tf_op jit(solution)/shard_map/ppermute | solution.py:514
  50.7 9.7 %collective-permute-start.27 = (f32[64,768]{1,0:T(8,128)S(1)}, f32[64,768]{1,0:T(8,128)S(1)}, u32[]{:S(2)}, u32[]{:S(2)}) collective-permute-start(f32[64,768]{1,0:T(8,128)S(1)} %get-tuple-element.115), channel_id=1, source_target_pairs={{0,8},{8,0},{16,24},{24,16},{1,9},{9,1},{17,25},{25,17},{2,10},{10... | collective-permute-start | bytes 589832 | tf_op jit(solution)/shard_map/ppermute | solution.py:457
  53.4 1.2 %collective-permute-start.21 = (f32[8,128]{1,0:T(8,128)S(1)}, f32[8,128]{1,0:T(8,128)S(1)}, u32[]{:S(2)}, u32[]{:S(2)}) collective-permute-start(f32[8,128]{1,0:T(8,128)S(1)} %add.14), channel_id=1, source_target_pairs={{0,2},{2,0},{4,6},{6,4},{1,3},{3,1},{5,7},{7,5},{8,10},{10,8},{12,... | collective-permute-start | bytes 12296 | tf_op jit(solution)/shard_map/ppermute | solution.py:515
  54.6 6.8 %collective-permute-start.22 = (f32[8,128]{1,0:T(8,128)S(1)}, f32[8,128]{1,0:T(8,128)S(1)}, u32[]{:S(2)}, u32[]{:S(2)}) collective-permute-start(f32[8,128]{1,0:T(8,128)S(1)} %add.15.refs_0_), channel_id=1, source_target_pairs={{0,12},{2,14},{4,8},{6,10},{8,4},{10,6},{12,0},{14,2},{16,28},{18,... | collective-permute-start | bytes 12296 | tf_op jit(solution)/shard_map/ppermute | solution.py:519
  57.6 3.8 %collective-permute-start.23 = (f32[8,128]{1,0:T(8,128)S(1)}, f32[8,128]{1,0:T(8,128)S(1)}, u32[]{:S(2)}, u32[]{:S(2)}) collective-permute-start(f32[8,128]{1,0:T(8,128)S(1)} %add.15.refs_0_), channel_id=1, source_target_pairs={{0,8},{8,0},{16,24},{24,16},{1,9},{9,1},{17,25},{25,17},{2,10},{10... | collective-permute-start | bytes 12296 | tf_op jit(solution)/shard_map/ppermute | solution.py:520
  57.6 3.8 %collective-permute-start.24 = (f32[8,128]{1,0:T(8,128)S(1)}, f32[8,128]{1,0:T(8,128)S(1)}, u32[]{:S(2)}, u32[]{:S(2)}) collective-permute-start(f32[8,128]{1,0:T(8,128)S(1)} %add.15.refs_0_), channel_id=1, source_target_pairs={{0,4},{2,6},{4,0},{6,2},{1,5},{3,7},{5,1},{7,3},{8,12},{10,14},{12... | collective-permute-start | bytes 12296 | tf_op jit(solution)/shard_map/ppermute | solution.py:521

commit v7 on v6

--- a/solution.py
+++ b/solution.py
@@ -490,14 +490,14 @@
     receive(0)
     inner_count = rows // WIDE - 2
     receive(1)
+    take(inner_count, edge_chunks(weights, scaling, densities, tall, wide, one, two, chain[0]))
+    total(0)
     packs = done(*side_pack(scaling, densities, one, two, chain[0]))
     if gy == 2:
         from_left = from_right = lax.ppermute(packs[0], "gy", [(0, 1), (1, 0)])
     else:
         from_left = lax.ppermute(packs[0], "gy", [(i, i + 1) for i in range(gy - 1)])
         from_right = lax.ppermute(packs[1], "gy", [(i + 1, i) for i in range(gy - 1)])
-    take(inner_count, edge_chunks(weights, scaling, densities, tall, wide, one, two, chain[0]))
-    total(0)
     receive(2)
     total(1)
     receive(3)

time: 63.5 us -> 63.5 us (level)
    ppermute x1, starting transfers between devices: 3 us -> 1.96 us  [local(): lax.ppermute(own, ('map', 'gx'), swap)]
    ppermute x1, starting transfers between devices: 0.88 us -> 1.58 us  [local(): own = mass[0] + lax.ppermute(mass[0], 'gy', [(0, 1), (1, 0)])]
where the time goes in v7:
time: 63.5 us; the launch traced here: 63.4 us
  starting transfers between devices  38.8 us (61%)
  Pallas kernels  13.3 us (21%)
  waiting for transfers between devices  9.68 us (15%)
  between operations  1.57 us (2%)
    ppermute x12, starting transfers between devices, outward(): got[k] = lax.ppermute(value, 'map', outer)  29.6 us
    pallas_call x30, Pallas kernels, call(): return lambda *args: kernel(*args, *deps)  13.3 us
    ppermute x12, waiting for transfers between devices, outward(): got[k] = lax.ppermute(value, 'map', outer)  5.35 us
    ppermute x1, starting transfers between devices, local(): lax.ppermute(own, ('map', 'gx'), swap)  1.96 us
    ppermute x1, waiting for transfers between devices, local(): two = lax.ppermute(two, ('gx', 'gy'), far)  1.9 us
    ppermute x1, starting transfers between devices, local(): from_left = from_right = lax.ppermute(packs[0], 'gy', [(0, 1), (1, 0)])  1.58 us
    ppermute x1, starting transfers between devices, local(): own = mass[0] + lax.ppermute(mass[0], 'gy', [(0, 1), (1, 0)])  1.58 us
    ppermute x1, starting transfers between devices, local(): lax.ppermute(own, 'gx', [(i, i ^ 2) for i in range(gx)])  1.52 us
  transfers between devices with their start and end apart: 28, of which 10 were waited for; matrix products, arithmetic and copies ran while one was open for 0% of the time, Pallas kernels for 13%

profile of v7, /device:TPU:0, one launch (start us, length us, event | category | flops | bytes accessed | tf_op | source)
XLA Modules:
  0.0 63.4 jit_solution(8953446003544697120)
XLA Ops:
  1.3 2.9 %first.1 = (f32[64,768]{1,0:T(8,128)S(1)}, f32[64,768]{1,0:T(8,128)S(1)}, bf16[2,192,256]{2,1,0:T(8,128)(2,1)S(1)}, bf16[2,512,256]{2,1,0:T(8,128)(2,1)S(1)}, f3...) custom-call(f32[1]{0:T(128)S(6)} %copy.5.refs_0_, f32[1,384,1024]{2,1,0:T(8,128)} %refs_1_.1, ...), custom_call_target="tpu_custom_call" | custom-call | tf_op jit(solution)/shard_map/first/pallas_call | solution.py:116
  4.2 0.5 collective-permute-start
  4.7 2.7 %collective-permute-start.2 = (f32[64,768]{1,0:T(8,128)S(1)}, f32[64,768]{1,0:T(8,128)S(1)}, u32[]{:S(2)}, u32[]{:S(2)}) collective-permute-start(f32[64,768]{1,0:T(8,128)S(1)} %get-tuple-element.70.refs_0_), channel_id=1, source_target_pairs={{0,8},{8,0},{16,24},{24,16},{1,9},{9,1},{17,25},{25,17},{2,10},{10... | collective-permute-start | bytes 589832 | tf_op jit(solution)/shard_map/ppermute | solution.py:457
  7.4 2.4 %inner.1 = (f32[64,768]{1,0:T(8,128)S(1)}, f32[64,768]{1,0:T(8,128)S(1)}, f32[64,768]{1,0:T(8,128)S(1)}, f32[64,768]{1,0:T(8,128)S(1)}, f32[64,768]{1,0:T(8,128)...) custom-call(f32[1]{0:T(128)S(6)} %copy.5.refs_0_, f32[1,384,1024]{2,1,0:T(8,128)S(1)} %get-tuple-element.64.refs_1_.refs_0_, ...), custom_call_target="tpu_custom_call" | custom-call | flops 2500000000 | tf_op jit(solution)/shard_map/inner/pallas_call | solution.py:116
  9.7 1.7 %collective-permute-start.4 = (f32[64,768]{1,0:T(8,128)S(1)}, f32[64,768]{1,0:T(8,128)S(1)}, u32[]{:S(2)}, u32[]{:S(2)}) collective-permute-start(f32[64,768]{1,0:T(8,128)S(1)} %get-tuple-element.71.refs_2_.refs_0_), channel_id=1, source_target_pairs={{0,8},{8,0},{16,24},{24,16},{1,9},{9,1},{17,25},{25,17},{2,10},{10... | collective-permute-start | bytes 589832 | tf_op jit(solution)/shard_map/ppermute | solution.py:457
  11.4 1.5 %collective-permute-start.1 = (f32[96,1024]{1,0:T(8,128)S(1)}, f32[96,1024]{1,0:T(8,128)S(1)}, u32[]{:S(2)}, u32[]{:S(2)}) collective-permute-start(f32[96,1024]{1,0:T(8,128)S(1)} %get-tuple-element.69), channel_id=1, source_target_pairs={{0,1},{1,0},{2,4},{3,5},{4,2},{5,3},{6,7},{7,6},{8,9},{9,8},{10,12... | collective-permute-start | bytes 1179656 | tf_op jit(solution)/shard_map/ppermute | solution.py:489
  13.0 0.2 collective-permute-done.2.refs_1_
  13.2 0.1 collective-permute-start.3
  13.2 3.4 %collective-permute-start.8 = (f32[64,768]{1,0:T(8,128)S(1)}, f32[64,768]{1,0:T(8,128)S(1)}, u32[]{:S(2)}, u32[]{:S(2)}) collective-permute-start(f32[64,768]{1,0:T(8,128)S(1)} %get-tuple-element.77.refs_0_), channel_id=1, source_target_pairs={{0,8},{8,0},{16,24},{24,16},{1,9},{9,1},{17,25},{25,17},{2,10},{10... | collective-permute-start | bytes 589832 | tf_op jit(solution)/shard_map/ppermute | solution.py:457
  16.7 0.5 collective-permute-done.4.refs_1_
  17.2 0.1 collective-permute-start.7
  17.3 1.9 %collective-permute-done.1.refs_6_.refs_3_.refs_5_ = f32[96,1024]{1,0:T(8,128)S(1)} collective-permute-done((f32[96,1024]{1,0:T(8,128)S(1)}, f32[96,1024]{1,0:T(8,128)S(1)}, u32[]{:S(2)}, u32[]{:S(2)}) %collective-permute-start.1) | collective-permute-done | bytes 393248 | tf_op jit(solution)/shard_map/ppermute | solution.py:489
  19.2 2.2 %edges.1 = (f32[64,768]{1,0:T(8,128)S(1)}, f32[64,768]{1,0:T(8,128)S(1)}, f32[64,768]{1,0:T(8,128)S(1)}, f32[64,768]{1,0:T(8,128)S(1)}) custom-call(f32[1]{0:T(128)S(6)} %copy.5.refs_0_, f32[1,384,1024]{2,1,0:T(8,128)S(1)} %get-tuple-element.64.refs_1_.refs_0_, f32[1,384,1024]{2,1,0:T(8,128)S(1)} %get-tuple-element.65.refs_2_.refs_1_, ...), custom_call_target="tpu_custom_call" | custom-call | flops 2300000000 | tf_op jit(solution)/shard_map/edges/pallas_call | solution.py:116
  21.5 0.2 side_pack.1.refs_2_
  21.7 1.6 %collective-permute-start.5 = (f32[512,128]{1,0:T(8,128)S(1)}, f32[512,128]{1,0:T(8,128)S(1)}, u32[]{:S(2)}, u32[]{:S(2)}) collective-permute-start(f32[512,128]{1,0:T(8,128)S(1)} %side_pack.1.refs_2_), channel_id=1, source_target_pairs={{0,1},{1,0},{2,3},{3,2},{4,5},{5,4},{6,7},{7,6},{8,9},{9,8},{10,11... | collective-permute-start | bytes 786440 | tf_op jit(solution)/shard_map/ppermute | solution.py:497
  23.3 0.1 collective-permute-start.10
  23.4 3.1 %collective-permute-start.11 = (f32[64,768]{1,0:T(8,128)S(1)}, f32[64,768]{1,0:T(8,128)S(1)}, u32[]{:S(2)}, u32[]{:S(2)}) collective-permute-start(f32[64,768]{1,0:T(8,128)S(1)} %get-tuple-element.83), channel_id=1, source_target_pairs={{0,8},{8,0},{16,24},{24,16},{1,9},{9,1},{17,25},{25,17},{2,10},{10... | collective-permute-start | bytes 589832 | tf_op jit(solution)/shard_map/ppermute | solution.py:457
  26.6 0.1 collective-permute-start.9
  26.7 2.5 %collective-permute-start.14 = (f32[64,768]{1,0:T(8,128)S(1)}, f32[64,768]{1,0:T(8,128)S(1)}, u32[]{:S(2)}, u32[]{:S(2)}) collective-permute-start(f32[64,768]{1,0:T(8,128)S(1)} %get-tuple-element.88), channel_id=1, source_target_pairs={{0,8},{8,0},{16,24},{24,16},{1,9},{9,1},{17,25},{25,17},{2,10},{10... | collective-permute-start | bytes 589832 | tf_op jit(solution)/shard_map/ppermute | solution.py:457
  29.2 0.4 collective-permute-done.5.refs_6_.refs_7_
  29.6 2.5 %sides.1 = (f32[64,768]{1,0:T(8,128)S(1)}, f32[64,768]{1,0:T(8,128)S(1)}, f32[64,768]{1,0:T(8,128)S(1)}, f32[64,768]{1,0:T(8,128)S(1)}) custom-call(f32[1]{0:T(128)S(6)} %copy.5.refs_0_, f32[1,384,1024]{2,1,0:T(8,128)S(1)} %get-tuple-element.64.refs_1_.refs_0_, f32[1,384,1024]{2,1,0:T(8,128)S(1)} %get-tuple-element.65.refs_2_.refs_1_, ...), custom_call_target="tpu_custom_call" | custom-call | flops 2500000000 | tf_op jit(solution)/shard_map/sides/pallas_call | solution.py:116
  32.2 0.1 collective-permute-start.16
  32.3 3.1 %collective-permute-start.13 = (f32[64,768]{1,0:T(8,128)S(1)}, f32[64,768]{1,0:T(8,128)S(1)}, u32[]{:S(2)}, u32[]{:S(2)}) collective-permute-start(f32[64,768]{1,0:T(8,128)S(1)} %get-tuple-element.86), channel_id=1, source_target_pairs={{0,8},{8,0},{16,24},{24,16},{1,9},{9,1},{17,25},{25,17},{2,10},{10... | collective-permute-start | bytes 589832 | tf_op jit(solution)/shard_map/ppermute | solution.py:457
  35.5 0.1 finish.5
  35.6 0.1 collective-permute-start.15
  35.7 1.7 %collective-permute-start.12 = (f32[64,768]{1,0:T(8,128)S(1)}, f32[64,768]{1,0:T(8,128)S(1)}, u32[]{:S(2)}, u32[]{:S(2)}) collective-permute-start(f32[64,768]{1,0:T(8,128)S(1)} %get-tuple-element.85), channel_id=1, source_target_pairs={{0,8},{8,0},{16,24},{24,16},{1,9},{9,1},{17,25},{25,17},{2,10},{10... | collective-permute-start | bytes 589832 | tf_op jit(solution)/shard_map/ppermute | solution.py:457
  37.4 0.1 finish.6
  37.5 3.0 %collective-permute-done.13.refs_1_ = f32[64,768]{1,0:T(8,128)S(1)} collective-permute-done((f32[64,768]{1,0:T(8,128)S(1)}, f32[64,768]{1,0:T(8,128)S(1)}, u32[]{:S(2)}, u32[]{:S(2)}) %collective-permute-start.13) | collective-permute-done | bytes 196640 | tf_op jit(solution)/shard_map/ppermute | solution.py:457
  40.5 0.1 collective-permute-start.18
  40.6 3.2 %collective-permute-start.19 = (f32[64,768]{1,0:T(8,128)S(1)}, f32[64,768]{1,0:T(8,128)S(1)}, u32[]{:S(2)}, u32[]{:S(2)}) collective-permute-start(f32[64,768]{1,0:T(8,128)S(1)} %get-tuple-element.101), channel_id=1, source_target_pairs={{0,8},{8,0},{16,24},{24,16},{1,9},{9,1},{17,25},{25,17},{2,10},{10... | collective-permute-start | bytes 589832 | tf_op jit(solution)/shard_map/ppermute | solution.py:457
  43.9 0.1 finish.7
  43.9 0.2 collective-permute-done.12.refs_1_
  44.1 0.1 collective-permute-start.17
  44.2 3.0 %collective-permute-start.25 = (f32[64,768]{1,0:T(8,128)S(1)}, f32[64,768]{1,0:T(8,128)S(1)}, u32[]{:S(2)}, u32[]{:S(2)}) collective-permute-start(f32[64,768]{1,0:T(8,128)S(1)} %get-tuple-element.108), channel_id=1, source_target_pairs={{0,8},{8,0},{16,24},{24,16},{1,9},{9,1},{17,25},{25,17},{2,10},{10... | collective-permute-start | bytes 589832 | tf_op jit(solution)/shard_map/ppermute | solution.py:457
  47.2 3.3 %collective-permute-start.26 = (f32[64,768]{1,0:T(8,128)S(1)}, f32[64,768]{1,0:T(8,128)S(1)}, u32[]{:S(2)}, u32[]{:S(2)}) collective-permute-start(f32[64,768]{1,0:T(8,128)S(1)} %get-tuple-element.112), channel_id=1, source_target_pairs={{0,8},{8,0},{16,24},{24,16},{1,9},{9,1},{17,25},{25,17},{2,10},{10... | collective-permute-start | bytes 589832 | tf_op jit(solution)/shard_map/ppermute | solution.py:457
  50.6 0.1 finish.8
  50.7 0.1 finish.9
  50.8 1.6 %collective-permute-start.20 = (f32[8,128]{1,0:T(8,128)S(1)}, f32[8,128]{1,0:T(8,128)S(1)}, u32[]{:S(2)}, u32[]{:S(2)}) collective-permute-start(f32[8,128]{1,0:T(8,128)S(1)} %get-tuple-element.107), channel_id=1, source_target_pairs={{0,1},{1,0},{2,3},{3,2},{4,5},{5,4},{6,7},{7,6},{8,9},{9,8},{10,11... | collective-permute-start | bytes 12296 | tf_op jit(solution)/shard_map/ppermute | solution.py:514
  52.4 1.8 %collective-permute-start.27 = (f32[64,768]{1,0:T(8,128)S(1)}, f32[64,768]{1,0:T(8,128)S(1)}, u32[]{:S(2)}, u32[]{:S(2)}) collective-permute-start(f32[64,768]{1,0:T(8,128)S(1)} %get-tuple-element.115), channel_id=1, source_target_pairs={{0,8},{8,0},{16,24},{24,16},{1,9},{9,1},{17,25},{25,17},{2,10},{10... | collective-permute-start | bytes 589832 | tf_op jit(solution)/shard_map/ppermute | solution.py:457
  54.2 0.3 collective-permute-done.20
  54.5 0.1 finish_last.3
  54.6 1.1 %collective-permute-done.21 = f32[8,128]{1,0:T(8,128)S(1)} collective-permute-done((f32[8,128]{1,0:T(8,128)S(1)}, f32[8,128]{1,0:T(8,128)S(1)}, u32[]{:S(2)}, u32[]{:S(2)}) %collective-permute-start.21) | collective-permute-done | bytes 4128 | tf_op jit(solution)/shard_map/ppermute | solution.py:515
  55.7 2.0 %collective-permute-start.22 = (f32[8,128]{1,0:T(8,128)S(1)}, f32[8,128]{1,0:T(8,128)S(1)}, u32[]{:S(2)}, u32[]{:S(2)}) collective-permute-start(f32[8,128]{1,0:T(8,128)S(1)} %add.15.refs_0_), channel_id=1, source_target_pairs={{0,12},{2,14},{4,8},{6,10},{8,4},{10,6},{12,0},{14,2},{16,28},{18,... | collective-permute-start | bytes 12296 | tf_op jit(solution)/shard_map/ppermute | solution.py:519
  57.6 1.5 %collective-permute-start.24 = (f32[8,128]{1,0:T(8,128)S(1)}, f32[8,128]{1,0:T(8,128)S(1)}, u32[]{:S(2)}, u32[]{:S(2)}) collective-permute-start(f32[8,128]{1,0:T(8,128)S(1)} %add.15.refs_0_), channel_id=1, source_target_pairs={{0,4},{2,6},{4,0},{6,2},{1,5},{3,7},{5,1},{7,3},{8,12},{10,14},{12... | collective-permute-start | bytes 12296 | tf_op jit(solution)/shard_map/ppermute | solution.py:521
  59.2 0.1 finish_last.4
  59.2 1.5 %collective-permute-done.27.refs_1_ = f32[64,768]{1,0:T(8,128)S(1)} collective-permute-done((f32[64,768]{1,0:T(8,128)S(1)}, f32[64,768]{1,0:T(8,128)S(1)}, u32[]{:S(2)}, u32[]{:S(2)}) %collective-permute-start.27) | collective-permute-done | bytes 196640 | tf_op jit(solution)/shard_map/ppermute | solution.py:457
  60.8 0.6 %collective-permute-done.22.refs_1_ = f32[8,128]{1,0:T(8,128)S(1)} collective-permute-done((f32[8,128]{1,0:T(8,128)S(1)}, f32[8,128]{1,0:T(8,128)S(1)}, u32[]{:S(2)}, u32[]{:S(2)}) %collective-permute-start.22) | collective-permute-done | bytes 4128 | tf_op jit(solution)/shard_map/ppermute | solution.py:519
  61.5 1.9 %assemble.1 = (f32[384,1024]{1,0:T(8,128)}, f32[1,384,1024]{2,1,0:T(8,128)}) custom-call(f32[8,128]{1,0:T(8,128)S(1)} %add.15.refs_0_, f32[8,128]{1,0:T(8,128)S(1)} %collective-permute-done.22.refs_1_, f32[8,128]{1,0:T(8,128)S(1)} %collective-permute-done.23.refs_2_, f32[8,128]{1,0:T(8,128)S(1)} %collective-permute-done.24.refs_3_, ...), custom_call_target="tpu_custom_call" | custom-call | tf_op jit(solution)/shard_map/assemble/pallas_call | solution.py:116
  (40 shorter events, 0.8 us)
Async XLA Ops:
  4.2 3.2 %collective-permute-start = (f32[96,1024]{1,0:T(8,128)S(1)}, f32[96,1024]{1,0:T(8,128)S(1)}, u32[]{:S(2)}, u32[]{:S(2)}) collective-permute-start(f32[96,1024]{1,0:T(8,128)S(1)} %get-tuple-element.67), channel_id=1, source_target_pairs={{0,2},{2,0},{4,6},{6,4},{1,3},{3,1},{5,7},{7,5},{8,10},{10,8},{12,... | collective-permute-start | bytes 1179656 | tf_op jit(solution)/shard_map/ppermute | solution.py:484
  4.7 8.4 %collective-permute-start.2 = (f32[64,768]{1,0:T(8,128)S(1)}, f32[64,768]{1,0:T(8,128)S(1)}, u32[]{:S(2)}, u32[]{:S(2)}) collective-permute-start(f32[64,768]{1,0:T(8,128)S(1)} %get-tuple-element.70.refs_0_), channel_id=1, source_target_pairs={{0,8},{8,0},{16,24},{24,16},{1,9},{9,1},{17,25},{25,17},{2,10},{10... | collective-permute-start | bytes 589832 | tf_op jit(solution)/shard_map/ppermute | solution.py:457
  9.7 7.5 %collective-permute-start.4 = (f32[64,768]{1,0:T(8,128)S(1)}, f32[64,768]{1,0:T(8,128)S(1)}, u32[]{:S(2)}, u32[]{:S(2)}) collective-permute-start(f32[64,768]{1,0:T(8,128)S(1)} %get-tuple-element.71.refs_2_.refs_0_), channel_id=1, source_target_pairs={{0,8},{8,0},{16,24},{24,16},{1,9},{9,1},{17,25},{25,17},{2,10},{10... | collective-permute-start | bytes 589832 | tf_op jit(solution)/shard_map/ppermute | solution.py:457
  11.4 7.8 %collective-permute-start.1 = (f32[96,1024]{1,0:T(8,128)S(1)}, f32[96,1024]{1,0:T(8,128)S(1)}, u32[]{:S(2)}, u32[]{:S(2)}) collective-permute-start(f32[96,1024]{1,0:T(8,128)S(1)} %get-tuple-element.69), channel_id=1, source_target_pairs={{0,1},{1,0},{2,4},{3,5},{4,2},{5,3},{6,7},{7,6},{8,9},{9,8},{10,12... | collective-permute-start | bytes 1179656 | tf_op jit(solution)/shard_map/ppermute | solution.py:489
  13.2 8.3 %collective-permute-start.3 = (f32[64,768]{1,0:T(8,128)S(1)}, f32[64,768]{1,0:T(8,128)S(1)}, u32[]{:S(2)}, u32[]{:S(2)}) collective-permute-start(f32[64,768]{1,0:T(8,128)S(1)} %add.16.refs_2_.refs_0_), channel_id=1, source_target_pairs={{8,16},{16,8},{0,2},{24,26},{10,18},{18,10},{2,0},{26,24},{12,20},... | collective-permute-start | bytes 589832 | tf_op jit(solution)/shard_map/ppermute | solution.py:462
  13.2 10.1 %collective-permute-start.8 = (f32[64,768]{1,0:T(8,128)S(1)}, f32[64,768]{1,0:T(8,128)S(1)}, u32[]{:S(2)}, u32[]{:S(2)}) collective-permute-start(f32[64,768]{1,0:T(8,128)S(1)} %get-tuple-element.77.refs_0_), channel_id=1, source_target_pairs={{0,8},{8,0},{16,24},{24,16},{1,9},{9,1},{17,25},{25,17},{2,10},{10... | collective-permute-start | bytes 589832 | tf_op jit(solution)/shard_map/ppermute | solution.py:457
  16.7 9.9 %collective-permute-start.6 = (f32[64,768]{1,0:T(8,128)S(1)}, f32[64,768]{1,0:T(8,128)S(1)}, u32[]{:S(2)}, u32[]{:S(2)}) collective-permute-start(f32[64,768]{1,0:T(8,128)S(1)} %get-tuple-element.74.refs_0_), channel_id=1, source_target_pairs={{0,8},{8,0},{16,24},{24,16},{1,9},{9,1},{17,25},{25,17},{2,10},{10... | collective-permute-start | bytes 589832 | tf_op jit(solution)/shard_map/ppermute | solution.py:457
  17.2 9.3 %collective-permute-start.7 = (f32[64,768]{1,0:T(8,128)S(1)}, f32[64,768]{1,0:T(8,128)S(1)}, u32[]{:S(2)}, u32[]{:S(2)}) collective-permute-start(f32[64,768]{1,0:T(8,128)S(1)} %add.17.refs_7_.refs_0_), channel_id=1, source_target_pairs={{8,16},{16,8},{0,2},{24,26},{10,18},{18,10},{2,0},{26,24},{12,20},... | collective-permute-start | bytes 589832 | tf_op jit(solution)/shard_map/ppermute | solution.py:462
  21.7 7.9 %collective-permute-start.5 = (f32[512,128]{1,0:T(8,128)S(1)}, f32[512,128]{1,0:T(8,128)S(1)}, u32[]{:S(2)}, u32[]{:S(2)}) collective-permute-start(f32[512,128]{1,0:T(8,128)S(1)} %side_pack.1.refs_2_), channel_id=1, source_target_pairs={{0,1},{1,0},{2,3},{3,2},{4,5},{5,4},{6,7},{7,6},{8,9},{9,8},{10,11... | collective-permute-start | bytes 786440 | tf_op jit(solution)/shard_map/ppermute | solution.py:497
  23.3 8.8 %collective-permute-start.10 = (f32[64,768]{1,0:T(8,128)S(1)}, f32[64,768]{1,0:T(8,128)S(1)}, u32[]{:S(2)}, u32[]{:S(2)}) collective-permute-start(f32[64,768]{1,0:T(8,128)S(1)} %add.18.refs_4_.refs_0_), channel_id=1, source_target_pairs={{8,16},{16,8},{0,2},{24,26},{10,18},{18,10},{2,0},{26,24},{12,20},... | collective-permute-start | bytes 589832 | tf_op jit(solution)/shard_map/ppermute | solution.py:462
  23.4 8.8 %collective-permute-start.11 = (f32[64,768]{1,0:T(8,128)S(1)}, f32[64,768]{1,0:T(8,128)S(1)}, u32[]{:S(2)}, u32[]{:S(2)}) collective-permute-start(f32[64,768]{1,0:T(8,128)S(1)} %get-tuple-element.83), channel_id=1, source_target_pairs={{0,8},{8,0},{16,24},{24,16},{1,9},{9,1},{17,25},{25,17},{2,10},{10... | collective-permute-start | bytes 589832 | tf_op jit(solution)/shard_map/ppermute | solution.py:457
  26.6 8.8 %collective-permute-start.9 = (f32[64,768]{1,0:T(8,128)S(1)}, f32[64,768]{1,0:T(8,128)S(1)}, u32[]{:S(2)}, u32[]{:S(2)}) collective-permute-start(f32[64,768]{1,0:T(8,128)S(1)} %add.19.refs_8_.refs_0_), channel_id=1, source_target_pairs={{8,16},{16,8},{0,2},{24,26},{10,18},{18,10},{2,0},{26,24},{12,20},... | collective-permute-start | bytes 589832 | tf_op jit(solution)/shard_map/ppermute | solution.py:462
  26.7 8.9 %collective-permute-start.14 = (f32[64,768]{1,0:T(8,128)S(1)}, f32[64,768]{1,0:T(8,128)S(1)}, u32[]{:S(2)}, u32[]{:S(2)}) collective-permute-start(f32[64,768]{1,0:T(8,128)S(1)} %get-tuple-element.88), channel_id=1, source_target_pairs={{0,8},{8,0},{16,24},{24,16},{1,9},{9,1},{17,25},{25,17},{2,10},{10... | collective-permute-start | bytes 589832 | tf_op jit(solution)/shard_map/ppermute | solution.py:457
  32.2 5.2 %collective-permute-start.16 = (f32[64,768]{1,0:T(8,128)S(1)}, f32[64,768]{1,0:T(8,128)S(1)}, u32[]{:S(2)}, u32[]{:S(2)}) collective-permute-start(f32[64,768]{1,0:T(8,128)S(1)} %add.20.refs_4_.refs_0_), channel_id=1, source_target_pairs={{8,16},{16,8},{0,2},{24,26},{10,18},{18,10},{2,0},{26,24},{12,20},... | collective-permute-start | bytes 589832 | tf_op jit(solution)/shard_map/ppermute | solution.py:462
  32.3 8.2 %collective-permute-start.13 = (f32[64,768]{1,0:T(8,128)S(1)}, f32[64,768]{1,0:T(8,128)S(1)}, u32[]{:S(2)}, u32[]{:S(2)}) collective-permute-start(f32[64,768]{1,0:T(8,128)S(1)} %get-tuple-element.86), channel_id=1, source_target_pairs={{0,8},{8,0},{16,24},{24,16},{1,9},{9,1},{17,25},{25,17},{2,10},{10... | collective-permute-start | bytes 589832 | tf_op jit(solution)/shard_map/ppermute | solution.py:457
  35.6 8.2 %collective-permute-start.15 = (f32[64,768]{1,0:T(8,128)S(1)}, f32[64,768]{1,0:T(8,128)S(1)}, u32[]{:S(2)}, u32[]{:S(2)}) collective-permute-start(f32[64,768]{1,0:T(8,128)S(1)} %add.21.refs_4_.refs_0_), channel_id=1, source_target_pairs={{8,16},{16,8},{0,2},{24,26},{10,18},{18,10},{2,0},{26,24},{12,20},... | collective-permute-start | bytes 589832 | tf_op jit(solution)/shard_map/ppermute | solution.py:462
  35.7 8.4 %collective-permute-start.12 = (f32[64,768]{1,0:T(8,128)S(1)}, f32[64,768]{1,0:T(8,128)S(1)}, u32[]{:S(2)}, u32[]{:S(2)}) collective-permute-start(f32[64,768]{1,0:T(8,128)S(1)} %get-tuple-element.85), channel_id=1, source_target_pairs={{0,8},{8,0},{16,24},{24,16},{1,9},{9,1},{17,25},{25,17},{2,10},{10... | collective-permute-start | bytes 589832 | tf_op jit(solution)/shard_map/ppermute | solution.py:457
  40.5 6.7 %collective-permute-start.18 = (f32[64,768]{1,0:T(8,128)S(1)}, f32[64,768]{1,0:T(8,128)S(1)}, u32[]{:S(2)}, u32[]{:S(2)}) collective-permute-start(f32[64,768]{1,0:T(8,128)S(1)} %add.22.refs_4_.refs_0_), channel_id=1, source_target_pairs={{8,16},{16,8},{0,2},{24,26},{10,18},{18,10},{2,0},{26,24},{12,20},... | collective-permute-start | bytes 589832 | tf_op jit(solution)/shard_map/ppermute | solution.py:462
  40.6 10.1 %collective-permute-start.19 = (f32[64,768]{1,0:T(8,128)S(1)}, f32[64,768]{1,0:T(8,128)S(1)}, u32[]{:S(2)}, u32[]{:S(2)}) collective-permute-start(f32[64,768]{1,0:T(8,128)S(1)} %get-tuple-element.101), channel_id=1, source_target_pairs={{0,8},{8,0},{16,24},{24,16},{1,9},{9,1},{17,25},{25,17},{2,10},{10... | collective-permute-start | bytes 589832 | tf_op jit(solution)/shard_map/ppermute | solution.py:457
  44.1 6.6 %collective-permute-start.17 = (f32[64,768]{1,0:T(8,128)S(1)}, f32[64,768]{1,0:T(8,128)S(1)}, u32[]{:S(2)}, u32[]{:S(2)}) collective-permute-start(f32[64,768]{1,0:T(8,128)S(1)} %add.23.refs_4_.refs_0_), channel_id=1, source_target_pairs={{8,16},{16,8},{0,2},{24,26},{10,18},{18,10},{2,0},{26,24},{12,20},... | collective-permute-start | bytes 589832 | tf_op jit(solution)/shard_map/ppermute | solution.py:462
  44.2 10.3 %collective-permute-start.25 = (f32[64,768]{1,0:T(8,128)S(1)}, f32[64,768]{1,0:T(8,128)S(1)}, u32[]{:S(2)}, u32[]{:S(2)}) collective-permute-start(f32[64,768]{1,0:T(8,128)S(1)} %get-tuple-element.108), channel_id=1, source_target_pairs={{0,8},{8,0},{16,24},{24,16},{1,9},{9,1},{17,25},{25,17},{2,10},{10... | collective-permute-start | bytes 589832 | tf_op jit(solution)/shard_map/ppermute | solution.py:457
  47.2 11.9 %collective-permute-start.26 = (f32[64,768]{1,0:T(8,128)S(1)}, f32[64,768]{1,0:T(8,128)S(1)}, u32[]{:S(2)}, u32[]{:S(2)}) collective-permute-start(f32[64,768]{1,0:T(8,128)S(1)} %get-tuple-element.112), channel_id=1, source_target_pairs={{0,8},{8,0},{16,24},{24,16},{1,9},{9,1},{17,25},{25,17},{2,10},{10... | collective-permute-start | bytes 589832 | tf_op jit(solution)/shard_map/ppermute | solution.py:457
  50.8 3.7 %collective-permute-start.20 = (f32[8,128]{1,0:T(8,128)S(1)}, f32[8,128]{1,0:T(8,128)S(1)}, u32[]{:S(2)}, u32[]{:S(2)}) collective-permute-start(f32[8,128]{1,0:T(8,128)S(1)} %get-tuple-element.107), channel_id=1, source_target_pairs={{0,1},{1,0},{2,3},{3,2},{4,5},{5,4},{6,7},{7,6},{8,9},{9,8},{10,11... | collective-permute-start | bytes 12296 | tf_op jit(solution)/shard_map/ppermute | solution.py:514
  52.4 8.3 %collective-permute-start.27 = (f32[64,768]{1,0:T(8,128)S(1)}, f32[64,768]{1,0:T(8,128)S(1)}, u32[]{:S(2)}, u32[]{:S(2)}) collective-permute-start(f32[64,768]{1,0:T(8,128)S(1)} %get-tuple-element.115), channel_id=1, source_target_pairs={{0,8},{8,0},{16,24},{24,16},{1,9},{9,1},{17,25},{25,17},{2,10},{10... | collective-permute-start | bytes 589832 | tf_op jit(solution)/shard_map/ppermute | solution.py:457
  54.5 1.2 %collective-permute-start.21 = (f32[8,128]{1,0:T(8,128)S(1)}, f32[8,128]{1,0:T(8,128)S(1)}, u32[]{:S(2)}, u32[]{:S(2)}) collective-permute-start(f32[8,128]{1,0:T(8,128)S(1)} %add.14), channel_id=1, source_target_pairs={{0,2},{2,0},{4,6},{6,4},{1,3},{3,1},{5,7},{7,5},{8,10},{10,8},{12,... | collective-permute-start | bytes 12296 | tf_op jit(solution)/shard_map/ppermute | solution.py:515
  55.7 5.8 %collective-permute-start.22 = (f32[8,128]{1,0:T(8,128)S(1)}, f32[8,128]{1,0:T(8,128)S(1)}, u32[]{:S(2)}, u32[]{:S(2)}) collective-permute-start(f32[8,128]{1,0:T(8,128)S(1)} %add.15.refs_0_), channel_id=1, source_target_pairs={{0,12},{2,14},{4,8},{6,10},{8,4},{10,6},{12,0},{14,2},{16,28},{18,... | collective-permute-start | bytes 12296 | tf_op jit(solution)/shard_map/ppermute | solution.py:519
  57.6 3.8 %collective-permute-start.23 = (f32[8,128]{1,0:T(8,128)S(1)}, f32[8,128]{1,0:T(8,128)S(1)}, u32[]{:S(2)}, u32[]{:S(2)}) collective-permute-start(f32[8,128]{1,0:T(8,128)S(1)} %add.15.refs_0_), channel_id=1, source_target_pairs={{0,8},{8,0},{16,24},{24,16},{1,9},{9,1},{17,25},{25,17},{2,10},{10... | collective-permute-start | bytes 12296 | tf_op jit(solution)/shard_map/ppermute | solution.py:520
  57.6 3.8 %collective-permute-start.24 = (f32[8,128]{1,0:T(8,128)S(1)}, f32[8,128]{1,0:T(8,128)S(1)}, u32[]{:S(2)}, u32[]{:S(2)}) collective-permute-start(f32[8,128]{1,0:T(8,128)S(1)} %add.15.refs_0_), channel_id=1, source_target_pairs={{0,4},{2,6},{4,0},{6,2},{1,5},{3,7},{5,1},{7,3},{8,12},{10,14},{12... | collective-permute-start | bytes 12296 | tf_op jit(solution)/shard_map/ppermute | solution.py:521

commit v8 on v5

--- a/solution.py
+++ b/solution.py
@@ -41,7 +41,9 @@
 
 def times(left, right):
     (lh, ll), (rh, rl) = left, right
-    return mm(jnp.concatenate([lh, lh, ll], axis=1), jnp.concatenate([rh, rl, rh], axis=0))
+    n = lh.shape[0]
+    both = mm(jnp.concatenate([lh, ll], axis=0), rh)
+    return both[:n] + both[n:] + mm(lh, rl)
 
 
 def part(pair, rows=slice(None), cols=slice(None)):
@@ -386,7 +388,7 @@
         total = mass[0][...]
         if m > 1:
             total = jnp.where(in_middle(), total + mass[3][...], mass[2][...] + mass[1][...])
-        scale = cells / jnp.sum(total)
+        scale = cells / jnp.sum(jnp.sum(total, axis=0, keepdims=True), axis=1, keepdims=True)
         copies = []
         for row in range(0, rows, WIDE):
             band_rows = pl.ds(row, WIDE)

time: 63.6 us -> 63.5 us (level)
    ppermute x1, waiting for transfers between devices: 0.28 us -> 1.1 us  [local(): own = mass[0] + lax.ppermute(mass[0], 'gy', [(0, 1), (1, 0)])]
    ppermute x1, starting transfers between devices: 0.85 us -> 0.07 us  [local(): own = mass[0] + lax.ppermute(mass[0], 'gy', [(0, 1), (1, 0)])]
    ppermute x12, starting transfers between devices: 29.8 us -> 30.5 us  [outward(): got[k] = lax.ppermute(value, 'map', outer)]
    ppermute x1, starting transfers between devices: 2.98 us -> 2.34 us  [local(): lax.ppermute(own, ('map', 'gx'), swap)]
  transfers between devices with their start and end apart: 28 -> 28, of which waited for: 10 -> 10; matrix products, arithmetic and copies ran while one was open for 0% -> 0% of each run, Pallas kernels for 13% -> 14%
where the time goes in v8:
time: 63.5 us; the launch traced here: 63.4 us
  starting transfers between devices  38.3 us (60%)
  Pallas kernels  13.4 us (21%)
  waiting for transfers between devices  10.1 us (16%)
  between operations  1.55 us (2%)
    ppermute x12, starting transfers between devices, outward(): got[k] = lax.ppermute(value, 'map', outer)  30.5 us
    pallas_call x30, Pallas kernels, call(): return lambda *args: kernel(*args, *deps)  13.4 us
    ppermute x12, waiting for transfers between devices, outward(): got[k] = lax.ppermute(value, 'map', outer)  4.82 us
    ppermute x1, starting transfers between devices, local(): lax.ppermute(own, ('map', 'gx'), swap)  2.34 us
    ppermute x1, waiting for transfers between devices, local(): two = lax.ppermute(two, ('gx', 'gy'), far)  2.14 us
    ppermute x1, starting transfers between devices, local(): from_left = from_right = lax.ppermute(packs[0], 'gy', [(0, 1), (1, 0)])  1.59 us
    ppermute x1, starting transfers between devices, local(): two = lax.ppermute(two, ('gx', 'gy'), far)  1.52 us
  transfers between devices with their start and end apart: 28, of which 10 were waited for; matrix products, arithmetic and copies ran while one was open for 0% of the time, Pallas kernels for 14%

profile of v8, /device:TPU:0, one launch (start us, length us, event | category | flops | bytes accessed | tf_op | source)
XLA Modules:
  0.0 63.4 jit_solution(424788681030687600)
XLA Ops:
  1.3 2.9 %first.1 = (f32[64,768]{1,0:T(8,128)S(1)}, f32[64,768]{1,0:T(8,128)S(1)}, bf16[2,192,256]{2,1,0:T(8,128)(2,1)S(1)}, bf16[2,512,256]{2,1,0:T(8,128)(2,1)S(1)}, f3...) custom-call(f32[1]{0:T(128)S(6)} %copy.5.refs_0_, f32[1,384,1024]{2,1,0:T(8,128)} %refs_1_.1, ...), custom_call_target="tpu_custom_call" | custom-call | tf_op jit(solution)/shard_map/first/pallas_call | solution.py:118
  4.2 0.5 collective-permute-start
  4.7 2.6 %collective-permute-start.3 = (f32[64,768]{1,0:T(8,128)S(1)}, f32[64,768]{1,0:T(8,128)S(1)}, u32[]{:S(2)}, u32[]{:S(2)}) collective-permute-start(f32[64,768]{1,0:T(8,128)S(1)} %get-tuple-element.71.refs_0_), channel_id=1, source_target_pairs={{0,8},{8,0},{16,24},{24,16},{1,9},{9,1},{17,25},{25,17},{2,10},{10... | collective-permute-start | bytes 589832 | tf_op jit(solution)/shard_map/ppermute | solution.py:461
  7.3 2.5 %inner.1 = (f32[64,768]{1,0:T(8,128)S(1)}, f32[64,768]{1,0:T(8,128)S(1)}, f32[64,768]{1,0:T(8,128)S(1)}, f32[64,768]{1,0:T(8,128)S(1)}, f32[64,768]{1,0:T(8,128)...) custom-call(f32[1]{0:T(128)S(6)} %copy.5.refs_0_, f32[1,384,1024]{2,1,0:T(8,128)S(1)} %get-tuple-element.64.refs_1_.refs_0_, ...), custom_call_target="tpu_custom_call" | custom-call | flops 2500000000 | tf_op jit(solution)/shard_map/inner/pallas_call | solution.py:118
  9.8 1.7 %collective-permute-start.2 = (f32[64,768]{1,0:T(8,128)S(1)}, f32[64,768]{1,0:T(8,128)S(1)}, u32[]{:S(2)}, u32[]{:S(2)}) collective-permute-start(f32[64,768]{1,0:T(8,128)S(1)} %get-tuple-element.70.refs_2_.refs_0_), channel_id=1, source_target_pairs={{0,8},{8,0},{16,24},{24,16},{1,9},{9,1},{17,25},{25,17},{2,10},{10... | collective-permute-start | bytes 589832 | tf_op jit(solution)/shard_map/ppermute | solution.py:461
  11.5 1.5 %collective-permute-start.1 = (f32[96,1024]{1,0:T(8,128)S(1)}, f32[96,1024]{1,0:T(8,128)S(1)}, u32[]{:S(2)}, u32[]{:S(2)}) collective-permute-start(f32[96,1024]{1,0:T(8,128)S(1)} %get-tuple-element.69), channel_id=1, source_target_pairs={{0,1},{1,0},{2,4},{3,5},{4,2},{5,3},{6,7},{7,6},{8,9},{9,8},{10,12... | collective-permute-start | bytes 1179656 | tf_op jit(solution)/shard_map/ppermute | solution.py:493
  13.1 0.2 collective-permute-start.7
  13.2 3.3 %collective-permute-start.8 = (f32[64,768]{1,0:T(8,128)S(1)}, f32[64,768]{1,0:T(8,128)S(1)}, u32[]{:S(2)}, u32[]{:S(2)}) collective-permute-start(f32[64,768]{1,0:T(8,128)S(1)} %get-tuple-element.76.refs_0_), channel_id=1, source_target_pairs={{0,8},{8,0},{16,24},{24,16},{1,9},{9,1},{17,25},{25,17},{2,10},{10... | collective-permute-start | bytes 589832 | tf_op jit(solution)/shard_map/ppermute | solution.py:461
  16.6 0.5 collective-permute-done.2.refs_1_
  17.1 0.1 collective-permute-start.6
  17.2 2.1 %collective-permute-done.1.refs_3_.refs_6_.refs_5_ = f32[96,1024]{1,0:T(8,128)S(1)} collective-permute-done((f32[96,1024]{1,0:T(8,128)S(1)}, f32[96,1024]{1,0:T(8,128)S(1)}, u32[]{:S(2)}, u32[]{:S(2)}) %collective-permute-start.1) | collective-permute-done | bytes 393248 | tf_op jit(solution)/shard_map/ppermute | solution.py:493
  19.3 0.2 side_pack.1.refs_7_
  19.5 1.6 %collective-permute-start.4 = (f32[512,128]{1,0:T(8,128)S(1)}, f32[512,128]{1,0:T(8,128)S(1)}, u32[]{:S(2)}, u32[]{:S(2)}) collective-permute-start(f32[512,128]{1,0:T(8,128)S(1)} %side_pack.1.refs_7_), channel_id=1, source_target_pairs={{0,1},{1,0},{2,3},{3,2},{4,5},{5,4},{6,7},{7,6},{8,9},{9,8},{10,11... | collective-permute-start | bytes 786440 | tf_op jit(solution)/shard_map/ppermute | solution.py:499
  21.1 2.3 %edges.1 = (f32[64,768]{1,0:T(8,128)S(1)}, f32[64,768]{1,0:T(8,128)S(1)}, f32[64,768]{1,0:T(8,128)S(1)}, f32[64,768]{1,0:T(8,128)S(1)}) custom-call(f32[1]{0:T(128)S(6)} %copy.5.refs_0_, f32[1,384,1024]{2,1,0:T(8,128)S(1)} %get-tuple-element.64.refs_1_.refs_0_, f32[1,384,1024]{2,1,0:T(8,128)S(1)} %get-tuple-element.65.refs_2_.refs_1_, ...), custom_call_target="tpu_custom_call" | custom-call | flops 2300000000 | tf_op jit(solution)/shard_map/edges/pallas_call | solution.py:118
  23.5 0.1 collective-permute-start.10
  23.6 3.1 %collective-permute-start.11 = (f32[64,768]{1,0:T(8,128)S(1)}, f32[64,768]{1,0:T(8,128)S(1)}, u32[]{:S(2)}, u32[]{:S(2)}) collective-permute-start(f32[64,768]{1,0:T(8,128)S(1)} %get-tuple-element.83), channel_id=1, source_target_pairs={{0,8},{8,0},{16,24},{24,16},{1,9},{9,1},{17,25},{25,17},{2,10},{10... | collective-permute-start | bytes 589832 | tf_op jit(solution)/shard_map/ppermute | solution.py:461
  26.9 0.1 collective-permute-start.9
  26.9 2.0 %collective-permute-start.14 = (f32[64,768]{1,0:T(8,128)S(1)}, f32[64,768]{1,0:T(8,128)S(1)}, u32[]{:S(2)}, u32[]{:S(2)}) collective-permute-start(f32[64,768]{1,0:T(8,128)S(1)} %get-tuple-element.88), channel_id=1, source_target_pairs={{0,8},{8,0},{16,24},{24,16},{1,9},{9,1},{17,25},{25,17},{2,10},{10... | collective-permute-start | bytes 589832 | tf_op jit(solution)/shard_map/ppermute | solution.py:461
  28.9 2.4 %sides.1 = (f32[64,768]{1,0:T(8,128)S(1)}, f32[64,768]{1,0:T(8,128)S(1)}, f32[64,768]{1,0:T(8,128)S(1)}, f32[64,768]{1,0:T(8,128)S(1)}) custom-call(f32[1]{0:T(128)S(6)} %copy.5.refs_0_, f32[1,384,1024]{2,1,0:T(8,128)S(1)} %get-tuple-element.64.refs_1_.refs_0_, f32[1,384,1024]{2,1,0:T(8,128)S(1)} %get-tuple-element.65.refs_2_.refs_1_, ...), custom_call_target="tpu_custom_call" | custom-call | flops 2500000000 | tf_op jit(solution)/shard_map/sides/pallas_call | solution.py:118
  31.4 0.5 collective-permute-done.11.refs_1_
  32.0 0.1 collective-permute-start.16
  32.0 2.7 %collective-permute-start.13 = (f32[64,768]{1,0:T(8,128)S(1)}, f32[64,768]{1,0:T(8,128)S(1)}, u32[]{:S(2)}, u32[]{:S(2)}) collective-permute-start(f32[64,768]{1,0:T(8,128)S(1)} %get-tuple-element.86), channel_id=1, source_target_pairs={{0,8},{8,0},{16,24},{24,16},{1,9},{9,1},{17,25},{25,17},{2,10},{10... | collective-permute-start | bytes 589832 | tf_op jit(solution)/shard_map/ppermute | solution.py:461
  34.8 0.1 finish.5
  34.9 0.5 collective-permute-done.14.refs_1_
  35.4 0.1 collective-permute-start.15
  35.5 2.9 %collective-permute-start.12 = (f32[64,768]{1,0:T(8,128)S(1)}, f32[64,768]{1,0:T(8,128)S(1)}, u32[]{:S(2)}, u32[]{:S(2)}) collective-permute-start(f32[64,768]{1,0:T(8,128)S(1)} %get-tuple-element.85), channel_id=1, source_target_pairs={{0,8},{8,0},{16,24},{24,16},{1,9},{9,1},{17,25},{25,17},{2,10},{10... | collective-permute-start | bytes 589832 | tf_op jit(solution)/shard_map/ppermute | solution.py:461
  38.4 0.1 finish.6
  38.5 1.6 %collective-permute-done.13.refs_1_ = f32[64,768]{1,0:T(8,128)S(1)} collective-permute-done((f32[64,768]{1,0:T(8,128)S(1)}, f32[64,768]{1,0:T(8,128)S(1)}, u32[]{:S(2)}, u32[]{:S(2)}) %collective-permute-start.13) | collective-permute-done | bytes 196640 | tf_op jit(solution)/shard_map/ppermute | solution.py:461
  40.1 0.1 collective-permute-start.18
  40.2 3.7 %collective-permute-start.19 = (f32[64,768]{1,0:T(8,128)S(1)}, f32[64,768]{1,0:T(8,128)S(1)}, u32[]{:S(2)}, u32[]{:S(2)}) collective-permute-start(f32[64,768]{1,0:T(8,128)S(1)} %get-tuple-element.101), channel_id=1, source_target_pairs={{0,8},{8,0},{16,24},{24,16},{1,9},{9,1},{17,25},{25,17},{2,10},{10... | collective-permute-start | bytes 589832 | tf_op jit(solution)/shard_map/ppermute | solution.py:461
  44.0 0.1 finish.7
  44.1 0.3 collective-permute-done.12.refs_1_
  44.4 0.1 collective-permute-start.17
  44.4 3.4 %collective-permute-start.25 = (f32[64,768]{1,0:T(8,128)S(1)}, f32[64,768]{1,0:T(8,128)S(1)}, u32[]{:S(2)}, u32[]{:S(2)}) collective-permute-start(f32[64,768]{1,0:T(8,128)S(1)} %get-tuple-element.108), channel_id=1, source_target_pairs={{0,8},{8,0},{16,24},{24,16},{1,9},{9,1},{17,25},{25,17},{2,10},{10... | collective-permute-start | bytes 589832 | tf_op jit(solution)/shard_map/ppermute | solution.py:461
  47.9 2.5 %collective-permute-start.26 = (f32[64,768]{1,0:T(8,128)S(1)}, f32[64,768]{1,0:T(8,128)S(1)}, u32[]{:S(2)}, u32[]{:S(2)}) collective-permute-start(f32[64,768]{1,0:T(8,128)S(1)} %get-tuple-element.112), channel_id=1, source_target_pairs={{0,8},{8,0},{16,24},{24,16},{1,9},{9,1},{17,25},{25,17},{2,10},{10... | collective-permute-start | bytes 589832 | tf_op jit(solution)/shard_map/ppermute | solution.py:461
  50.4 0.1 finish.8
  50.5 0.1 finish.9
  50.6 0.1 collective-permute-start.20
  50.7 2.5 %collective-permute-start.27 = (f32[64,768]{1,0:T(8,128)S(1)}, f32[64,768]{1,0:T(8,128)S(1)}, u32[]{:S(2)}, u32[]{:S(2)}) collective-permute-start(f32[64,768]{1,0:T(8,128)S(1)} %get-tuple-element.115), channel_id=1, source_target_pairs={{0,8},{8,0},{16,24},{24,16},{1,9},{9,1},{17,25},{25,17},{2,10},{10... | collective-permute-start | bytes 589832 | tf_op jit(solution)/shard_map/ppermute | solution.py:461
  53.2 1.1 %collective-permute-done.20 = f32[8,128]{1,0:T(8,128)S(1)} collective-permute-done((f32[8,128]{1,0:T(8,128)S(1)}, f32[8,128]{1,0:T(8,128)S(1)}, u32[]{:S(2)}, u32[]{:S(2)}) %collective-permute-start.20) | collective-permute-done | bytes 4128 | tf_op jit(solution)/shard_map/ppermute | solution.py:518
  54.3 0.1 finish_last.3
  54.4 1.1 %collective-permute-done.21 = f32[8,128]{1,0:T(8,128)S(1)} collective-permute-done((f32[8,128]{1,0:T(8,128)S(1)}, f32[8,128]{1,0:T(8,128)S(1)}, u32[]{:S(2)}, u32[]{:S(2)}) %collective-permute-start.21) | collective-permute-done | bytes 4128 | tf_op jit(solution)/shard_map/ppermute | solution.py:519
  55.5 2.3 %collective-permute-start.22 = (f32[8,128]{1,0:T(8,128)S(1)}, f32[8,128]{1,0:T(8,128)S(1)}, u32[]{:S(2)}, u32[]{:S(2)}) collective-permute-start(f32[8,128]{1,0:T(8,128)S(1)} %add.15.refs_0_), channel_id=1, source_target_pairs={{0,12},{2,14},{4,8},{6,10},{8,4},{10,6},{12,0},{14,2},{16,28},{18,... | collective-permute-start | bytes 12296 | tf_op jit(solution)/shard_map/ppermute | solution.py:523
  57.8 1.1 %collective-permute-start.24 = (f32[8,128]{1,0:T(8,128)S(1)}, f32[8,128]{1,0:T(8,128)S(1)}, u32[]{:S(2)}, u32[]{:S(2)}) collective-permute-start(f32[8,128]{1,0:T(8,128)S(1)} %add.15.refs_0_), channel_id=1, source_target_pairs={{0,4},{2,6},{4,0},{6,2},{1,5},{3,7},{5,1},{7,3},{8,12},{10,14},{12... | collective-permute-start | bytes 12296 | tf_op jit(solution)/shard_map/ppermute | solution.py:525
  59.0 1.5 %collective-permute-done.27.refs_1_ = f32[64,768]{1,0:T(8,128)S(1)} collective-permute-done((f32[64,768]{1,0:T(8,128)S(1)}, f32[64,768]{1,0:T(8,128)S(1)}, u32[]{:S(2)}, u32[]{:S(2)}) %collective-permute-start.27) | collective-permute-done | bytes 196640 | tf_op jit(solution)/shard_map/ppermute | solution.py:461
  60.5 0.1 finish_last.5
  60.6 0.9 %collective-permute-done.22.refs_1_ = f32[8,128]{1,0:T(8,128)S(1)} collective-permute-done((f32[8,128]{1,0:T(8,128)S(1)}, f32[8,128]{1,0:T(8,128)S(1)}, u32[]{:S(2)}, u32[]{:S(2)}) %collective-permute-start.22) | collective-permute-done | bytes 4128 | tf_op jit(solution)/shard_map/ppermute | solution.py:523
  61.5 1.9 %assemble.1 = (f32[384,1024]{1,0:T(8,128)}, f32[1,384,1024]{2,1,0:T(8,128)}) custom-call(f32[8,128]{1,0:T(8,128)S(1)} %add.15.refs_0_, f32[8,128]{1,0:T(8,128)S(1)} %collective-permute-done.22.refs_1_, f32[8,128]{1,0:T(8,128)S(1)} %collective-permute-done.23.refs_2_, f32[8,128]{1,0:T(8,128)S(1)} %collective-permute-done.24.refs_3_, ...), custom_call_target="tpu_custom_call" | custom-call | tf_op jit(solution)/shard_map/assemble/pallas_call | solution.py:118
  (40 shorter events, 0.8 us)
Async XLA Ops:
  4.2 3.2 %collective-permute-start = (f32[96,1024]{1,0:T(8,128)S(1)}, f32[96,1024]{1,0:T(8,128)S(1)}, u32[]{:S(2)}, u32[]{:S(2)}) collective-permute-start(f32[96,1024]{1,0:T(8,128)S(1)} %get-tuple-element.67), channel_id=1, source_target_pairs={{0,2},{2,0},{4,6},{6,4},{1,3},{3,1},{5,7},{7,5},{8,10},{10,8},{12,... | collective-permute-start | bytes 1179656 | tf_op jit(solution)/shard_map/ppermute | solution.py:488
  4.7 8.4 %collective-permute-start.3 = (f32[64,768]{1,0:T(8,128)S(1)}, f32[64,768]{1,0:T(8,128)S(1)}, u32[]{:S(2)}, u32[]{:S(2)}) collective-permute-start(f32[64,768]{1,0:T(8,128)S(1)} %get-tuple-element.71.refs_0_), channel_id=1, source_target_pairs={{0,8},{8,0},{16,24},{24,16},{1,9},{9,1},{17,25},{25,17},{2,10},{10... | collective-permute-start | bytes 589832 | tf_op jit(solution)/shard_map/ppermute | solution.py:461
  9.8 7.2 %collective-permute-start.2 = (f32[64,768]{1,0:T(8,128)S(1)}, f32[64,768]{1,0:T(8,128)S(1)}, u32[]{:S(2)}, u32[]{:S(2)}) collective-permute-start(f32[64,768]{1,0:T(8,128)S(1)} %get-tuple-element.70.refs_2_.refs_0_), channel_id=1, source_target_pairs={{0,8},{8,0},{16,24},{24,16},{1,9},{9,1},{17,25},{25,17},{2,10},{10... | collective-permute-start | bytes 589832 | tf_op jit(solution)/shard_map/ppermute | solution.py:461
  11.5 7.8 %collective-permute-start.1 = (f32[96,1024]{1,0:T(8,128)S(1)}, f32[96,1024]{1,0:T(8,128)S(1)}, u32[]{:S(2)}, u32[]{:S(2)}) collective-permute-start(f32[96,1024]{1,0:T(8,128)S(1)} %get-tuple-element.69), channel_id=1, source_target_pairs={{0,1},{1,0},{2,4},{3,5},{4,2},{5,3},{6,7},{7,6},{8,9},{9,8},{10,12... | collective-permute-start | bytes 1179656 | tf_op jit(solution)/shard_map/ppermute | solution.py:493
  13.1 10.3 %collective-permute-start.7 = (f32[64,768]{1,0:T(8,128)S(1)}, f32[64,768]{1,0:T(8,128)S(1)}, u32[]{:S(2)}, u32[]{:S(2)}) collective-permute-start(f32[64,768]{1,0:T(8,128)S(1)} %add.16.refs_2_.refs_0_), channel_id=1, source_target_pairs={{8,16},{16,8},{0,2},{24,26},{10,18},{18,10},{2,0},{26,24},{12,20},... | collective-permute-start | bytes 589832 | tf_op jit(solution)/shard_map/ppermute | solution.py:466
  13.2 10.2 %collective-permute-start.8 = (f32[64,768]{1,0:T(8,128)S(1)}, f32[64,768]{1,0:T(8,128)S(1)}, u32[]{:S(2)}, u32[]{:S(2)}) collective-permute-start(f32[64,768]{1,0:T(8,128)S(1)} %get-tuple-element.76.refs_0_), channel_id=1, source_target_pairs={{0,8},{8,0},{16,24},{24,16},{1,9},{9,1},{17,25},{25,17},{2,10},{10... | collective-permute-start | bytes 589832 | tf_op jit(solution)/shard_map/ppermute | solution.py:461
  16.5 10.3 %collective-permute-start.5 = (f32[64,768]{1,0:T(8,128)S(1)}, f32[64,768]{1,0:T(8,128)S(1)}, u32[]{:S(2)}, u32[]{:S(2)}) collective-permute-start(f32[64,768]{1,0:T(8,128)S(1)} %get-tuple-element.72.refs_0_), channel_id=1, source_target_pairs={{0,8},{8,0},{16,24},{24,16},{1,9},{9,1},{17,25},{25,17},{2,10},{10... | collective-permute-start | bytes 589832 | tf_op jit(solution)/shard_map/ppermute | solution.py:461
  17.1 9.7 %collective-permute-start.6 = (f32[64,768]{1,0:T(8,128)S(1)}, f32[64,768]{1,0:T(8,128)S(1)}, u32[]{:S(2)}, u32[]{:S(2)}) collective-permute-start(f32[64,768]{1,0:T(8,128)S(1)} %add.17.refs_4_.refs_0_), channel_id=1, source_target_pairs={{8,16},{16,8},{0,2},{24,26},{10,18},{18,10},{2,0},{26,24},{12,20},... | collective-permute-start | bytes 589832 | tf_op jit(solution)/shard_map/ppermute | solution.py:466
  19.5 9.4 %collective-permute-start.4 = (f32[512,128]{1,0:T(8,128)S(1)}, f32[512,128]{1,0:T(8,128)S(1)}, u32[]{:S(2)}, u32[]{:S(2)}) collective-permute-start(f32[512,128]{1,0:T(8,128)S(1)} %side_pack.1.refs_7_), channel_id=1, source_target_pairs={{0,1},{1,0},{2,3},{3,2},{4,5},{5,4},{6,7},{7,6},{8,9},{9,8},{10,11... | collective-permute-start | bytes 786440 | tf_op jit(solution)/shard_map/ppermute | solution.py:499
  23.5 7.8 %collective-permute-start.10 = (f32[64,768]{1,0:T(8,128)S(1)}, f32[64,768]{1,0:T(8,128)S(1)}, u32[]{:S(2)}, u32[]{:S(2)}) collective-permute-start(f32[64,768]{1,0:T(8,128)S(1)} %add.18.refs_4_.refs_0_), channel_id=1, source_target_pairs={{8,16},{16,8},{0,2},{24,26},{10,18},{18,10},{2,0},{26,24},{12,20},... | collective-permute-start | bytes 589832 | tf_op jit(solution)/shard_map/ppermute | solution.py:466
  23.6 8.3 %collective-permute-start.11 = (f32[64,768]{1,0:T(8,128)S(1)}, f32[64,768]{1,0:T(8,128)S(1)}, u32[]{:S(2)}, u32[]{:S(2)}) collective-permute-start(f32[64,768]{1,0:T(8,128)S(1)} %get-tuple-element.83), channel_id=1, source_target_pairs={{0,8},{8,0},{16,24},{24,16},{1,9},{9,1},{17,25},{25,17},{2,10},{10... | collective-permute-start | bytes 589832 | tf_op jit(solution)/shard_map/ppermute | solution.py:461
  26.9 7.9 %collective-permute-start.9 = (f32[64,768]{1,0:T(8,128)S(1)}, f32[64,768]{1,0:T(8,128)S(1)}, u32[]{:S(2)}, u32[]{:S(2)}) collective-permute-start(f32[64,768]{1,0:T(8,128)S(1)} %add.19.refs_8_.refs_0_), channel_id=1, source_target_pairs={{8,16},{16,8},{0,2},{24,26},{10,18},{18,10},{2,0},{26,24},{12,20},... | collective-permute-start | bytes 589832 | tf_op jit(solution)/shard_map/ppermute | solution.py:466
  26.9 8.4 %collective-permute-start.14 = (f32[64,768]{1,0:T(8,128)S(1)}, f32[64,768]{1,0:T(8,128)S(1)}, u32[]{:S(2)}, u32[]{:S(2)}) collective-permute-start(f32[64,768]{1,0:T(8,128)S(1)} %get-tuple-element.88), channel_id=1, source_target_pairs={{0,8},{8,0},{16,24},{24,16},{1,9},{9,1},{17,25},{25,17},{2,10},{10... | collective-permute-start | bytes 589832 | tf_op jit(solution)/shard_map/ppermute | solution.py:461
  32.0 6.4 %collective-permute-start.16 = (f32[64,768]{1,0:T(8,128)S(1)}, f32[64,768]{1,0:T(8,128)S(1)}, u32[]{:S(2)}, u32[]{:S(2)}) collective-permute-start(f32[64,768]{1,0:T(8,128)S(1)} %add.20.refs_4_.refs_0_), channel_id=1, source_target_pairs={{8,16},{16,8},{0,2},{24,26},{10,18},{18,10},{2,0},{26,24},{12,20},... | collective-permute-start | bytes 589832 | tf_op jit(solution)/shard_map/ppermute | solution.py:466
  32.0 8.1 %collective-permute-start.13 = (f32[64,768]{1,0:T(8,128)S(1)}, f32[64,768]{1,0:T(8,128)S(1)}, u32[]{:S(2)}, u32[]{:S(2)}) collective-permute-start(f32[64,768]{1,0:T(8,128)S(1)} %get-tuple-element.86), channel_id=1, source_target_pairs={{0,8},{8,0},{16,24},{24,16},{1,9},{9,1},{17,25},{25,17},{2,10},{10... | collective-permute-start | bytes 589832 | tf_op jit(solution)/shard_map/ppermute | solution.py:461
  35.4 8.5 %collective-permute-start.15 = (f32[64,768]{1,0:T(8,128)S(1)}, f32[64,768]{1,0:T(8,128)S(1)}, u32[]{:S(2)}, u32[]{:S(2)}) collective-permute-start(f32[64,768]{1,0:T(8,128)S(1)} %add.21.refs_4_.refs_0_), channel_id=1, source_target_pairs={{8,16},{16,8},{0,2},{24,26},{10,18},{18,10},{2,0},{26,24},{12,20},... | collective-permute-start | bytes 589832 | tf_op jit(solution)/shard_map/ppermute | solution.py:466
  35.5 8.8 %collective-permute-start.12 = (f32[64,768]{1,0:T(8,128)S(1)}, f32[64,768]{1,0:T(8,128)S(1)}, u32[]{:S(2)}, u32[]{:S(2)}) collective-permute-start(f32[64,768]{1,0:T(8,128)S(1)} %get-tuple-element.85), channel_id=1, source_target_pairs={{0,8},{8,0},{16,24},{24,16},{1,9},{9,1},{17,25},{25,17},{2,10},{10... | collective-permute-start | bytes 589832 | tf_op jit(solution)/shard_map/ppermute | solution.py:461
  40.1 7.7 %collective-permute-start.18 = (f32[64,768]{1,0:T(8,128)S(1)}, f32[64,768]{1,0:T(8,128)S(1)}, u32[]{:S(2)}, u32[]{:S(2)}) collective-permute-start(f32[64,768]{1,0:T(8,128)S(1)} %add.22.refs_4_.refs_0_), channel_id=1, source_target_pairs={{8,16},{16,8},{0,2},{24,26},{10,18},{18,10},{2,0},{26,24},{12,20},... | collective-permute-start | bytes 589832 | tf_op jit(solution)/shard_map/ppermute | solution.py:466
  40.2 10.2 %collective-permute-start.19 = (f32[64,768]{1,0:T(8,128)S(1)}, f32[64,768]{1,0:T(8,128)S(1)}, u32[]{:S(2)}, u32[]{:S(2)}) collective-permute-start(f32[64,768]{1,0:T(8,128)S(1)} %get-tuple-element.101), channel_id=1, source_target_pairs={{0,8},{8,0},{16,24},{24,16},{1,9},{9,1},{17,25},{25,17},{2,10},{10... | collective-permute-start | bytes 589832 | tf_op jit(solution)/shard_map/ppermute | solution.py:461
  44.4 6.2 %collective-permute-start.17 = (f32[64,768]{1,0:T(8,128)S(1)}, f32[64,768]{1,0:T(8,128)S(1)}, u32[]{:S(2)}, u32[]{:S(2)}) collective-permute-start(f32[64,768]{1,0:T(8,128)S(1)} %add.23.refs_4_.refs_0_), channel_id=1, source_target_pairs={{8,16},{16,8},{0,2},{24,26},{10,18},{18,10},{2,0},{26,24},{12,20},... | collective-permute-start | bytes 589832 | tf_op jit(solution)/shard_map/ppermute | solution.py:466
  44.4 9.9 %collective-permute-start.25 = (f32[64,768]{1,0:T(8,128)S(1)}, f32[64,768]{1,0:T(8,128)S(1)}, u32[]{:S(2)}, u32[]{:S(2)}) collective-permute-start(f32[64,768]{1,0:T(8,128)S(1)} %get-tuple-element.108), channel_id=1, source_target_pairs={{0,8},{8,0},{16,24},{24,16},{1,9},{9,1},{17,25},{25,17},{2,10},{10... | collective-permute-start | bytes 589832 | tf_op jit(solution)/shard_map/ppermute | solution.py:461
  47.9 11.1 %collective-permute-start.26 = (f32[64,768]{1,0:T(8,128)S(1)}, f32[64,768]{1,0:T(8,128)S(1)}, u32[]{:S(2)}, u32[]{:S(2)}) collective-permute-start(f32[64,768]{1,0:T(8,128)S(1)} %get-tuple-element.112), channel_id=1, source_target_pairs={{0,8},{8,0},{16,24},{24,16},{1,9},{9,1},{17,25},{25,17},{2,10},{10... | collective-permute-start | bytes 589832 | tf_op jit(solution)/shard_map/ppermute | solution.py:461
  50.6 3.7 %collective-permute-start.20 = (f32[8,128]{1,0:T(8,128)S(1)}, f32[8,128]{1,0:T(8,128)S(1)}, u32[]{:S(2)}, u32[]{:S(2)}) collective-permute-start(f32[8,128]{1,0:T(8,128)S(1)} %get-tuple-element.107), channel_id=1, source_target_pairs={{0,1},{1,0},{2,3},{3,2},{4,5},{5,4},{6,7},{7,6},{8,9},{9,8},{10,11... | collective-permute-start | bytes 12296 | tf_op jit(solution)/shard_map/ppermute | solution.py:518
  50.7 9.8 %collective-permute-start.27 = (f32[64,768]{1,0:T(8,128)S(1)}, f32[64,768]{1,0:T(8,128)S(1)}, u32[]{:S(2)}, u32[]{:S(2)}) collective-permute-start(f32[64,768]{1,0:T(8,128)S(1)} %get-tuple-element.115), channel_id=1, source_target_pairs={{0,8},{8,0},{16,24},{24,16},{1,9},{9,1},{17,25},{25,17},{2,10},{10... | collective-permute-start | bytes 589832 | tf_op jit(solution)/shard_map/ppermute | solution.py:461
  54.3 1.2 %collective-permute-start.21 = (f32[8,128]{1,0:T(8,128)S(1)}, f32[8,128]{1,0:T(8,128)S(1)}, u32[]{:S(2)}, u32[]{:S(2)}) collective-permute-start(f32[8,128]{1,0:T(8,128)S(1)} %add.14), channel_id=1, source_target_pairs={{0,2},{2,0},{4,6},{6,4},{1,3},{3,1},{5,7},{7,5},{8,10},{10,8},{12,... | collective-permute-start | bytes 12296 | tf_op jit(solution)/shard_map/ppermute | solution.py:519
  55.5 6.0 %collective-permute-start.22 = (f32[8,128]{1,0:T(8,128)S(1)}, f32[8,128]{1,0:T(8,128)S(1)}, u32[]{:S(2)}, u32[]{:S(2)}) collective-permute-start(f32[8,128]{1,0:T(8,128)S(1)} %add.15.refs_0_), channel_id=1, source_target_pairs={{0,12},{2,14},{4,8},{6,10},{8,4},{10,6},{12,0},{14,2},{16,28},{18,... | collective-permute-start | bytes 12296 | tf_op jit(solution)/shard_map/ppermute | solution.py:523
  57.8 3.7 %collective-permute-start.23 = (f32[8,128]{1,0:T(8,128)S(1)}, f32[8,128]{1,0:T(8,128)S(1)}, u32[]{:S(2)}, u32[]{:S(2)}) collective-permute-start(f32[8,128]{1,0:T(8,128)S(1)} %add.15.refs_0_), channel_id=1, source_target_pairs={{0,8},{8,0},{16,24},{24,16},{1,9},{9,1},{17,25},{25,17},{2,10},{10... | collective-permute-start | bytes 12296 | tf_op jit(solution)/shard_map/ppermute | solution.py:524
  57.8 3.7 %collective-permute-start.24 = (f32[8,128]{1,0:T(8,128)S(1)}, f32[8,128]{1,0:T(8,128)S(1)}, u32[]{:S(2)}, u32[]{:S(2)}) collective-permute-start(f32[8,128]{1,0:T(8,128)S(1)} %add.15.refs_0_), channel_id=1, source_target_pairs={{0,4},{2,6},{4,0},{6,2},{1,5},{3,7},{5,1},{7,3},{8,12},{10,14},{12... | collective-permute-start | bytes 12296 | tf_op jit(solution)/shard_map/ppermute | solution.py:525
